TPU v7x, 128 devices: a whole 4x4x4 slice. The times are simulated.
128 devices in a mesh: colat: 16 (over x_lo, y, core), depth: 8 (over x_hi, z).
Axes of the slice: x: 4 (x_hi: 2, x_lo: 2; x = x_hi * 2 + x_lo), y: 4, z: 4, core: 2. Of those that a mesh axis runs over, the one named last changes fastest.
Arguments:
- displacement: float32 [3, 64, 32, 2048], P(None, 'colat', 'depth'), may hold values from -6 to 6
- previous: float32 [3, 64, 32, 2048], P(None, 'colat', 'depth'), may hold values from -6 to 6
- node_blocks: int32 [64, 32], P('colat', 'depth'), may hold values from 1 to 8
- inverse_mass: float32 [64, 32], P('colat', 'depth'), may hold values from 0.0008 to 0.003
- jacobian_diag: float32 [2, 16, 5, 8, 5], P(None, 'colat', None, 'depth'), may hold values from 0.6 to 1.5
- jacobian_off: float32 [2, 16, 5, 8, 5], P(None, 'colat', None, 'depth'), may hold values from -0.25 to 0.25
- inverse_radius: float32 [16, 5, 8, 5], P('colat', None, 'depth'), may hold values from 2 to 6
- lame_lambda: float32 [16, 5, 8, 5, 2048], P('colat', None, 'depth'), may hold values from 0.3 to 1
- lame_mu: float32 [16, 5, 8, 5, 2048], P('colat', None, 'depth'), may hold values from 0.3 to 1
Outputs:
- displacement_mid: float32 [3, 64, 32, 2048], P(None, 'colat', 'depth')
- displacement_final: float32 [3, 64, 32, 2048], P(None, 'colat', 'depth')
All inputs are finite; a program needn't handle non-finite values.
Results may differ from a plain program's by a relative error of at most 0.0014.
Values may be sent and summed in bfloat16 or wider, within the bound.
No kernel may reach another device: no remote copies, remote signals or barrier semaphores. Data moves between devices by JAX's collectives and lax.ppermute only.
A program may use at most 64 MiB of HBM per device.

v0:
```python
import functools
import math

import jax
import jax.numpy as jnp
import ml_dtypes
import numpy as np
from jax import lax
from jax.experimental import pallas as pl
from jax.experimental.pallas import tpu as pltpu
from jax.sharding import PartitionSpec as P

BF16 = jnp.bfloat16
F32 = jnp.float32
WIDTH = 2048
LANES = 128
RADIX = 16
OWN = 48
NODES = 80
STRAINS = 152
VMEM_LIMIT = 40 * 1024 * 1024


def gll_derivative():
    points = np.array([-1.0, -math.sqrt(3.0 / 7.0), 0.0, math.sqrt(3.0 / 7.0), 1.0])
    weights = np.ones(5)
    for row in range(5):
        for col in range(5):
            if row != col:
                weights[row] /= points[row] - points[col]
    matrix = np.zeros((5, 5))
    for row in range(5):
        for col in range(5):
            if row != col:
                matrix[row, col] = weights[col] / weights[row] / (points[row] - points[col])
        matrix[row, row] = -np.sum(matrix[row])
    return matrix


def node_row(comp, i, j):
    if i == 4:
        return OWN + (12 + comp if j == 4 else 4 * comp + j)
    if j == 4:
        return OWN + 16 + 4 * comp + i
    return 16 * comp + 4 * i + j


def strain_row(strain, node):
    return 24 * strain + node if node < 24 else 144 + strain


def strain_terms():
    deriv = gll_derivative()
    parts = np.zeros((5, STRAINS, 2 * NODES))
    node_of = np.zeros((STRAINS, 25))
    half = math.sqrt(0.5)
    for i in range(5):
        for j in range(5):
            node = 5 * i + j

            def grad(strain, along_z, comp, scale):
                row = strain_row(strain, node)
                for other in range(5):
                    xi, eta = (2, 3) if along_z else (0, 1)
                    parts[xi, row, node_row(comp, other, j)] += scale * deriv[i, other]
                    parts[eta, row, node_row(comp, i, other)] += scale * deriv[j, other]

            def radial(strain, comp, azimuthal, scale):
                row = strain_row(strain, node)
                parts[4, row, NODES * azimuthal + node_row(comp, i, j)] += scale / 1024.0

            grad(0, False, 0, 1.0)
            grad(1, True, 2, 1.0)
            radial(2, 1, 1, 1.0)
            radial(2, 0, 0, 1.0)
            grad(3, True, 0, half)
            grad(3, False, 2, half)
            radial(4, 0, 1, half)
            radial(4, 1, 0, -half)
            grad(4, False, 1, half)
            radial(5, 2, 1, half)
            grad(5, True, 1, half)
            for strain in range(6):
                node_of[strain_row(strain, node), node] = 1.0
    parts[:, 150] = parts[:, 144] + parts[:, 145] + parts[:, 146]
    node_of[150, 24] = 1.0
    return parts.astype(np.float32), node_of.astype(np.float32)


def sample_tables():
    order = np.arange(LANES)[:, None]
    table = np.zeros((RADIX, 2 * LANES, LANES))
    for k0 in range(RADIX):
        angle = 2.0 * math.pi * (order * (16 * np.arange(LANES)[None, :] + k0) % WIDTH) / WIDTH
        table[k0, :LANES] = np.cos(angle)
        table[k0, LANES:] = -np.sin(angle)
    return (
        table.astype(ml_dtypes.bfloat16),
        np.ascontiguousarray(table.transpose(0, 2, 1)).astype(ml_dtypes.bfloat16),
    )


def lane_shuffle():
    shuffle = np.zeros((LANES, LANES))
    for t in range(8):
        for k0 in range(16):
            shuffle[16 * t + k0, 8 * k0 + t] = 1.0
    return shuffle.astype(ml_dtypes.bfloat16)


def face(fixed_i, fixed_j):
    return [(fixed_i, n) if fixed_j is None else (n, fixed_j) for n in range(5)]


def message_row(comp, n):
    return 12 + comp if n == 4 else 4 * comp + n


def first_halo_select():
    select = np.zeros((48, OWN))
    for comp in range(3):
        for n in range(4):
            select[4 * comp + n, node_row(comp, 0, n)] = 1.0
            select[16 + 4 * comp + n, node_row(comp, n, 0)] = 1.0
        select[32 + 12 + comp, node_row(comp, 0, 0)] = 1.0
    return select.astype(ml_dtypes.bfloat16)


def pick(faces):
    select = np.zeros((16 * len(faces), NODES))
    for index, nodes in enumerate(faces):
        for comp in range(3):
            for n, (i, j) in enumerate(nodes):
                select[16 * index + message_row(comp, n), node_row(comp, i, j)] = 1.0
    return select


ROW_LOW, ROW_HIGH = face(0, None), face(4, None)
COL_LOW, COL_HIGH = face(None, 0), face(None, 4)


def outgoing_select():
    even = pick([ROW_HIGH, ROW_LOW, COL_HIGH, COL_LOW])
    odd = pick([ROW_LOW, ROW_HIGH, COL_HIGH, COL_LOW])
    return np.stack([even, odd]).astype(ml_dtypes.bfloat16)


def column_select():
    out = np.zeros((4, 32, 64))
    for par_c in range(2):
        faces = [ROW_HIGH, ROW_LOW] if par_c == 0 else [ROW_LOW, ROW_HIGH]
        arrive = pick(faces).T
        full = np.concatenate([pick([COL_HIGH]), pick([COL_LOW])], axis=0)
        whole = np.concatenate([np.eye(32), full @ arrive], axis=1)
        for par_d in range(2):
            out[2 * par_c + par_d] = whole if par_d == 0 else np.roll(whole, 16, axis=0)
    return out.astype(ml_dtypes.bfloat16)


def arrival_select():
    out = np.zeros((4, NODES, 64))
    for par_c in range(2):
        rows = [ROW_HIGH, ROW_LOW] if par_c == 0 else [ROW_LOW, ROW_HIGH]
        for par_d in range(2):
            cols = [COL_HIGH, COL_LOW] if par_d == 0 else [COL_LOW, COL_HIGH]
            out[2 * par_c + par_d] = pick(rows + cols).T
    return out.astype(ml_dtypes.bfloat16)


def last_select():
    select = np.zeros((OWN, 48))
    for comp in range(3):
        for n in range(4):
            select[node_row(comp, 0, n), 4 * comp + n] = 1.0
            select[node_row(comp, n, 0), 16 + 4 * comp + n] = 1.0
        select[node_row(comp, 0, 0), 32 + 12 + comp] = 1.0
    return select.astype(ml_dtypes.bfloat16)


def turned(value, eighths, scale_sign):
    re, im = value
    eighths = (scale_sign * eighths) % 16
    if eighths == 0:
        return re, im
    if eighths == 4:
        return -im, re
    if eighths == 8:
        return -re, -im
    if eighths == 12:
        return im, -re
    root = math.sqrt(0.5)
    if eighths == 2:
        return (re - im) * root, (im + re) * root
    if eighths == 14:
        return (re + im) * root, (im - re) * root
    cosine = math.cos(2.0 * math.pi * eighths / 16)
    sine = math.sin(2.0 * math.pi * eighths / 16)
    return re * cosine - im * sine, im * cosine + re * sine


def add(left, right):
    return left[0] + right[0], left[1] + right[1]


def sub(left, right):
    return left[0] - right[0], left[1] - right[1]


def transform(values, sign):
    count = len(values)
    if count == 1:
        return values
    even = transform(values[0::2], sign)
    odd = transform(values[1::2], sign)
    odd = [turned(value, q * (16 // count), sign) for q, value in enumerate(odd)]
    return [add(a, b) for a, b in zip(even, odd)] + [sub(a, b) for a, b in zip(even, odd)]


def spread(blocks):
    even = transform(blocks, 1)
    odd = transform([turned(value, b, 1) for b, value in enumerate(blocks)], 1)
    return [value for pair in zip(even, odd) for value in pair]


def gathered(values):
    even = transform(values[0::2], -1)
    odd = transform(values[1::2], -1)
    return [add(a, turned(b, index, -1)) for index, (a, b) in enumerate(zip(even, odd))]


def block(index, part):
    return slice(2 * LANES * index + LANES * part, 2 * LANES * index + LANES * (part + 1))


def orders(index):
    lane = lax.broadcasted_iota(jnp.int32, (1, LANES), 1)
    return (lane + LANES * index).astype(F32)


def dot(left, right):
    return jnp.dot(left, right, preferred_element_type=F32)


def first_kernel(disp_ref, meta_ref, select_ref, out_ref):
    live = meta_ref[:, 1:2]
    for index in range(8):
        lanes = slice(256 * index, 256 * (index + 1))
        value = jnp.where(live > index, disp_ref[:, lanes], 0.0).astype(BF16)
        out_ref[:, lanes] = dot(select_ref[...], value).astype(BF16)
    mass = meta_ref[:, 0:1]
    high = mass.astype(BF16).astype(F32)
    lane = lax.broadcasted_iota(jnp.int32, (OWN, LANES), 1)
    info = jnp.where(lane == 0, high, jnp.where(lane == 1, mass - high, jnp.where(lane == 2, live, 0.0)))
    out_ref[:, WIDTH:] = dot(select_ref[...], info.astype(BF16)).astype(BF16)


def material_kernel(lambda_ref, mu_ref, shuffle_ref, out_ref, work):
    for index in range(16):
        lanes = slice(LANES * index, LANES * (index + 1))
        lam, mu = lambda_ref[:, lanes], mu_ref[:, lanes] * 2.0
        row = lax.broadcasted_iota(jnp.int32, (8, LANES), 0)
        last = jnp.where(row < 6, mu[24:25], jnp.where(row == 6, lam[24:25], 0.0))
        stacked = jnp.concatenate([lam[:24], mu[:24], last], axis=0)
        high = stacked.astype(BF16)
        low = (stacked - high.astype(F32)).astype(BF16)
        shuffled = dot(high, shuffle_ref[...]) + dot(low, shuffle_ref[...])
        work[index] = shuffled if index == 0 else pltpu.roll(shuffled, 8 * index, 1)
    group = lax.broadcasted_iota(jnp.int32, (8, LANES), 1) // 8
    for rows in range(7):
        part = slice(8 * rows, 8 * rows + 8)
        held = [work[(16 - index) % 16, part] for index in range(16)]
        for bit in range(4):
            chosen = (group >> bit) % 2 == 1
            held = [jnp.where(chosen, held[(index - (1 << bit)) % 16], held[index]) for index in range(16)]
        for index in range(16):
            out_ref[index, part] = held[index] if index == 0 else pltpu.roll(held[index], LANES - 8 * index, 1)


def forces(nodes, operator_ref, back_ref, table_ref, tback_ref, material_ref, both, strain, spectrum, emit):
    for index in range(8):
        order = orders(index)
        re = nodes(block(index, 0))
        im = nodes(block(index, 1))
        both[:NODES, block(index, 0)] = re.astype(BF16)
        both[:NODES, block(index, 1)] = im.astype(BF16)
        both[NODES:, block(index, 0)] = (im * (-order)).astype(BF16)
        both[NODES:, block(index, 1)] = (re * order).astype(BF16)
        lanes = slice(256 * index, 256 * (index + 1))
        strain[:, lanes] = dot(operator_ref[...], both[:, lanes])

    @pl.loop(0, STRAINS // 8)
    def _(group):
        rows = pl.ds(pl.multiple_of(group * 8, 8), 8)
        values = [(strain[rows, block(b, 0)], strain[rows, block(b, 1)]) for b in range(8)]
        for k0, (re, im) in enumerate(spread(values)):
            spectrum[k0, rows, :LANES] = re
            spectrum[k0, rows, LANES:] = im

    for k0 in range(RADIX):
        sample = dot(spectrum[k0].astype(BF16), table_ref[k0])
        lam, mu, last = material_ref[k0, :24], material_ref[k0, 24:48], material_ref[k0, 48:]
        parts = [sample[24 * s : 24 * s + 24] for s in range(6)]
        volume = lam * (parts[0] + parts[1] + parts[2])
        stress = [volume + mu * part for part in parts[:3]] + [mu * part for part in parts[3:]]
        stress.append(last * sample[144:])
        stress = jnp.concatenate(stress, axis=0).astype(BF16)
        spectrum[k0] = dot(stress, tback_ref[k0])

    @pl.loop(0, STRAINS // 8)
    def _(group):
        rows = pl.ds(pl.multiple_of(group * 8, 8), 8)
        values = [(spectrum[k0, rows, :LANES], spectrum[k0, rows, LANES:]) for k0 in range(RADIX)]
        for b, (re, im) in enumerate(gathered(values)):
            strain[rows, block(b, 0)] = re
            strain[rows, block(b, 1)] = im

    for index in range(8):
        lanes = slice(256 * index, 256 * (index + 1))
        order = orders(index)
        pulled = dot(back_ref[...], strain[:, lanes].astype(BF16))
        re = pulled[:NODES, :LANES] + order * pulled[NODES:, LANES:]
        im = pulled[:NODES, LANES:] - order * pulled[NODES:, :LANES]
        emit(index, re, im)


def step_one_kernel(
    place, disp_ref, prev_ref, meta_ref, row_ref, col_ref, corner_ref,
    operator_ref, back_ref, table_ref, tback_ref, material_ref, select_ref,
    sum_ref, pair_ref, side_ref, faces_ref,
    tiles, both, strain, spectrum,
):
    rest_c, rest_d = place[2].astype(F32), place[3].astype(F32)
    tiles[:16] = row_ref[...].astype(F32) * rest_c + corner_ref[...].astype(F32) * (rest_c * rest_d)
    tiles[16:] = col_ref[...].astype(F32) * rest_d
    info = tiles[:, WIDTH:]
    lane = lax.broadcasted_iota(jnp.int32, (32, LANES), 1)
    halo_info = jnp.where(lane == 0, info[:, 0:1] + info[:, 1:2], jnp.where(lane == 1, info[:, 2:3], 0.0))
    sum_ref[:OWN, WIDTH:] = meta_ref[...]
    sum_ref[OWN:, WIDTH:] = halo_info
    live = meta_ref[:, 1:2]

    def nodes(lanes):
        own = jnp.where(live > lanes.start // 256, disp_ref[:, lanes], 0.0)
        return jnp.concatenate([own, tiles[:, lanes]], axis=0)

    mass = sum_ref[:, WIDTH : WIDTH + 1] * (-1.0 / WIDTH)

    def emit(index, re, im):
        for part, value in ((0, re), (1, im)):
            lanes = block(index, part)
            value = mass * value
            total = 2.0 * disp_ref[:, lanes] - prev_ref[:, lanes] + value[:OWN]
            total = jnp.concatenate([total, value[OWN:]], axis=0)
            sum_ref[:, lanes] = total
            sent = dot(select_ref[place[0]], total.astype(BF16)).astype(BF16)
            pair_ref[:, lanes] = sent[:16]
            side_ref[:, lanes] = sent[16:32]
            faces_ref[:, lanes] = sent[32:]

    forces(nodes, operator_ref, back_ref, table_ref, tback_ref, material_ref, both, strain, spectrum, emit)


def column_kernel(place, faces_ref, pair_ref, side_ref, select_ref, pair_out, side_out):
    select = select_ref[2 * place[0] + place[1]]
    for index in range(8):
        lanes = slice(256 * index, 256 * (index + 1))
        stacked = jnp.concatenate([faces_ref[:, lanes], pair_ref[:, lanes], side_ref[:, lanes]], axis=0)
        sent = dot(select, stacked).astype(BF16)
        pair_out[:, lanes] = sent[:16]
        side_out[:, lanes] = sent[16:]


def step_two_kernel(
    place, disp_ref, sum_ref, cpair_ref, cside_ref, dpair_ref, dside_ref,
    operator_ref, back_ref, table_ref, tback_ref, material_ref, select_ref,
    mid_ref, sum_out, row_out, col_out,
    current, both, strain, spectrum,
):
    select = select_ref[2 * place[0] + place[1]]
    live = sum_ref[:, WIDTH + 1 : WIDTH + 2]
    for index in range(8):
        lanes = slice(256 * index, 256 * (index + 1))
        arrived = jnp.concatenate([ref[:, lanes] for ref in (cpair_ref, cside_ref, dpair_ref, dside_ref)], axis=0)
        value = jnp.where(live > index, sum_ref[:, lanes] + dot(select, arrived), 0.0)
        current[:, lanes] = value
        mid_ref[:, lanes] = value[:OWN]
    mass = sum_ref[:, WIDTH : WIDTH + 1] * (-1.0 / WIDTH)

    def emit(index, re, im):
        for part, value in ((0, re), (1, im)):
            lanes = block(index, part)
            value = mass * value
            sum_out[:, lanes] = 2.0 * current[:OWN, lanes] - disp_ref[:, lanes] + value[:OWN]
            row_out[:, lanes] = value[OWN : OWN + 16].astype(BF16)
            col_out[:, lanes] = value[OWN + 16 :].astype(BF16)

    forces(
        lambda lanes: current[:, lanes],
        operator_ref, back_ref, table_ref, tback_ref, material_ref, both, strain, spectrum, emit,
    )


def last_kernel(sum_ref, meta_ref, row_ref, col_ref, corner_ref, select_ref, out_ref):
    live = meta_ref[:, 1:2]
    for index in range(8):
        lanes = slice(256 * index, 256 * (index + 1))
        arrived = jnp.concatenate([row_ref[:, lanes], col_ref[:, lanes], corner_ref[:, lanes]], axis=0)
        value = sum_ref[:, lanes] + dot(select_ref[...], arrived)
        out_ref[:, lanes] = jnp.where(live > index, value, 0.0)


def call(kernel, outs, scratch=(), scalars=False, inputs=0, flops=0):
    vmem = pl.BlockSpec(memory_space=pltpu.VMEM)
    specs = [vmem] * inputs
    if scalars:
        specs = [pl.BlockSpec(memory_space=pltpu.SMEM)] + specs
    return pl.pallas_call(
        kernel,
        out_shape=outs,
        in_specs=specs,
        out_specs=jax.tree.map(lambda _: vmem, outs),
        scratch_shapes=list(scratch),
        compiler_params=pltpu.CompilerParams(vmem_limit_bytes=VMEM_LIMIT),
        cost_estimate=pl.CostEstimate(flops=flops, bytes_accessed=1 << 20, transcendentals=0),
    )


def shape(*dims, dtype=F32):
    return jax.ShapeDtypeStruct(dims, dtype)


def solution(mesh):
    bands, layers = mesh.shape["colat"], mesh.shape["depth"]
    parts, node_of = strain_terms()
    table, tback = sample_tables()

    def shifted(array, by_c, by_d):
        pairs = [
            (c * layers + d, (c + by_c) % bands * layers + (d + by_d) % layers)
            for c in range(bands)
            for d in range(layers)
        ]
        return lax.ppermute(array, ("colat", "depth"), pairs)

    def swapped(array, axis, odd):
        count = mesh.shape[axis]
        pairs = [(n, (n + 1) % count if n % 2 == odd else (n - 1) % count) for n in range(count)]
        return lax.ppermute(array, axis, pairs)

    def per_device(displacement, previous, node_blocks, inverse_mass, jac_diag, jac_off, inv_radius, lame_l, lame_m):
        at_c, at_d = lax.axis_index("colat"), lax.axis_index("depth")
        place = jnp.stack([at_c % 2, at_d % 2, at_c < bands - 1, at_d < layers - 1]).astype(jnp.int32)
        disp = displacement.reshape(OWN, WIDTH)
        prev = previous.reshape(OWN, WIDTH)
        lane = lax.broadcasted_iota(jnp.int32, (3, 4, 4, LANES), 3)
        meta = jnp.where(
            lane == 0,
            inverse_mass[None, :, :, None],
            jnp.where(lane == 1, node_blocks.astype(F32)[None, :, :, None], 0.0),
        ).reshape(OWN, LANES)

        halo = call(first_kernel, shape(OWN, WIDTH + LANES, dtype=BF16), inputs=3)(
            disp, meta, jnp.asarray(first_halo_select())
        )
        row = shifted(halo[:16], -1, 0)
        col = shifted(halo[16:32], 0, -1)
        corner = shifted(halo[32:], -1, -1)

        factors = jnp.stack(
            [item.reshape(25) for item in (jac_diag[0], jac_off[0], jac_off[1], jac_diag[1], inv_radius)]
        )
        spread_factors = jnp.dot(factors, jnp.asarray(node_of.T), precision=lax.Precision.HIGHEST)
        operator = jnp.sum(spread_factors[:, :, None] * jnp.asarray(parts), axis=0).astype(BF16)
        back = jnp.sum(spread_factors[:, None, :] * jnp.asarray(parts.transpose(0, 2, 1)), axis=0).astype(BF16)
        material = call(
            material_kernel, shape(RADIX, 56, LANES), [pltpu.VMEM((16, 56, LANES), F32)], inputs=3
        )(lame_l.reshape(25, WIDTH), lame_m.reshape(25, WIDTH), jnp.asarray(lane_shuffle()))

        work = [
            pltpu.VMEM((2 * NODES, WIDTH), BF16),
            pltpu.VMEM((STRAINS, WIDTH), F32),
            pltpu.VMEM((RADIX, STRAINS, 2 * LANES), F32),
        ]
        tile = shape(16, WIDTH, dtype=BF16)
        shared = (operator, back, jnp.asarray(table), jnp.asarray(tback), material)
        total, pair, side, faces = call(
            step_one_kernel,
            (shape(NODES, WIDTH + LANES), tile, tile, shape(32, WIDTH, dtype=BF16)),
            [pltpu.VMEM((32, WIDTH + LANES), F32)] + work,
            scalars=True, inputs=12, flops=10**9,
        )(place, disp, prev, meta, row, col, corner, *shared, jnp.asarray(outgoing_select()))
        cpair = swapped(pair, "colat", 0)
        cside = swapped(side, "colat", 1)
        pair, side = call(column_kernel, (tile, tile), scalars=True, inputs=4)(
            place, faces, cpair, cside, jnp.asarray(column_select())
        )
        dpair = swapped(pair, "depth", 0)
        dside = swapped(side, "depth", 1)
        middle, final, row, col = call(
            step_two_kernel,
            (shape(OWN, WIDTH), shape(OWN, WIDTH), tile, tile),
            [pltpu.VMEM((NODES, WIDTH), F32)] + work,
            scalars=True, inputs=12, flops=10**9,
        )(place, disp, total, cpair, cside, dpair, dside, *shared, jnp.asarray(arrival_select()))
        corner = shifted(row, 1, 1)
        col = shifted(col, 0, 1)
        row = shifted(row, 1, 0)
        final = call(last_kernel, shape(OWN, WIDTH), inputs=6)(
            final, meta, row, col, corner, jnp.asarray(last_select())
        )
        return middle.reshape(displacement.shape), final.reshape(displacement.shape)

    return jax.shard_map(
        per_device,
        mesh=mesh,
        in_specs=(
            P(None, "colat", "depth", None),
            P(None, "colat", "depth", None),
            P("colat", "depth"),
            P("colat", "depth"),
            P(None, "colat", None, "depth", None),
            P(None, "colat", None, "depth", None),
            P("colat", None, "depth", None),
            P("colat", None, "depth", None, None),
            P("colat", None, "depth", None, None),
        ),
        out_specs=(P(None, "colat", "depth", None), P(None, "colat", "depth", None)),
        check_vma=False,
    )
```

profile of v0, /device:TPU:1, one launch (start us, length us, event | category | flops | bytes accessed | tf_op | source)
XLA Modules:
  0.0 57.6 jit_solution(8523836839763624990)
XLA Ops:
  0.6 0.7 %convert_element_type.11 = f32[4,4]{1,0:T(4,128)S(1)} convert(s32[4,4]{1,0:T(4,128)} %param.22) | non-fusion elementwise | flops 16 | bytes 128 | tf_op jit(solution)/shard_map/convert_element_type | solution.py:459
  1.3 0.1 broadcast_in_dim.36
  1.4 0.6 %copy-done.17 = f32[4,4]{1,0:T(4,128)S(1)} copy-done((f32[4,4]{1,0:T(4,128)S(1)}, f32[4,4]{1,0:T(4,128)}, u32[]{:S(2)}) %copy-start.17) | copy-done | bytes 88
  2.0 0.1 broadcast_in_dim.33
  2.1 0.0 copy-start.10
  2.1 1.2 %reshape.29.disp_ref = f32[48,2048]{1,0:T(8,128)S(1)} reshape(f32[3,4,4,2048]{3,2,1,0:T(4,128)} %param.20) | data formatting | bytes 786432 | tf_op jit(solution)/shard_map/reshape | solution.py:453
  3.3 0.0 copy-start.8
  3.3 0.1 select_select_fusion.meta_ref
  3.4 0.6 %copy-done.8 = bf16[48,48]{1,0:T(8,128)(2,1)S(1)} copy-done((bf16[48,48]{1,0:T(8,128)(2,1)S(1)}, bf16[48,48]{1,0:T(8,128)(2,1)}, u32[]{:S(2)}) %copy-start.8) | copy-done | bytes 4632
  4.1 0.3 shard_map.203
  4.3 0.7 %fusion = (bf16[16,2176]{1,0:T(8,128)(2,1)}, bf16[16,2176]{1,0:T(8,128)(2,1)}, bf16[16,2176]{1,0:T(8,128)(2,1)}) fusion(bf16[48,2176]{1,0:T(8,128)(2,1)S(1)} %shard_map.203), kind=kLoop, calls=%fused_computation.10 | loop fusion | bytes 417792 | tf_op jit(solution)/shard_map/slice | solution.py:467
  5.0 7.6 %collective-permute-start.2 = (bf16[16,2176]{1,0:T(8,128)(2,1)}, bf16[16,2176]{1,0:T(8,128)(2,1)}, u32[]{:S(2)}, u32[]{:S(2)}) collective-permute-start(bf16[16,2176]{1,0:T(8,128)(2,1)} %get-tuple-element.26), channel_id=1, source_target_pairs={{0,127},{1,120},{2,121},{3,122},{4,123},{5,124},{6,125},{7,126},{8... | collective-permute-start | bytes 208904 | tf_op jit(solution)/shard_map/ppermute | solution.py:443
  12.6 0.1 collective-permute-start.1
  12.8 3.2 %collective-permute-start = (bf16[16,2176]{1,0:T(8,128)(2,1)}, bf16[16,2176]{1,0:T(8,128)(2,1)}, u32[]{:S(2)}, u32[]{:S(2)}) collective-permute-start(bf16[16,2176]{1,0:T(8,128)(2,1)} %get-tuple-element.28), channel_id=1, source_target_pairs={{0,120},{1,121},{2,122},{3,123},{4,124},{5,125},{6,126},{7,127},{8... | collective-permute-start | bytes 208904 | tf_op jit(solution)/shard_map/ppermute | solution.py:443
  16.0 0.1 stack_reshape.3
  16.1 0.1 stack_reshape_squeeze.15
  16.2 0.1 stack_reshape_squeeze.12
  16.3 0.1 stack_reshape_squeeze.14
  16.3 0.1 stack_reshape_squeeze.13
  16.4 0.1 fusion.1
  16.6 0.8 %multiply_reduce_fusion.1.operator_ref = bf16[152,160]{1,0:T(8,128)(2,1)} fusion(f32[5,152,160]{2,1,0:T(8,128)S(1)} %copy-done.10, f32[5,152]{1,0:T(8,128)S(1)} %fusion.1), kind=kLoop, calls=%fused_computation.1 | loop fusion | flops 218880 | bytes 538080 | tf_op jit(solution)/shard_map/reduce_sum | solution.py:473
  17.4 0.2 multiply_reduce_fusion
  17.6 0.1 copy.22.back_ref
  17.7 0.6 %copy-done.11 = f32[1,5,1,5,2048]{4,2,3,1,0:T(1,128)S(1)} copy-done((f32[1,5,1,5,2048]{4,2,3,1,0:T(1,128)S(1)}, f32[1,5,1,5,2048]{4,2,3,1,0:T(1,128)}, u32[]{:S(2)}) %copy-start.11) | copy-done | bytes 204824
  18.3 0.5 reduce.5
  18.9 0.9 %copy-done.12 = f32[1,5,1,5,2048]{4,2,3,1,0:T(1,128)S(1)} copy-done((f32[1,5,1,5,2048]{4,2,3,1,0:T(1,128)S(1)}, f32[1,5,1,5,2048]{4,2,3,1,0:T(1,128)}, u32[]{:S(2)}) %copy-start.12) | copy-done | bytes 204824
  19.8 0.5 reduce.6
  20.3 1.3 %reshape.30.prev_ref = f32[48,2048]{1,0:T(8,128)S(1)} reshape(f32[3,4,4,2048]{3,2,1,0:T(4,128)} %param.21) | data formatting | bytes 786432 | tf_op jit(solution)/shard_map/reshape | solution.py:454
  21.6 0.7 %shard_map.204.material_ref = f32[16,56,128]{2,1,0:T(8,128)S(1)} custom-call(f32[25,2048]{1,0:T(8,128)S(1)} %reshape.31.lambda_ref, f32[25,2048]{1,0:T(8,128)S(1)} %reshape.32.mu_ref, bf16[128,128]{1,0:T(8,128)(2,1)S(1)} %copy-done.6), custom_call_target="tpu_custom_call" | custom-call | bytes 1048576 | tf_op jit(solution)/shard_map/pallas_call | solution.py:475
  22.3 0.1 pad_add_fusion.place
  22.4 0.2 copy-done.2
  22.6 5.1 %shard_map.205 = (f32[80,2176]{1,0:T(8,128)S(1)}, bf16[16,2048]{1,0:T(8,128)(2,1)S(1)}, bf16[16,2048]{1,0:T(8,128)(2,1)S(1)}, bf16[32,2048]{1,0:T(8,128)(2,1)S(1)}) custom-call(s32[4]{0:T(128)S(1)} %pad_add_fusion.place, f32[48,2048]{1,0:T(8,128)S(1)} %reshape.29.disp_ref, f32[48,2048]{1,0:T(8,128)S(1)} %reshape.30.prev_ref, ...), custom_call_target="tpu_custom_call" | custom-call | flops 1000000000 | bytes 1048576 | tf_op jit(solution)/shard_map/pallas_call | solution.py:486
  27.7 0.1 collective-permute-start.3
  27.8 0.1 collective-permute-start.4
  27.9 1.1 %collective-permute-done.3.pair_ref.cpair_ref = bf16[16,2048]{1,0:T(8,128)(2,1)S(1)} collective-permute-done((bf16[16,2048]{1,0:T(8,128)(2,1)S(1)}, bf16[16,2048]{1,0:T(8,128)(2,1)S(1)}, u32[]{:S(2)}, u32[]{:S(2)}) %collective-permute-start.3) | collective-permute-done | bytes 65568 | tf_op jit(solution)/shard_map/ppermute | solution.py:448
  29.1 2.5 %collective-permute-done.4.side_ref.cside_ref = bf16[16,2048]{1,0:T(8,128)(2,1)S(1)} collective-permute-done((bf16[16,2048]{1,0:T(8,128)(2,1)S(1)}, bf16[16,2048]{1,0:T(8,128)(2,1)S(1)}, u32[]{:S(2)}, u32[]{:S(2)}) %collective-permute-start.4) | collective-permute-done | bytes 65568 | tf_op jit(solution)/shard_map/ppermute | solution.py:448
  31.6 0.7 %shard_map.206 = (bf16[16,2048]{1,0:T(8,128)(2,1)S(1)}, bf16[16,2048]{1,0:T(8,128)(2,1)S(1)}) custom-call(s32[4]{0:T(128)S(1)} %pad_add_fusion.place, bf16[32,2048]{1,0:T(8,128)(2,1)S(1)} %get-tuple-element.15.faces_ref, bf16[16,2048]{1,0:T(8,128)(2,1)S(1)} %collective-permute-done.3.pair_ref.cpair_ref, ...), custom_call_target="tpu_custom_call" | custom-call | bytes 1048576 | tf_op jit(solution)/shard_map/pallas_call | solution.py:494
  32.3 1.3 %collective-permute-start.5 = (bf16[16,2048]{1,0:T(8,128)(2,1)S(1)}, bf16[16,2048]{1,0:T(8,128)(2,1)S(1)}, u32[]{:S(2)}, u32[]{:S(2)}) collective-permute-start(bf16[16,2048]{1,0:T(8,128)(2,1)S(1)} %get-tuple-element.16), channel_id=1, source_target_pairs={{0,1},{1,0},{2,3},{3,2},{4,5},{5,4},{6,7},{7,6},{8,9},{9,8},{10,11... | collective-permute-start | bytes 196616 | tf_op jit(solution)/shard_map/ppermute | solution.py:448
  33.6 0.1 collective-permute-start.6
  33.7 1.8 %collective-permute-done.5.dpair_ref = bf16[16,2048]{1,0:T(8,128)(2,1)S(1)} collective-permute-done((bf16[16,2048]{1,0:T(8,128)(2,1)S(1)}, bf16[16,2048]{1,0:T(8,128)(2,1)S(1)}, u32[]{:S(2)}, u32[]{:S(2)}) %collective-permute-start.5) | collective-permute-done | bytes 65568 | tf_op jit(solution)/shard_map/ppermute | solution.py:448
  35.5 4.8 %collective-permute-done.6.dside_ref = bf16[16,2048]{1,0:T(8,128)(2,1)S(1)} collective-permute-done((bf16[16,2048]{1,0:T(8,128)(2,1)S(1)}, bf16[16,2048]{1,0:T(8,128)(2,1)S(1)}, u32[]{:S(2)}, u32[]{:S(2)}) %collective-permute-start.6) | collective-permute-done | bytes 65568 | tf_op jit(solution)/shard_map/ppermute | solution.py:448
  40.3 4.2 %shard_map.207 = (f32[48,2048]{1,0:T(8,128)S(1)}, f32[48,2048]{1,0:T(8,128)S(1)}, bf16[16,2048]{1,0:T(8,128)(2,1)}, bf16[16,2048]{1,0:T(8,128)(2,1)}) custom-call(s32[4]{0:T(128)S(1)} %pad_add_fusion.place, f32[48,2048]{1,0:T(8,128)S(1)} %reshape.29.disp_ref, f32[80,2176]{1,0:T(8,128)S(1)} %get-tuple-element.12.sum_ref, ...), custom_call_target="tpu_custom_call" | custom-call | flops 1000000000 | bytes 1048576 | tf_op jit(solution)/shard_map/pallas_call | solution.py:499
  44.5 1.5 %collective-permute-start.7 = (bf16[16,2048]{1,0:T(8,128)(2,1)}, bf16[16,2048]{1,0:T(8,128)(2,1)S(1)}, u32[]{:S(2)}, u32[]{:S(2)}) collective-permute-start(bf16[16,2048]{1,0:T(8,128)(2,1)} %get-tuple-element.20), channel_id=1, source_target_pairs={{0,8},{1,9},{2,10},{3,11},{4,12},{5,13},{6,14},{7,15},{8,16},{9,17... | collective-permute-start | bytes 196616 | tf_op jit(solution)/shard_map/ppermute | solution.py:443
  46.0 0.9 %reshape.33 = f32[3,4,4,2048]{3,2,1,0:T(4,128)} reshape(f32[48,2048]{1,0:T(8,128)S(1)} %get-tuple-element.18) | data formatting | bytes 786432 | tf_op jit(solution)/shard_map/reshape | solution.py:511
  46.9 4.6 %collective-permute-done.8.col_ref = bf16[16,2048]{1,0:T(8,128)(2,1)S(1)} collective-permute-done((bf16[16,2048]{1,0:T(8,128)(2,1)}, bf16[16,2048]{1,0:T(8,128)(2,1)S(1)}, u32[]{:S(2)}, u32[]{:S(2)}) %collective-permute-start.8) | collective-permute-done | bytes 65568 | tf_op jit(solution)/shard_map/ppermute | solution.py:443
  51.5 5.1 %collective-permute-done.9.corner_ref = bf16[16,2048]{1,0:T(8,128)(2,1)S(1)} collective-permute-done((bf16[16,2048]{1,0:T(8,128)(2,1)}, bf16[16,2048]{1,0:T(8,128)(2,1)S(1)}, u32[]{:S(2)}, u32[]{:S(2)}) %collective-permute-start.9) | collective-permute-done | bytes 65568 | tf_op jit(solution)/shard_map/ppermute | solution.py:443
  56.6 0.2 shard_map.208
  56.8 0.9 %reshape.34 = f32[3,4,4,2048]{3,2,1,0:T(4,128)} reshape(f32[48,2048]{1,0:T(8,128)S(1)} %shard_map.208) | data formatting | bytes 786432 | tf_op jit(solution)/shard_map/reshape | solution.py:511
  (44 shorter events, 0.3 us)
Async XLA Ops:
  1.3 0.7 %copy-start.17 = (f32[4,4]{1,0:T(4,128)S(1)}, f32[4,4]{1,0:T(4,128)}, u32[]{:S(2)}) copy-start(f32[4,4]{1,0:T(4,128)} %param.23) | copy-start | bytes 196
  2.1 14.5 %copy-start.10 = (f32[5,152,160]{2,1,0:T(8,128)S(1)}, f32[5,152,160]{2,1,0:T(8,128)}, u32[]{:S(2)}) copy-start(f32[5,152,160]{2,1,0:T(8,128)} %constant.58.clone) | copy-start | bytes 1459204
  3.3 0.7 %copy-start.8 = (bf16[48,48]{1,0:T(8,128)(2,1)S(1)}, bf16[48,48]{1,0:T(8,128)(2,1)}, u32[]{:S(2)}) copy-start(bf16[48,48]{1,0:T(8,128)(2,1)} %constant.56.clone.select_ref) | copy-start | bytes 13828
  4.0 11.9 %copy-start.16 = (f32[1,5,1,5]{3,2,1,0:T(1,128)S(1)}, f32[1,5,1,5]{3,2,1,0:T(1,128)}, u32[]{:S(2)}) copy-start(f32[1,5,1,5]{3,2,1,0:T(1,128)} %param.26) | copy-start | bytes 304
  4.0 12.0 %copy-start.14 = (f32[2,1,5,1,5]{4,3,2,1,0:T(1,128)S(1)}, f32[2,1,5,1,5]{4,3,2,1,0:T(1,128)}, u32[]{:S(2)}) copy-start(f32[2,1,5,1,5]{4,3,2,1,0:T(1,128)} %param.24) | copy-start | bytes 604
  4.0 12.2 %copy-start.15 = (f32[2,1,5,1,5]{4,3,2,1,0:T(1,128)S(1)}, f32[2,1,5,1,5]{4,3,2,1,0:T(1,128)}, u32[]{:S(2)}) copy-start(f32[2,1,5,1,5]{4,3,2,1,0:T(1,128)} %param.25) | copy-start | bytes 604
  4.0 12.4 %copy-start.13 = (f32[25,152]{1,0:T(8,128)S(1)}, f32[25,152]{1,0:T(8,128)}, u32[]{:S(2)}) copy-start(f32[25,152]{1,0:T(8,128)} %constant.57.clone) | copy-start | bytes 45604
  4.3 13.1 %copy-start.9 = (f32[5,160,152]{1,2,0:T(8,128)S(1)}, f32[5,160,152]{1,2,0:T(8,128)}, u32[]{:S(2)}) copy-start(f32[5,160,152]{1,2,0:T(8,128)} %constant.59.clone) | copy-start | bytes 1459204
  5.0 17.4 %collective-permute-start.2 = (bf16[16,2176]{1,0:T(8,128)(2,1)}, bf16[16,2176]{1,0:T(8,128)(2,1)}, u32[]{:S(2)}, u32[]{:S(2)}) collective-permute-start(bf16[16,2176]{1,0:T(8,128)(2,1)} %get-tuple-element.26), channel_id=1, source_target_pairs={{0,127},{1,120},{2,121},{3,122},{4,123},{5,124},{6,125},{7,126},{8... | collective-permute-start | bytes 208904 | tf_op jit(solution)/shard_map/ppermute | solution.py:443
  12.6 9.8 %collective-permute-start.1 = (bf16[16,2176]{1,0:T(8,128)(2,1)}, bf16[16,2176]{1,0:T(8,128)(2,1)}, u32[]{:S(2)}, u32[]{:S(2)}) collective-permute-start(bf16[16,2176]{1,0:T(8,128)(2,1)} %get-tuple-element.27), channel_id=1, source_target_pairs={{0,7},{1,0},{2,1},{3,2},{4,3},{5,4},{6,5},{7,6},{8,15},{9,8},{10,9... | collective-permute-start | bytes 208904 | tf_op jit(solution)/shard_map/ppermute | solution.py:443
  12.8 9.7 %collective-permute-start = (bf16[16,2176]{1,0:T(8,128)(2,1)}, bf16[16,2176]{1,0:T(8,128)(2,1)}, u32[]{:S(2)}, u32[]{:S(2)}) collective-permute-start(bf16[16,2176]{1,0:T(8,128)(2,1)} %get-tuple-element.28), channel_id=1, source_target_pairs={{0,120},{1,121},{2,122},{3,123},{4,124},{5,125},{6,126},{7,127},{8... | collective-permute-start | bytes 208904 | tf_op jit(solution)/shard_map/ppermute | solution.py:443
  17.4 0.9 %copy-start.11 = (f32[1,5,1,5,2048]{4,2,3,1,0:T(1,128)S(1)}, f32[1,5,1,5,2048]{4,2,3,1,0:T(1,128)}, u32[]{:S(2)}) copy-start(f32[1,5,1,5,2048]{4,2,3,1,0:T(1,128)} %param.27) | copy-start | bytes 614404
  18.8 0.9 %copy-start.12 = (f32[1,5,1,5,2048]{4,2,3,1,0:T(1,128)S(1)}, f32[1,5,1,5,2048]{4,2,3,1,0:T(1,128)}, u32[]{:S(2)}) copy-start(f32[1,5,1,5,2048]{4,2,3,1,0:T(1,128)} %param.28) | copy-start | bytes 614404
  20.2 1.4 %copy-start.6 = (bf16[128,128]{1,0:T(8,128)(2,1)S(1)}, bf16[128,128]{1,0:T(8,128)(2,1)}, u32[]{:S(2)}) copy-start(bf16[128,128]{1,0:T(8,128)(2,1)} %constant.60.clone.shuffle_ref) | copy-start | bytes 98308
  20.2 2.2 %copy-start.1 = (bf16[16,256,128]{2,1,0:T(8,128)(2,1)S(1)}, bf16[16,256,128]{2,1,0:T(8,128)(2,1)}, u32[]{:S(2)}) copy-start(bf16[16,256,128]{2,1,0:T(8,128)(2,1)} %constant.61.clone.table_ref) | copy-start | bytes 3145732
  20.3 2.1 %copy-start = (bf16[16,128,256]{2,1,0:T(8,128)(2,1)S(1)}, bf16[16,128,256]{2,1,0:T(8,128)(2,1)}, u32[]{:S(2)}) copy-start(bf16[16,128,256]{2,1,0:T(8,128)(2,1)} %constant.62.clone.tback_ref) | copy-start | bytes 3145732
  21.6 1.0 %copy-start.2 = (bf16[152,160]{1,0:T(8,128)(2,1)S(1)}, bf16[152,160]{1,0:T(8,128)(2,1)}, u32[]{:S(2)}) copy-start(bf16[152,160]{1,0:T(8,128)(2,1)} %multiply_reduce_fusion.1.operator_ref) | copy-start | bytes 145924
  21.6 1.0 %copy-start.4 = (bf16[2,64,80]{2,1,0:T(8,128)(2,1)S(1)}, bf16[2,64,80]{2,1,0:T(8,128)(2,1)}, u32[]{:S(2)}) copy-start(bf16[2,64,80]{2,1,0:T(8,128)(2,1)} %constant.63.clone.select_ref) | copy-start | bytes 61444
  22.4 9.2 %copy-start.5 = (bf16[4,32,64]{2,1,0:T(8,128)(2,1)S(1)}, bf16[4,32,64]{2,1,0:T(8,128)(2,1)}, u32[]{:S(2)}) copy-start(bf16[4,32,64]{2,1,0:T(8,128)(2,1)} %constant.64.clone.select_ref) | copy-start | bytes 49156
  27.7 1.3 %collective-permute-start.3 = (bf16[16,2048]{1,0:T(8,128)(2,1)S(1)}, bf16[16,2048]{1,0:T(8,128)(2,1)S(1)}, u32[]{:S(2)}, u32[]{:S(2)}) collective-permute-start(bf16[16,2048]{1,0:T(8,128)(2,1)S(1)} %get-tuple-element.13), channel_id=1, source_target_pairs={{0,8},{8,0},{16,24},{24,16},{32,40},{40,32},{48,56},{56,48},{64,72... | collective-permute-start | bytes 196616 | tf_op jit(solution)/shard_map/ppermute | solution.py:448
  27.8 3.8 %collective-permute-start.4 = (bf16[16,2048]{1,0:T(8,128)(2,1)S(1)}, bf16[16,2048]{1,0:T(8,128)(2,1)S(1)}, u32[]{:S(2)}, u32[]{:S(2)}) collective-permute-start(bf16[16,2048]{1,0:T(8,128)(2,1)S(1)} %get-tuple-element.14), channel_id=1, source_target_pairs={{0,120},{8,16},{16,8},{24,32},{32,24},{40,48},{48,40},{56,64},{64,... | collective-permute-start | bytes 196616 | tf_op jit(solution)/shard_map/ppermute | solution.py:448
  31.6 8.7 %copy-start.3 = (bf16[4,80,64]{2,1,0:T(8,128)(2,1)S(1)}, bf16[4,80,64]{2,1,0:T(8,128)(2,1)}, u32[]{:S(2)}) copy-start(bf16[4,80,64]{2,1,0:T(8,128)(2,1)} %constant.65.clone.select_ref) | copy-start | bytes 122884
  32.3 3.2 %collective-permute-start.5 = (bf16[16,2048]{1,0:T(8,128)(2,1)S(1)}, bf16[16,2048]{1,0:T(8,128)(2,1)S(1)}, u32[]{:S(2)}, u32[]{:S(2)}) collective-permute-start(bf16[16,2048]{1,0:T(8,128)(2,1)S(1)} %get-tuple-element.16), channel_id=1, source_target_pairs={{0,1},{1,0},{2,3},{3,2},{4,5},{5,4},{6,7},{7,6},{8,9},{9,8},{10,11... | collective-permute-start | bytes 196616 | tf_op jit(solution)/shard_map/ppermute | solution.py:448
  33.6 6.7 %collective-permute-start.6 = (bf16[16,2048]{1,0:T(8,128)(2,1)S(1)}, bf16[16,2048]{1,0:T(8,128)(2,1)S(1)}, u32[]{:S(2)}, u32[]{:S(2)}) collective-permute-start(bf16[16,2048]{1,0:T(8,128)(2,1)S(1)} %get-tuple-element.17), channel_id=1, source_target_pairs={{0,7},{1,2},{2,1},{3,4},{4,3},{5,6},{6,5},{7,0},{8,15},{9,10},{10,... | collective-permute-start | bytes 196616 | tf_op jit(solution)/shard_map/ppermute | solution.py:448
  44.5 6.9 %collective-permute-start.8 = (bf16[16,2048]{1,0:T(8,128)(2,1)}, bf16[16,2048]{1,0:T(8,128)(2,1)S(1)}, u32[]{:S(2)}, u32[]{:S(2)}) collective-permute-start(bf16[16,2048]{1,0:T(8,128)(2,1)} %get-tuple-element.21), channel_id=1, source_target_pairs={{0,1},{1,2},{2,3},{3,4},{4,5},{5,6},{6,7},{7,0},{8,9},{9,10},{10,1... | collective-permute-start | bytes 196616 | tf_op jit(solution)/shard_map/ppermute | solution.py:443
  44.5 12.0 %collective-permute-start.9 = (bf16[16,2048]{1,0:T(8,128)(2,1)}, bf16[16,2048]{1,0:T(8,128)(2,1)S(1)}, u32[]{:S(2)}, u32[]{:S(2)}) collective-permute-start(bf16[16,2048]{1,0:T(8,128)(2,1)} %get-tuple-element.20), channel_id=1, source_target_pairs={{0,9},{1,10},{2,11},{3,12},{4,13},{5,14},{6,15},{7,8},{8,17},{9,18... | collective-permute-start | bytes 196616 | tf_op jit(solution)/shard_map/ppermute | solution.py:443
  44.5 12.0 %collective-permute-start.7 = (bf16[16,2048]{1,0:T(8,128)(2,1)}, bf16[16,2048]{1,0:T(8,128)(2,1)S(1)}, u32[]{:S(2)}, u32[]{:S(2)}) collective-permute-start(bf16[16,2048]{1,0:T(8,128)(2,1)} %get-tuple-element.20), channel_id=1, source_target_pairs={{0,8},{1,9},{2,10},{3,11},{4,12},{5,13},{6,14},{7,15},{8,16},{9,17... | collective-permute-start | bytes 196616 | tf_op jit(solution)/shard_map/ppermute | solution.py:443
  46.0 10.6 %copy-start.7 = (bf16[48,48]{1,0:T(8,128)(2,1)S(1)}, bf16[48,48]{1,0:T(8,128)(2,1)}, u32[]{:S(2)}) copy-start(bf16[48,48]{1,0:T(8,128)(2,1)} %constant.66.clone.select_ref) | copy-start | bytes 13828
where the time goes:
time: 58 us; the launch traced here: 57.6 us
  waiting for transfers between devices  20 us (34%)
  starting transfers between devices  14 us (24%)
  Pallas kernels  11.1 us (19%)
  local copies, waits for them, and re-layouts  8.65 us (15%)
  other arithmetic  2.82 us (5%)
  between operations  0.9 us (2%)
    ppermute x6, starting transfers between devices, shifted(): return lax.ppermute(array, ('colat', 'depth'), pairs)  12.4 us
    ppermute x4, waiting for transfers between devices, swapped(): return lax.ppermute(array, axis, pairs)  10.3 us
    ppermute x6, waiting for transfers between devices, shifted(): return lax.ppermute(array, ('colat', 'depth'), pairs)  9.7 us
    pallas_call x1, Pallas kernels, per_device(): call(step_one_kernel, (shape(NODES, WIDTH + LANES), tile, tile, shape(32,...  5.13 us
    pallas_call x1, Pallas kernels, per_device(): call(step_two_kernel, (shape(OWN, WIDTH), shape(OWN, WIDTH), tile, tile),...  4.21 us
    unnamed x36, local copies, waits for them, and re-layouts  2.97 us
    ppermute x4, starting transfers between devices, swapped(): return lax.ppermute(array, axis, pairs)  1.6 us
    reshape x1, local copies, waits for them, and re-layouts, per_device(): prev = previous.reshape(OWN, WIDTH)  1.27 us
  transfers between devices with their start and end apart: 10, of which 6 were waited for; matrix products, arithmetic and copies ran while one was open for 9% of the time, Pallas kernels for 1%

commit v1 on v0

--- a/solution.py
+++ b/solution.py
@@ -116,16 +116,6 @@
     return 12 + comp if n == 4 else 4 * comp + n
 
 
-def first_halo_select():
-    select = np.zeros((48, OWN))
-    for comp in range(3):
-        for n in range(4):
-            select[4 * comp + n, node_row(comp, 0, n)] = 1.0
-            select[16 + 4 * comp + n, node_row(comp, n, 0)] = 1.0
-        select[32 + 12 + comp, node_row(comp, 0, 0)] = 1.0
-    return select.astype(ml_dtypes.bfloat16)
-
-
 def pick(faces):
     select = np.zeros((16 * len(faces), NODES))
     for index, nodes in enumerate(faces):
@@ -165,16 +155,6 @@
             cols = [COL_HIGH, COL_LOW] if par_d == 0 else [COL_LOW, COL_HIGH]
             out[2 * par_c + par_d] = pick(rows + cols).T
     return out.astype(ml_dtypes.bfloat16)
-
-
-def last_select():
-    select = np.zeros((OWN, 48))
-    for comp in range(3):
-        for n in range(4):
-            select[node_row(comp, 0, n), 4 * comp + n] = 1.0
-            select[node_row(comp, n, 0), 16 + 4 * comp + n] = 1.0
-        select[node_row(comp, 0, 0), 32 + 12 + comp] = 1.0
-    return select.astype(ml_dtypes.bfloat16)
 
 
 def turned(value, eighths, scale_sign):
@@ -241,23 +221,56 @@
     return jnp.dot(left, right, preferred_element_type=F32)
 
 
-def first_kernel(disp_ref, meta_ref, select_ref, out_ref):
-    live = meta_ref[:, 1:2]
-    for index in range(8):
-        lanes = slice(256 * index, 256 * (index + 1))
-        value = jnp.where(live > index, disp_ref[:, lanes], 0.0).astype(BF16)
-        out_ref[:, lanes] = dot(select_ref[...], value).astype(BF16)
-    mass = meta_ref[:, 0:1]
-    high = mass.astype(BF16).astype(F32)
-    lane = lax.broadcasted_iota(jnp.int32, (OWN, LANES), 1)
-    info = jnp.where(lane == 0, high, jnp.where(lane == 1, mass - high, jnp.where(lane == 2, live, 0.0)))
-    out_ref[:, WIDTH:] = dot(select_ref[...], info.astype(BF16)).astype(BF16)
+def node_column(scalar, rows):
+    row = lax.broadcasted_iota(jnp.int32, (len(rows), 1), 0)
+    column = jnp.zeros((len(rows), 1), F32)
+    for value in sorted(set(rows)):
+        chosen = functools.reduce(jnp.logical_or, [row == at for at, held in enumerate(rows) if held == value])
+        column = jnp.where(chosen, scalar(value), column)
+    return column
+
+
+def own_rows(ref, lanes):
+    return jnp.concatenate([ref[c, i, :, lanes] for c in range(3) for i in range(4)], axis=0)
+
+
+def own_columns(blocks_ref, mass_ref):
+    rows = [(i, j) for i in range(4) for j in range(4)]
+    live = node_column(lambda at: blocks_ref[at[0], at[1]].astype(F32), rows)
+    mass = node_column(lambda at: mass_ref[at[0], at[1]], rows)
+    return jnp.concatenate([live] * 3, axis=0), jnp.concatenate([mass] * 3, axis=0)
+
+
+def first_kernel(blocks_ref, mass_ref, disp_ref, row_out, col_out, corner_out):
+    faces = (
+        (row_out, [(0, n) for n in range(4)]),
+        (col_out, [(n, 0) for n in range(4)]),
+        (corner_out, [(0, 0)]),
+    )
+    for out, rows in faces:
+        live = node_column(lambda at: blocks_ref[at[0], at[1]].astype(F32), rows)
+        mass = node_column(lambda at: mass_ref[at[0], at[1]], rows)
+        high = mass.astype(BF16).astype(F32)
+        lane = lax.broadcasted_iota(jnp.int32, (len(rows), LANES), 1)
+        info = jnp.where(lane == 0, high, jnp.where(lane == 1, mass - high, jnp.where(lane == 2, live, 0.0)))
+        for c in range(3):
+            for index in range(8):
+                lanes = slice(256 * index, 256 * (index + 1))
+                if out is row_out:
+                    value = disp_ref[c, 0, :, lanes]
+                elif out is col_out:
+                    value = jnp.concatenate([disp_ref[c, n, 0:1, lanes] for n in range(4)], axis=0)
+                else:
+                    value = disp_ref[c, 0, 0:1, lanes]
+                out[c, :, lanes] = jnp.where(live > index, value, 0.0).astype(BF16)
+            out[c, :, WIDTH:] = info.astype(BF16)
 
 
 def material_kernel(lambda_ref, mu_ref, shuffle_ref, out_ref, work):
     for index in range(16):
         lanes = slice(LANES * index, LANES * (index + 1))
-        lam, mu = lambda_ref[:, lanes], mu_ref[:, lanes] * 2.0
+        lam = jnp.concatenate([lambda_ref[i, :, lanes] for i in range(5)], axis=0)
+        mu = jnp.concatenate([mu_ref[i, :, lanes] for i in range(5)], axis=0) * 2.0
         row = lax.broadcasted_iota(jnp.int32, (8, LANES), 0)
         last = jnp.where(row < 6, mu[24:25], jnp.where(row == 6, lam[24:25], 0.0))
         stacked = jnp.concatenate([lam[:24], mu[:24], last], axis=0)
@@ -324,24 +337,32 @@
 
 
 def step_one_kernel(
-    place, disp_ref, prev_ref, meta_ref, row_ref, col_ref, corner_ref,
+    place, blocks_ref, mass_ref, disp_ref, prev_ref, row_ref, col_ref, corner_ref,
     operator_ref, back_ref, table_ref, tback_ref, material_ref, select_ref,
     sum_ref, pair_ref, side_ref, faces_ref,
-    tiles, both, strain, spectrum,
+    own, tiles, both, strain, spectrum,
 ):
     rest_c, rest_d = place[2].astype(F32), place[3].astype(F32)
-    tiles[:16] = row_ref[...].astype(F32) * rest_c + corner_ref[...].astype(F32) * (rest_c * rest_d)
-    tiles[16:] = col_ref[...].astype(F32) * rest_d
+    for lanes in [slice(256 * n, 256 * (n + 1)) for n in range(8)] + [slice(WIDTH, WIDTH + LANES)]:
+        rows = [row_ref[c, :, lanes].astype(F32) * rest_c for c in range(3)]
+        corner = [corner_ref[c, :, lanes].astype(F32) * (rest_c * rest_d) for c in range(3)]
+        cols = [col_ref[c, :, lanes].astype(F32) * rest_d for c in range(3)]
+        width = lanes.stop - lanes.start
+        pieces = rows + corner + [jnp.zeros((1, width), F32)] + cols + [jnp.zeros((4, width), F32)]
+        tiles[:, lanes] = jnp.concatenate(pieces, axis=0)
     info = tiles[:, WIDTH:]
     lane = lax.broadcasted_iota(jnp.int32, (32, LANES), 1)
     halo_info = jnp.where(lane == 0, info[:, 0:1] + info[:, 1:2], jnp.where(lane == 1, info[:, 2:3], 0.0))
-    sum_ref[:OWN, WIDTH:] = meta_ref[...]
+    live, mass = own_columns(blocks_ref, mass_ref)
+    lane = lax.broadcasted_iota(jnp.int32, (OWN, LANES), 1)
+    sum_ref[:OWN, WIDTH:] = jnp.where(lane == 0, mass, jnp.where(lane == 1, live, 0.0))
     sum_ref[OWN:, WIDTH:] = halo_info
-    live = meta_ref[:, 1:2]
 
     def nodes(lanes):
-        own = jnp.where(live > lanes.start // 256, disp_ref[:, lanes], 0.0)
-        return jnp.concatenate([own, tiles[:, lanes]], axis=0)
+        value = own_rows(disp_ref, lanes)
+        own[:, lanes] = 2.0 * value - own_rows(prev_ref, lanes)
+        value = jnp.where(live > lanes.start // 256, value, 0.0)
+        return jnp.concatenate([value, tiles[:, lanes]], axis=0)
 
     mass = sum_ref[:, WIDTH : WIDTH + 1] * (-1.0 / WIDTH)
 
@@ -349,8 +370,7 @@
         for part, value in ((0, re), (1, im)):
             lanes = block(index, part)
             value = mass * value
-            total = 2.0 * disp_ref[:, lanes] - prev_ref[:, lanes] + value[:OWN]
-            total = jnp.concatenate([total, value[OWN:]], axis=0)
+            total = jnp.concatenate([own[:, lanes] + value[:OWN], value[OWN:]], axis=0)
             sum_ref[:, lanes] = total
             sent = dot(select_ref[place[0]], total.astype(BF16)).astype(BF16)
             pair_ref[:, lanes] = sent[:16]
@@ -373,7 +393,7 @@
 def step_two_kernel(
     place, disp_ref, sum_ref, cpair_ref, cside_ref, dpair_ref, dside_ref,
     operator_ref, back_ref, table_ref, tback_ref, material_ref, select_ref,
-    mid_ref, sum_out, row_out, col_out,
+    mid_ref, sum_out, row_out, col_out, corner_out,
     current, both, strain, spectrum,
 ):
     select = select_ref[2 * place[0] + place[1]]
@@ -390,9 +410,16 @@
         for part, value in ((0, re), (1, im)):
             lanes = block(index, part)
             value = mass * value
-            sum_out[:, lanes] = 2.0 * current[:OWN, lanes] - disp_ref[:, lanes] + value[:OWN]
-            row_out[:, lanes] = value[OWN : OWN + 16].astype(BF16)
-            col_out[:, lanes] = value[OWN + 16 :].astype(BF16)
+            total = 2.0 * current[:OWN, lanes] - own_rows(disp_ref, lanes) + value[:OWN]
+            value = value.astype(BF16)
+            for c in range(3):
+                for i in range(4):
+                    at = 16 * c + 4 * i
+                    sum_out[c, i, :, lanes] = total[at : at + 4]
+                at = OWN + 4 * c
+                row_out[c, :, lanes] = value[at : at + 4]
+                corner_out[c, :, lanes] = value[OWN + 12 + c : OWN + 13 + c]
+                col_out[c, :, lanes] = value[at + 16 : at + 20]
 
     forces(
         lambda lanes: current[:, lanes],
@@ -400,24 +427,28 @@
     )
 
 
-def last_kernel(sum_ref, meta_ref, row_ref, col_ref, corner_ref, select_ref, out_ref):
-    live = meta_ref[:, 1:2]
-    for index in range(8):
-        lanes = slice(256 * index, 256 * (index + 1))
-        arrived = jnp.concatenate([row_ref[:, lanes], col_ref[:, lanes], corner_ref[:, lanes]], axis=0)
-        value = sum_ref[:, lanes] + dot(select_ref[...], arrived)
-        out_ref[:, lanes] = jnp.where(live > index, value, 0.0)
-
-
-def call(kernel, outs, scratch=(), scalars=False, inputs=0, flops=0):
+def last_kernel(blocks_ref, sum_ref, row_ref, col_ref, corner_ref, out_ref):
+    for i in range(4):
+        live = node_column(lambda at: blocks_ref[at[0], at[1]].astype(F32), [(i, n) for n in range(4)])
+        first = lax.broadcasted_iota(jnp.int32, (4, 1), 0) == 0
+        for c in range(3):
+            for index in range(8):
+                lanes = slice(256 * index, 256 * (index + 1))
+                arrived = col_ref[c, i : i + 1, lanes].astype(F32)
+                if i == 0:
+                    arrived = arrived + corner_ref[c, :, lanes].astype(F32)
+                value = sum_ref[c, i, :, lanes] + jnp.where(first, arrived, 0.0)
+                if i == 0:
+                    value = value + row_ref[c, :, lanes].astype(F32)
+                out_ref[c, i, :, lanes] = jnp.where(live > index, value, 0.0)
+
+
+def call(kernel, outs, scratch=(), scalars=0, inputs=0, flops=0):
     vmem = pl.BlockSpec(memory_space=pltpu.VMEM)
-    specs = [vmem] * inputs
-    if scalars:
-        specs = [pl.BlockSpec(memory_space=pltpu.SMEM)] + specs
     return pl.pallas_call(
         kernel,
         out_shape=outs,
-        in_specs=specs,
+        in_specs=[pl.BlockSpec(memory_space=pltpu.SMEM)] * scalars + [vmem] * inputs,
         out_specs=jax.tree.map(lambda _: vmem, outs),
         scratch_shapes=list(scratch),
         compiler_params=pltpu.CompilerParams(vmem_limit_bytes=VMEM_LIMIT),
@@ -450,21 +481,14 @@
     def per_device(displacement, previous, node_blocks, inverse_mass, jac_diag, jac_off, inv_radius, lame_l, lame_m):
         at_c, at_d = lax.axis_index("colat"), lax.axis_index("depth")
         place = jnp.stack([at_c % 2, at_d % 2, at_c < bands - 1, at_d < layers - 1]).astype(jnp.int32)
-        disp = displacement.reshape(OWN, WIDTH)
-        prev = previous.reshape(OWN, WIDTH)
-        lane = lax.broadcasted_iota(jnp.int32, (3, 4, 4, LANES), 3)
-        meta = jnp.where(
-            lane == 0,
-            inverse_mass[None, :, :, None],
-            jnp.where(lane == 1, node_blocks.astype(F32)[None, :, :, None], 0.0),
-        ).reshape(OWN, LANES)
-
-        halo = call(first_kernel, shape(OWN, WIDTH + LANES, dtype=BF16), inputs=3)(
-            disp, meta, jnp.asarray(first_halo_select())
+        row_face = shape(3, 4, WIDTH + LANES, dtype=BF16)
+        point = shape(3, 1, WIDTH + LANES, dtype=BF16)
+        row, col, corner = call(first_kernel, (row_face, row_face, point), scalars=2, inputs=1)(
+            node_blocks, inverse_mass, displacement
         )
-        row = shifted(halo[:16], -1, 0)
-        col = shifted(halo[16:32], 0, -1)
-        corner = shifted(halo[32:], -1, -1)
+        corner = shifted(corner, -1, -1)
+        col = shifted(col, 0, -1)
+        row = shifted(row, -1, 0)
 
         factors = jnp.stack(
             [item.reshape(25) for item in (jac_diag[0], jac_off[0], jac_off[1], jac_diag[1], inv_radius)]
@@ -474,7 +498,7 @@
         back = jnp.sum(spread_factors[:, None, :] * jnp.asarray(parts.transpose(0, 2, 1)), axis=0).astype(BF16)
         material = call(
             material_kernel, shape(RADIX, 56, LANES), [pltpu.VMEM((16, 56, LANES), F32)], inputs=3
-        )(lame_l.reshape(25, WIDTH), lame_m.reshape(25, WIDTH), jnp.asarray(lane_shuffle()))
+        )(lame_l.reshape(5, 5, WIDTH), lame_m.reshape(5, 5, WIDTH), jnp.asarray(lane_shuffle()))
 
         work = [
             pltpu.VMEM((2 * NODES, WIDTH), BF16),
@@ -486,29 +510,36 @@
         total, pair, side, faces = call(
             step_one_kernel,
             (shape(NODES, WIDTH + LANES), tile, tile, shape(32, WIDTH, dtype=BF16)),
-            [pltpu.VMEM((32, WIDTH + LANES), F32)] + work,
-            scalars=True, inputs=12, flops=10**9,
-        )(place, disp, prev, meta, row, col, corner, *shared, jnp.asarray(outgoing_select()))
+            [pltpu.VMEM((OWN, WIDTH), F32), pltpu.VMEM((32, WIDTH + LANES), F32)] + work,
+            scalars=3, inputs=11, flops=10**9,
+        )(
+            place, node_blocks, inverse_mass, displacement, previous, row, col, corner,
+            *shared, jnp.asarray(outgoing_select()),
+        )
         cpair = swapped(pair, "colat", 0)
         cside = swapped(side, "colat", 1)
-        pair, side = call(column_kernel, (tile, tile), scalars=True, inputs=4)(
+        pair, side = call(column_kernel, (tile, tile), scalars=1, inputs=4)(
             place, faces, cpair, cside, jnp.asarray(column_select())
         )
         dpair = swapped(pair, "depth", 0)
         dside = swapped(side, "depth", 1)
-        middle, final, row, col = call(
+        row_face = shape(3, 4, WIDTH, dtype=BF16)
+        middle, final, row, col, corner = call(
             step_two_kernel,
-            (shape(OWN, WIDTH), shape(OWN, WIDTH), tile, tile),
+            (
+                shape(OWN, WIDTH), shape(3, 4, 4, WIDTH), row_face, row_face,
+                shape(3, 1, WIDTH, dtype=BF16),
+            ),
             [pltpu.VMEM((NODES, WIDTH), F32)] + work,
-            scalars=True, inputs=12, flops=10**9,
-        )(place, disp, total, cpair, cside, dpair, dside, *shared, jnp.asarray(arrival_select()))
-        corner = shifted(row, 1, 1)
+            scalars=1, inputs=12, flops=10**9,
+        )(place, displacement, total, cpair, cside, dpair, dside, *shared, jnp.asarray(arrival_select()))
+        corner = shifted(corner, 1, 1)
         col = shifted(col, 0, 1)
         row = shifted(row, 1, 0)
-        final = call(last_kernel, shape(OWN, WIDTH), inputs=6)(
-            final, meta, row, col, corner, jnp.asarray(last_select())
+        final = call(last_kernel, shape(3, 4, 4, WIDTH), scalars=1, inputs=4)(
+            node_blocks, final, row, col, corner
         )
-        return middle.reshape(displacement.shape), final.reshape(displacement.shape)
+        return middle.reshape(displacement.shape), final
 
     return jax.shard_map(
         per_device,

time: 58 us -> 57.6 us (level)
  the two profiles are of different devices: /device:TPU:1 before, /device:TPU:0 now
where the time goes in v1:
time: 57.6 us; the launch traced here: 57.2 us
  waiting for transfers between devices  22.4 us (39%)
  starting transfers between devices  12.1 us (21%)
  Pallas kernels  11.9 us (21%)
  local copies, waits for them, and re-layouts  6.8 us (12%)
  other arithmetic  2.3 us (4%)
  between operations  0.91 us (2%)
  matrix products  0.88 us (2%)
    ppermute x4, waiting for transfers between devices, swapped(): return lax.ppermute(array, axis, pairs)  13.5 us
    ppermute x6, starting transfers between devices, shifted(): return lax.ppermute(array, ('colat', 'depth'), pairs)  10.6 us
    ppermute x6, waiting for transfers between devices, shifted(): return lax.ppermute(array, ('colat', 'depth'), pairs)  8.84 us
    pallas_call x1, Pallas kernels, per_device(): call(step_one_kernel, (shape(NODES, WIDTH + LANES), tile, tile, shape(32,...  4.79 us
    unnamed x31, local copies, waits for them, and re-layouts  3.99 us
    pallas_call x1, Pallas kernels, per_device(): call(step_two_kernel, (shape(OWN, WIDTH), shape(3, 4, 4, WIDTH), row_face...  3.53 us
    pallas_call x1, Pallas kernels, per_device(): call(last_kernel, shape(3, 4, 4, WIDTH), scalars=1, inputs=4)  1.5 us
    ppermute x4, starting transfers between devices, swapped(): return lax.ppermute(array, axis, pairs)  1.43 us
  transfers between devices with their start and end apart: 10, of which 5 were waited for; matrix products, arithmetic and copies ran while one was open for 13% of the time, Pallas kernels for 1%

profile of v1, /device:TPU:0, one launch (start us, length us, event | category | flops | bytes accessed | tf_op | source)
XLA Modules:
  0.0 57.2 jit_solution(17827692355021994433)
XLA Ops:
  0.6 0.0 copy-start
  0.6 1.0 %copy-done = f32[3,4,4,2048]{3,2,1,0:T(4,128)S(1)} copy-done((f32[3,4,4,2048]{3,2,1,0:T(4,128)S(1)}, f32[3,4,4,2048]{3,2,1,0:T(4,128)}, u32[]{:S(2)}) %copy-start) | copy-done | bytes 393240
  1.6 0.7 %copy-done.7 = s32[4,4]{1,0:T(4,128)S(1)} copy-done((s32[4,4]{1,0:T(4,128)S(1)}, s32[4,4]{1,0:T(4,128)}, u32[]{:S(2)}) %copy-start.7) | copy-done | bytes 88
  2.3 0.7 %copy-done.9 = f32[4,4]{1,0:T(4,128)S(1)} copy-done((f32[4,4]{1,0:T(4,128)S(1)}, f32[4,4]{1,0:T(4,128)}, u32[]{:S(2)}) %copy-start.9) | copy-done | bytes 88
  3.0 0.7 %shard_map.185 = (bf16[3,4,2176]{2,1,0:T(4,128)(2,1)S(1)}, bf16[3,4,2176]{2,1,0:T(4,128)(2,1)S(1)}, bf16[3,1,2176]{2,1,0:T(2,128)(2,1)S(1)}) custom-call(s32[4,4]{1,0:T(4,128)S(1)} %copy-done.7, f32[4,4]{1,0:T(4,128)S(1)} %copy-done.9, f32[3,4,4,2048]{3,2,1,0:T(4,128)S(1)} %copy-done), custom_call_target="tpu_custom_call" | custom-call | bytes 1048576 | tf_op jit(solution)/shard_map/pallas_call | solution.py:486
  3.7 8.3 %collective-permute-start.2 = (bf16[3,1,2176]{2,1,0:T(2,128)(2,1)S(1)}, bf16[3,1,2176]{2,1,0:T(2,128)(2,1)S(1)}, u32[]{:S(2)}, u32[]{:S(2)}) collective-permute-start(bf16[3,1,2176]{2,1,0:T(2,128)(2,1)S(1)} %get-tuple-element.18), channel_id=1, source_target_pairs={{0,127},{1,120},{2,121},{3,122},{4,123},{5,124},{6,125},{7,126},{8... | collective-permute-start | bytes 39176 | tf_op jit(solution)/shard_map/ppermute | solution.py:474
  12.0 1.1 %collective-permute-start = (bf16[3,4,2176]{2,1,0:T(4,128)(2,1)S(1)}, bf16[3,4,2176]{2,1,0:T(4,128)(2,1)S(1)}, u32[]{:S(2)}, u32[]{:S(2)}) collective-permute-start(bf16[3,4,2176]{2,1,0:T(4,128)(2,1)S(1)} %get-tuple-element.16), channel_id=1, source_target_pairs={{0,120},{1,121},{2,122},{3,123},{4,124},{5,125},{6,126},{7,127},{8... | collective-permute-start | bytes 156680 | tf_op jit(solution)/shard_map/ppermute | solution.py:474
  13.1 1.0 %collective-permute-start.1 = (bf16[3,4,2176]{2,1,0:T(4,128)(2,1)S(1)}, bf16[3,4,2176]{2,1,0:T(4,128)(2,1)S(1)}, u32[]{:S(2)}, u32[]{:S(2)}) collective-permute-start(bf16[3,4,2176]{2,1,0:T(4,128)(2,1)S(1)} %get-tuple-element.17), channel_id=1, source_target_pairs={{0,7},{1,0},{2,1},{3,2},{4,3},{5,4},{6,5},{7,6},{8,15},{9,8},{10,9... | collective-permute-start | bytes 156680 | tf_op jit(solution)/shard_map/ppermute | solution.py:474
  14.1 0.7 %reduce.4 = f32[5,5]{1,0:T(8,128)S(1)} reduce(f32[1,5,1,5]{3,2,1,0:T(1,128)} %param.24, f32[]{:T(128)} %constant.68), dimensions={0,2}, to_apply=%param.24.reduce_sub_computation | reduce | bytes 204 | tf_op args[6]
  14.8 0.1 stack_reshape.3
  14.9 0.7 %slice_reduce_fusion = (f32[5,5]{1,0:T(8,128)S(1)}, f32[5,5]{1,0:T(8,128)S(1)}) fusion(f32[2,1,5,1,5]{4,3,2,1,0:T(1,128)} %param.22), kind=kLoop, calls=%fused_computation.4 | loop fusion | bytes 400 | tf_op jit(solution)/shard_map/slice | solution.py:494
  15.6 0.1 stack_reshape_squeeze.15
  15.7 0.1 stack_reshape_squeeze.12
  15.8 0.7 %slice_reduce_fusion.1 = (f32[5,5]{1,0:T(8,128)S(1)}, f32[5,5]{1,0:T(8,128)S(1)}) fusion(f32[2,1,5,1,5]{4,3,2,1,0:T(1,128)} %param.23), kind=kLoop, calls=%fused_computation.5 | loop fusion | bytes 400 | tf_op jit(solution)/shard_map/slice | solution.py:494
  16.5 0.1 stack_reshape_squeeze.14
  16.6 0.1 stack_reshape_squeeze.13
  16.7 0.9 %fusion = f32[5,152]{1,0:T(8,128)S(1)} fusion(f32[5,25]{1,0:T(8,128)S(1)} %stack.31, f32[25,152]{1,0:T(8,128)} %constant.50.clone), kind=kOutput, calls=%fused_computation.9 | convolution fusion | flops 228000 | bytes 18740 | tf_op jit(solution)/shard_map/dot_general | solution.py:496
  17.6 1.4 %multiply_reduce_fusion.1.operator_ref = bf16[152,160]{1,0:T(8,128)(2,1)S(1)} fusion(f32[5,152,160]{2,1,0:T(8,128)} %constant.51.clone, f32[5,152]{1,0:T(8,128)S(1)} %fusion), kind=kLoop, calls=%fused_computation.1 | loop fusion | flops 218880 | bytes 538080 | tf_op jit(solution)/shard_map/reduce_sum | solution.py:497
  18.9 0.0 copy-start.6
  19.0 0.0 copy-start.3
  19.0 0.2 multiply_reduce_fusion
  19.2 0.0 copy-start.2
  19.2 1.2 %copy_bitcast_fusion = (f32[5,5,2048]{2,1,0:T(8,128)S(1)}, f32[5,5,2048]{2,1,0:T(8,128)S(1)}) fusion(f32[1,5,1,5,2048]{4,2,3,1,0:T(1,128)S(1)} %copy-done.14, f32[1,5,1,5,2048]{4,2,3,1,0:T(1,128)} %param.25), kind=kLoop, calls=%fused_computation.2 | loop fusion | bytes 819200
  20.4 0.1 pad_add_fusion.place
  20.5 0.1 copy.20.back_ref
  20.6 0.0 copy-start.10
  20.6 0.0 copy-start.11
  20.6 0.0 copy-start.12
  20.7 0.7 %shard_map.186.material_ref = f32[16,56,128]{2,1,0:T(8,128)S(1)} custom-call(f32[5,5,2048]{2,1,0:T(8,128)S(1)} %get-tuple-element.35.lambda_ref, f32[5,5,2048]{2,1,0:T(8,128)S(1)} %get-tuple-element.34.mu_ref, bf16[128,128]{1,0:T(8,128)(2,1)S(1)} %copy-done.6), custom_call_target="tpu_custom_call" | custom-call | bytes 1048576 | tf_op jit(solution)/shard_map/pallas_call | solution.py:499
  21.3 0.0 copy-start.5
  21.4 0.2 copy-done.1
  21.6 0.1 copy-done.11
  21.8 4.8 %shard_map.187 = (f32[80,2176]{1,0:T(8,128)S(1)}, bf16[16,2048]{1,0:T(8,128)(2,1)S(1)}, bf16[16,2048]{1,0:T(8,128)(2,1)S(1)}, bf16[32,2048]{1,0:T(8,128)(2,1)S(1)}) custom-call(s32[4]{0:T(128)S(1)} %pad_add_fusion.place, s32[4,4]{1,0:T(4,128)S(1)} %copy-done.8, f32[4,4]{1,0:T(4,128)S(1)} %copy-done.10, f32[3,4,4,2048]{3,2,1,0:T(4,128)S(1)} %copy-done.1, ...), custom_call_target="tpu_custom_call" | custom-call | flops 1000000000 | bytes 1048576 | tf_op jit(solution)/shard_map/pallas_call | solution.py:510
  26.6 0.1 collective-permute-start.3
  26.6 0.2 collective-permute-start.4
  26.9 1.0 %collective-permute-done.3.pair_ref.cpair_ref = bf16[16,2048]{1,0:T(8,128)(2,1)S(1)} collective-permute-done((bf16[16,2048]{1,0:T(8,128)(2,1)S(1)}, bf16[16,2048]{1,0:T(8,128)(2,1)S(1)}, u32[]{:S(2)}, u32[]{:S(2)}) %collective-permute-start.3) | collective-permute-done | bytes 65568 | tf_op jit(solution)/shard_map/ppermute | solution.py:479
  27.9 4.6 %collective-permute-done.4.side_ref.cside_ref = bf16[16,2048]{1,0:T(8,128)(2,1)S(1)} collective-permute-done((bf16[16,2048]{1,0:T(8,128)(2,1)S(1)}, bf16[16,2048]{1,0:T(8,128)(2,1)S(1)}, u32[]{:S(2)}, u32[]{:S(2)}) %collective-permute-start.4) | collective-permute-done | bytes 65568 | tf_op jit(solution)/shard_map/ppermute | solution.py:479
  32.5 0.7 %shard_map.188 = (bf16[16,2048]{1,0:T(8,128)(2,1)S(1)}, bf16[16,2048]{1,0:T(8,128)(2,1)S(1)}) custom-call(s32[4]{0:T(128)S(1)} %pad_add_fusion.place, bf16[32,2048]{1,0:T(8,128)(2,1)S(1)} %get-tuple-element.22.faces_ref, bf16[16,2048]{1,0:T(8,128)(2,1)S(1)} %collective-permute-done.3.pair_ref.cpair_ref, ...), custom_call_target="tpu_custom_call" | custom-call | bytes 1048576 | tf_op jit(solution)/shard_map/pallas_call | solution.py:521
  33.2 1.1 %collective-permute-start.5 = (bf16[16,2048]{1,0:T(8,128)(2,1)S(1)}, bf16[16,2048]{1,0:T(8,128)(2,1)S(1)}, u32[]{:S(2)}, u32[]{:S(2)}) collective-permute-start(bf16[16,2048]{1,0:T(8,128)(2,1)S(1)} %get-tuple-element.23), channel_id=1, source_target_pairs={{0,1},{1,0},{2,3},{3,2},{4,5},{5,4},{6,7},{7,6},{8,9},{9,8},{10,11... | collective-permute-start | bytes 196616 | tf_op jit(solution)/shard_map/ppermute | solution.py:479
  34.3 3.2 %collective-permute-done.5.dpair_ref = bf16[16,2048]{1,0:T(8,128)(2,1)S(1)} collective-permute-done((bf16[16,2048]{1,0:T(8,128)(2,1)S(1)}, bf16[16,2048]{1,0:T(8,128)(2,1)S(1)}, u32[]{:S(2)}, u32[]{:S(2)}) %collective-permute-start.5) | collective-permute-done | bytes 65568 | tf_op jit(solution)/shard_map/ppermute | solution.py:479
  37.6 4.6 %collective-permute-done.6.dside_ref = bf16[16,2048]{1,0:T(8,128)(2,1)S(1)} collective-permute-done((bf16[16,2048]{1,0:T(8,128)(2,1)S(1)}, bf16[16,2048]{1,0:T(8,128)(2,1)S(1)}, u32[]{:S(2)}, u32[]{:S(2)}) %collective-permute-start.6) | collective-permute-done | bytes 65568 | tf_op jit(solution)/shard_map/ppermute | solution.py:479
  42.2 3.5 %shard_map.189 = (f32[48,2048]{1,0:T(8,128)S(1)}, f32[3,4,4,2048]{3,2,1,0:T(4,128)S(1)}, bf16[3,4,2048]{2,1,0:T(4,128)(2,1)S(1)}, bf16[3,4,2048]{2,1,0:T(4,128)(2,1)S(1)}, bf16[3,1,2048]{2,1,0:T(2,128)(2,1)S(1)}) custom-call(s32[4]{0:T(128)S(1)} %pad_add_fusion.place, f32[3,4,4,2048]{3,2,1,0:T(4,128)S(1)} %copy-done.1, ...), custom_call_target="tpu_custom_call" | custom-call | flops 1000000000 | bytes 1048576 | tf_op jit(solution)/shard_map/pallas_call | solution.py:527
  45.8 0.1 collective-permute-start.7
  45.8 0.1 collective-permute-start.8
  45.9 0.1 collective-permute-start.9
  46.0 0.9 %reshape.17 = f32[3,4,4,2048]{3,2,1,0:T(4,128)} reshape(f32[48,2048]{1,0:T(8,128)S(1)} %get-tuple-element.25) | data formatting | bytes 786432 | tf_op jit(solution)/shard_map/reshape | solution.py:542
  46.9 8.8 %collective-permute-done.9.corner_ref = bf16[3,1,2048]{2,1,0:T(2,128)(2,1)S(1)} collective-permute-done((bf16[3,1,2048]{2,1,0:T(2,128)(2,1)S(1)}, bf16[3,1,2048]{2,1,0:T(2,128)(2,1)S(1)}, u32[]{:S(2)}, u32[]{:S(2)}) %collective-permute-start.9) | collective-permute-done | bytes 12320 | tf_op jit(solution)/shard_map/ppermute | solution.py:474
  55.7 1.5 %shard_map.190 = f32[3,4,4,2048]{3,2,1,0:T(4,128)} custom-call(s32[4,4]{1,0:T(4,128)S(1)} %copy-done.8, f32[3,4,4,2048]{3,2,1,0:T(4,128)S(1)} %get-tuple-element.26.sum_ref, bf16[3,4,2048]{2,1,0:T(4,128)(2,1)S(1)} %collective-permute-done.7.row_ref, bf16[3,4,2048]{2,1,0:T(4,128)(2,1)S(1)} %collective-permute-done.8.col_ref, ...), custom_call_target="tpu_custom_call" | custom-call | bytes 1048576 | tf_op jit(solution)/shard_map/pallas_call | solution.py:539
  (24 shorter events, 0.1 us)
Async XLA Ops:
  0.6 1.0 %copy-start = (f32[3,4,4,2048]{3,2,1,0:T(4,128)S(1)}, f32[3,4,4,2048]{3,2,1,0:T(4,128)}, u32[]{:S(2)}) copy-start(f32[3,4,4,2048]{3,2,1,0:T(4,128)} %disp_ref.5) | copy-start | bytes 1179652
  1.6 0.7 %copy-start.7 = (s32[4,4]{1,0:T(4,128)S(1)}, s32[4,4]{1,0:T(4,128)}, u32[]{:S(2)}) copy-start(s32[4,4]{1,0:T(4,128)} %blocks_ref.5) | copy-start | bytes 196
  2.3 0.7 %copy-start.9 = (f32[4,4]{1,0:T(4,128)S(1)}, f32[4,4]{1,0:T(4,128)}, u32[]{:S(2)}) copy-start(f32[4,4]{1,0:T(4,128)} %mass_ref.3) | copy-start | bytes 196
  3.0 15.9 %copy-start.13 = (f32[5,160,152]{1,2,0:T(8,128)S(1)}, f32[5,160,152]{1,2,0:T(8,128)}, u32[]{:S(2)}) copy-start(f32[5,160,152]{1,2,0:T(8,128)} %constant.52.clone) | copy-start | bytes 1459204
  3.7 17.6 %collective-permute-start.2 = (bf16[3,1,2176]{2,1,0:T(2,128)(2,1)S(1)}, bf16[3,1,2176]{2,1,0:T(2,128)(2,1)S(1)}, u32[]{:S(2)}, u32[]{:S(2)}) collective-permute-start(bf16[3,1,2176]{2,1,0:T(2,128)(2,1)S(1)} %get-tuple-element.18), channel_id=1, source_target_pairs={{0,127},{1,120},{2,121},{3,122},{4,123},{5,124},{6,125},{7,126},{8... | collective-permute-start | bytes 39176 | tf_op jit(solution)/shard_map/ppermute | solution.py:474
  12.0 9.4 %collective-permute-start = (bf16[3,4,2176]{2,1,0:T(4,128)(2,1)S(1)}, bf16[3,4,2176]{2,1,0:T(4,128)(2,1)S(1)}, u32[]{:S(2)}, u32[]{:S(2)}) collective-permute-start(bf16[3,4,2176]{2,1,0:T(4,128)(2,1)S(1)} %get-tuple-element.16), channel_id=1, source_target_pairs={{0,120},{1,121},{2,122},{3,123},{4,124},{5,125},{6,126},{7,127},{8... | collective-permute-start | bytes 156680 | tf_op jit(solution)/shard_map/ppermute | solution.py:474
  13.1 8.2 %collective-permute-start.1 = (bf16[3,4,2176]{2,1,0:T(4,128)(2,1)S(1)}, bf16[3,4,2176]{2,1,0:T(4,128)(2,1)S(1)}, u32[]{:S(2)}, u32[]{:S(2)}) collective-permute-start(bf16[3,4,2176]{2,1,0:T(4,128)(2,1)S(1)} %get-tuple-element.17), channel_id=1, source_target_pairs={{0,7},{1,0},{2,1},{3,2},{4,3},{5,4},{6,5},{7,6},{8,15},{9,8},{10,9... | collective-permute-start | bytes 156680 | tf_op jit(solution)/shard_map/ppermute | solution.py:474
  17.6 1.6 %copy-start.14 = (f32[1,5,1,5,2048]{4,2,3,1,0:T(1,128)S(1)}, f32[1,5,1,5,2048]{4,2,3,1,0:T(1,128)}, u32[]{:S(2)}) copy-start(f32[1,5,1,5,2048]{4,2,3,1,0:T(1,128)} %param.26) | copy-start | bytes 614404
  18.9 1.6 %copy-start.6 = (bf16[128,128]{1,0:T(8,128)(2,1)S(1)}, bf16[128,128]{1,0:T(8,128)(2,1)}, u32[]{:S(2)}) copy-start(bf16[128,128]{1,0:T(8,128)(2,1)} %constant.53.clone.shuffle_ref) | copy-start | bytes 98308
  19.0 2.4 %copy-start.3 = (bf16[16,256,128]{2,1,0:T(8,128)(2,1)S(1)}, bf16[16,256,128]{2,1,0:T(8,128)(2,1)}, u32[]{:S(2)}) copy-start(bf16[16,256,128]{2,1,0:T(8,128)(2,1)} %constant.54.clone.table_ref) | copy-start | bytes 3145732
  19.2 2.2 %copy-start.2 = (bf16[16,128,256]{2,1,0:T(8,128)(2,1)S(1)}, bf16[16,128,256]{2,1,0:T(8,128)(2,1)}, u32[]{:S(2)}) copy-start(bf16[16,128,256]{2,1,0:T(8,128)(2,1)} %constant.55.clone.tback_ref) | copy-start | bytes 3145732
  20.6 1.0 %copy-start.1 = (f32[3,4,4,2048]{3,2,1,0:T(4,128)S(1)}, f32[3,4,4,2048]{3,2,1,0:T(4,128)}, u32[]{:S(2)}) copy-start(f32[3,4,4,2048]{3,2,1,0:T(4,128)} %disp_ref.5) | copy-start | bytes 1179652
  20.6 1.0 %copy-start.8 = (s32[4,4]{1,0:T(4,128)S(1)}, s32[4,4]{1,0:T(4,128)}, u32[]{:S(2)}) copy-start(s32[4,4]{1,0:T(4,128)} %blocks_ref.5) | copy-start | bytes 196
  20.6 1.0 %copy-start.10 = (f32[4,4]{1,0:T(4,128)S(1)}, f32[4,4]{1,0:T(4,128)}, u32[]{:S(2)}) copy-start(f32[4,4]{1,0:T(4,128)} %mass_ref.3) | copy-start | bytes 196
  20.6 1.1 %copy-start.11 = (f32[3,4,4,2048]{3,2,1,0:T(4,128)S(1)}, f32[3,4,4,2048]{3,2,1,0:T(4,128)}, u32[]{:S(2)}) copy-start(f32[3,4,4,2048]{3,2,1,0:T(4,128)} %prev_ref.1) | copy-start | bytes 1179652
  20.6 1.1 %copy-start.12 = (bf16[2,64,80]{2,1,0:T(8,128)(2,1)S(1)}, bf16[2,64,80]{2,1,0:T(8,128)(2,1)}, u32[]{:S(2)}) copy-start(bf16[2,64,80]{2,1,0:T(8,128)(2,1)} %constant.56.clone.select_ref) | copy-start | bytes 61444
  21.3 11.2 %copy-start.5 = (bf16[4,32,64]{2,1,0:T(8,128)(2,1)S(1)}, bf16[4,32,64]{2,1,0:T(8,128)(2,1)}, u32[]{:S(2)}) copy-start(bf16[4,32,64]{2,1,0:T(8,128)(2,1)} %constant.57.clone.select_ref) | copy-start | bytes 49156
  26.6 1.3 %collective-permute-start.3 = (bf16[16,2048]{1,0:T(8,128)(2,1)S(1)}, bf16[16,2048]{1,0:T(8,128)(2,1)S(1)}, u32[]{:S(2)}, u32[]{:S(2)}) collective-permute-start(bf16[16,2048]{1,0:T(8,128)(2,1)S(1)} %get-tuple-element.20), channel_id=1, source_target_pairs={{0,8},{8,0},{16,24},{24,16},{32,40},{40,32},{48,56},{56,48},{64,72... | collective-permute-start | bytes 196616 | tf_op jit(solution)/shard_map/ppermute | solution.py:479
  26.6 5.9 %collective-permute-start.4 = (bf16[16,2048]{1,0:T(8,128)(2,1)S(1)}, bf16[16,2048]{1,0:T(8,128)(2,1)S(1)}, u32[]{:S(2)}, u32[]{:S(2)}) collective-permute-start(bf16[16,2048]{1,0:T(8,128)(2,1)S(1)} %get-tuple-element.21), channel_id=1, source_target_pairs={{0,120},{8,16},{16,8},{24,32},{32,24},{40,48},{48,40},{56,64},{64,... | collective-permute-start | bytes 196616 | tf_op jit(solution)/shard_map/ppermute | solution.py:479
  32.5 9.7 %copy-start.4 = (bf16[4,80,64]{2,1,0:T(8,128)(2,1)S(1)}, bf16[4,80,64]{2,1,0:T(8,128)(2,1)}, u32[]{:S(2)}) copy-start(bf16[4,80,64]{2,1,0:T(8,128)(2,1)} %constant.58.clone.select_ref) | copy-start | bytes 122884
  33.2 4.3 %collective-permute-start.5 = (bf16[16,2048]{1,0:T(8,128)(2,1)S(1)}, bf16[16,2048]{1,0:T(8,128)(2,1)S(1)}, u32[]{:S(2)}, u32[]{:S(2)}) collective-permute-start(bf16[16,2048]{1,0:T(8,128)(2,1)S(1)} %get-tuple-element.23), channel_id=1, source_target_pairs={{0,1},{1,0},{2,3},{3,2},{4,5},{5,4},{6,7},{7,6},{8,9},{9,8},{10,11... | collective-permute-start | bytes 196616 | tf_op jit(solution)/shard_map/ppermute | solution.py:479
  34.3 7.9 %collective-permute-start.6 = (bf16[16,2048]{1,0:T(8,128)(2,1)S(1)}, bf16[16,2048]{1,0:T(8,128)(2,1)S(1)}, u32[]{:S(2)}, u32[]{:S(2)}) collective-permute-start(bf16[16,2048]{1,0:T(8,128)(2,1)S(1)} %get-tuple-element.24), channel_id=1, source_target_pairs={{0,7},{1,2},{2,1},{3,4},{4,3},{5,6},{6,5},{7,0},{8,15},{9,10},{10,... | collective-permute-start | bytes 196616 | tf_op jit(solution)/shard_map/ppermute | solution.py:479
  45.8 9.9 %collective-permute-start.7 = (bf16[3,4,2048]{2,1,0:T(4,128)(2,1)S(1)}, bf16[3,4,2048]{2,1,0:T(4,128)(2,1)S(1)}, u32[]{:S(2)}, u32[]{:S(2)}) collective-permute-start(bf16[3,4,2048]{2,1,0:T(4,128)(2,1)S(1)} %get-tuple-element.27), channel_id=1, source_target_pairs={{0,8},{1,9},{2,10},{3,11},{4,12},{5,13},{6,14},{7,15},{8,16},{9,17... | collective-permute-start | bytes 147464 | tf_op jit(solution)/shard_map/ppermute | solution.py:474
  45.8 9.9 %collective-permute-start.8 = (bf16[3,4,2048]{2,1,0:T(4,128)(2,1)S(1)}, bf16[3,4,2048]{2,1,0:T(4,128)(2,1)S(1)}, u32[]{:S(2)}, u32[]{:S(2)}) collective-permute-start(bf16[3,4,2048]{2,1,0:T(4,128)(2,1)S(1)} %get-tuple-element.28), channel_id=1, source_target_pairs={{0,1},{1,2},{2,3},{3,4},{4,5},{5,6},{6,7},{7,0},{8,9},{9,10},{10,1... | collective-permute-start | bytes 147464 | tf_op jit(solution)/shard_map/ppermute | solution.py:474
  45.9 9.8 %collective-permute-start.9 = (bf16[3,1,2048]{2,1,0:T(2,128)(2,1)S(1)}, bf16[3,1,2048]{2,1,0:T(2,128)(2,1)S(1)}, u32[]{:S(2)}, u32[]{:S(2)}) collective-permute-start(bf16[3,1,2048]{2,1,0:T(2,128)(2,1)S(1)} %get-tuple-element.29), channel_id=1, source_target_pairs={{0,9},{1,10},{2,11},{3,12},{4,13},{5,14},{6,15},{7,8},{8,17},{9,18... | collective-permute-start | bytes 36872 | tf_op jit(solution)/shard_map/ppermute | solution.py:474

commit v2 on v1

--- a/solution.py
+++ b/solution.py
@@ -52,7 +52,7 @@
 def strain_terms():
     deriv = gll_derivative()
     parts = np.zeros((5, STRAINS, 2 * NODES))
-    node_of = np.zeros((STRAINS, 25))
+    place_of = np.zeros((2, STRAINS, 5))
     half = math.sqrt(0.5)
     for i in range(5):
         for j in range(5):
@@ -81,10 +81,11 @@
             radial(5, 2, 1, half)
             grad(5, True, 1, half)
             for strain in range(6):
-                node_of[strain_row(strain, node), node] = 1.0
+                place_of[0, strain_row(strain, node), i] = 1.0
+                place_of[1, strain_row(strain, node), j] = 1.0
     parts[:, 150] = parts[:, 144] + parts[:, 145] + parts[:, 146]
-    node_of[150, 24] = 1.0
-    return parts.astype(np.float32), node_of.astype(np.float32)
+    place_of[:, 150, 4] = 1.0
+    return parts.astype(np.float32), place_of.astype(np.float32)
 
 
 def sample_tables():
@@ -234,14 +235,17 @@
     return jnp.concatenate([ref[c, i, :, lanes] for c in range(3) for i in range(4)], axis=0)
 
 
-def own_columns(blocks_ref, mass_ref):
-    rows = [(i, j) for i in range(4) for j in range(4)]
-    live = node_column(lambda at: blocks_ref[at[0], at[1]].astype(F32), rows)
-    mass = node_column(lambda at: mass_ref[at[0], at[1]], rows)
-    return jnp.concatenate([live] * 3, axis=0), jnp.concatenate([mass] * 3, axis=0)
-
-
-def first_kernel(blocks_ref, mass_ref, disp_ref, row_out, col_out, corner_out):
+def first_kernel(blocks_hbm, mass_hbm, disp_hbm, row_out, col_out, corner_out, blocks_ref, mass_ref, disp_ref, sems):
+    loads = [
+        pltpu.make_async_copy(source, target, sems.at[n])
+        for n, (source, target) in enumerate(
+            ((blocks_hbm, blocks_ref), (mass_hbm, mass_ref), (disp_hbm, disp_ref))
+        )
+    ]
+    for load in loads:
+        load.start()
+    for load in loads:
+        load.wait()
     faces = (
         (row_out, [(0, n) for n in range(4)]),
         (col_out, [(n, 0) for n in range(4)]),
@@ -266,27 +270,64 @@
             out[c, :, WIDTH:] = info.astype(BF16)
 
 
-def material_kernel(lambda_ref, mu_ref, shuffle_ref, out_ref, work):
-    for index in range(16):
-        lanes = slice(LANES * index, LANES * (index + 1))
-        lam = jnp.concatenate([lambda_ref[i, :, lanes] for i in range(5)], axis=0)
-        mu = jnp.concatenate([mu_ref[i, :, lanes] for i in range(5)], axis=0) * 2.0
-        row = lax.broadcasted_iota(jnp.int32, (8, LANES), 0)
-        last = jnp.where(row < 6, mu[24:25], jnp.where(row == 6, lam[24:25], 0.0))
-        stacked = jnp.concatenate([lam[:24], mu[:24], last], axis=0)
-        high = stacked.astype(BF16)
-        low = (stacked - high.astype(F32)).astype(BF16)
-        shuffled = dot(high, shuffle_ref[...]) + dot(low, shuffle_ref[...])
-        work[index] = shuffled if index == 0 else pltpu.roll(shuffled, 8 * index, 1)
+def exact_dot(left, right):
+    return jnp.dot(left, right, preferred_element_type=F32, precision=lax.Precision.HIGHEST)
+
+
+def prepare_kernel(
+    place, blocks_ref, mass_ref, disp_ref, prev_ref, diag_ref, off_ref, radius_ref, lambda_ref, mu_ref,
+    parts_ref, place_of_ref, shuffle_ref, outgoing_ref, column_ref, arrival_ref,
+    operator_out, back_out, material_out, own_out, free_out, info_out, outgoing_out, column_out, arrival_out,
+    shuffled,
+):
+    operator = jnp.zeros((STRAINS, 2 * NODES), F32)
+    for term, factor in enumerate((diag_ref[0], off_ref[0], off_ref[1], diag_ref[1], radius_ref[...])):
+        spread_i = exact_dot(place_of_ref[0], factor) * place_of_ref[1]
+        operator = operator + parts_ref[term] * exact_dot(spread_i, jnp.ones((5, 2 * NODES), F32))
+    operator_out[...] = operator.astype(BF16)
+    back_out[...] = operator.T.astype(BF16)
+
+    nodes = [(i, j) for i in range(4) for j in range(4)]
+    live = jnp.concatenate([node_column(lambda at: blocks_ref[at[0], at[1]].astype(F32), nodes)] * 3, axis=0)
+    mass = jnp.concatenate([node_column(lambda at: mass_ref[at[0], at[1]], nodes)] * 3, axis=0)
+    lane = lax.broadcasted_iota(jnp.int32, (OWN, LANES), 1)
+    info_out[:OWN] = jnp.where(lane == 0, mass, jnp.where(lane == 1, live, 0.0))
+    lane = lax.broadcasted_iota(jnp.int32, (8, LANES), 1)
+    rests = jnp.where(lane == 0, place[2].astype(F32), jnp.where(lane == 1, place[3].astype(F32), 0.0))
+    info_out[OWN:] = rests
+    for index in range(8):
+        lanes = slice(256 * index, 256 * (index + 1))
+        value = jnp.where(live > index, own_rows(disp_ref, lanes), 0.0)
+        own_out[:, lanes] = value
+        free_out[:, lanes] = jnp.where(live > index, 2.0 * value - own_rows(prev_ref, lanes), 0.0)
+
+    outgoing_out[...] = outgoing_ref[place[0]]
+    column_out[...] = column_ref[2 * place[0] + place[1]]
+    arrival_out[...] = arrival_ref[2 * place[0] + place[1]]
+
+    for which, (ref, factor) in enumerate(((lambda_ref, 1.0), (mu_ref, 2.0))):
+        value = ref[...] * factor
+        high = value.astype(BF16)
+        low = (value - high.astype(F32)).astype(BF16)
+        shuffled[which] = dot(high, shuffle_ref[...]) + dot(low, shuffle_ref[...])
     group = lax.broadcasted_iota(jnp.int32, (8, LANES), 1) // 8
+    row = lax.broadcasted_iota(jnp.int32, (8, LANES), 0)
     for rows in range(7):
-        part = slice(8 * rows, 8 * rows + 8)
-        held = [work[(16 - index) % 16, part] for index in range(16)]
+        held = []
+        for s in range(16):
+            if rows < 6:
+                value = shuffled[rows // 3, pl.ds(128 * (rows % 3) + s, 8, stride=16), :]
+            else:
+                at = slice(384 + s, 385 + s)
+                value = jnp.where(row < 6, shuffled[1, at], jnp.where(row == 6, shuffled[0, at], 0.0))
+            held.append(value if s == 0 else pltpu.roll(value, 8 * s, 1))
+        held = [held[(16 - index) % 16] for index in range(16)]
         for bit in range(4):
             chosen = (group >> bit) % 2 == 1
             held = [jnp.where(chosen, held[(index - (1 << bit)) % 16], held[index]) for index in range(16)]
         for index in range(16):
-            out_ref[index, part] = held[index] if index == 0 else pltpu.roll(held[index], LANES - 8 * index, 1)
+            value = held[index] if index == 0 else pltpu.roll(held[index], LANES - 8 * index, 1)
+            material_out[index, 8 * rows : 8 * rows + 8] = value
 
 
 def forces(nodes, operator_ref, back_ref, table_ref, tback_ref, material_ref, both, strain, spectrum, emit):
@@ -301,9 +342,8 @@
         lanes = slice(256 * index, 256 * (index + 1))
         strain[:, lanes] = dot(operator_ref[...], both[:, lanes])
 
-    @pl.loop(0, STRAINS // 8)
-    def _(group):
-        rows = pl.ds(pl.multiple_of(group * 8, 8), 8)
+    for group in range(STRAINS // 8):
+        rows = slice(8 * group, 8 * group + 8)
         values = [(strain[rows, block(b, 0)], strain[rows, block(b, 1)]) for b in range(8)]
         for k0, (re, im) in enumerate(spread(values)):
             spectrum[k0, rows, :LANES] = re
@@ -319,9 +359,8 @@
         stress = jnp.concatenate(stress, axis=0).astype(BF16)
         spectrum[k0] = dot(stress, tback_ref[k0])
 
-    @pl.loop(0, STRAINS // 8)
-    def _(group):
-        rows = pl.ds(pl.multiple_of(group * 8, 8), 8)
+    for group in range(STRAINS // 8):
+        rows = slice(8 * group, 8 * group + 8)
         values = [(spectrum[k0, rows, :LANES], spectrum[k0, rows, LANES:]) for k0 in range(RADIX)]
         for b, (re, im) in enumerate(gathered(values)):
             strain[rows, block(b, 0)] = re
@@ -337,12 +376,12 @@
 
 
 def step_one_kernel(
-    place, blocks_ref, mass_ref, disp_ref, prev_ref, row_ref, col_ref, corner_ref,
+    own_ref, free_ref, info_ref, row_ref, col_ref, corner_ref,
     operator_ref, back_ref, table_ref, tback_ref, material_ref, select_ref,
     sum_ref, pair_ref, side_ref, faces_ref,
-    own, tiles, both, strain, spectrum,
+    tiles, both, strain, spectrum,
 ):
-    rest_c, rest_d = place[2].astype(F32), place[3].astype(F32)
+    rest_c, rest_d = info_ref[OWN : OWN + 1, 0:1], info_ref[OWN : OWN + 1, 1:2]
     for lanes in [slice(256 * n, 256 * (n + 1)) for n in range(8)] + [slice(WIDTH, WIDTH + LANES)]:
         rows = [row_ref[c, :, lanes].astype(F32) * rest_c for c in range(3)]
         corner = [corner_ref[c, :, lanes].astype(F32) * (rest_c * rest_d) for c in range(3)]
@@ -352,65 +391,60 @@
         tiles[:, lanes] = jnp.concatenate(pieces, axis=0)
     info = tiles[:, WIDTH:]
     lane = lax.broadcasted_iota(jnp.int32, (32, LANES), 1)
-    halo_info = jnp.where(lane == 0, info[:, 0:1] + info[:, 1:2], jnp.where(lane == 1, info[:, 2:3], 0.0))
-    live, mass = own_columns(blocks_ref, mass_ref)
-    lane = lax.broadcasted_iota(jnp.int32, (OWN, LANES), 1)
-    sum_ref[:OWN, WIDTH:] = jnp.where(lane == 0, mass, jnp.where(lane == 1, live, 0.0))
-    sum_ref[OWN:, WIDTH:] = halo_info
+    sum_ref[:OWN, WIDTH:] = info_ref[:OWN]
+    sum_ref[OWN:, WIDTH:] = jnp.where(
+        lane == 0, info[:, 0:1] + info[:, 1:2], jnp.where(lane == 1, info[:, 2:3], 0.0)
+    )
+    mass = sum_ref[:, WIDTH : WIDTH + 1] * (-1.0 / WIDTH)
 
     def nodes(lanes):
-        value = own_rows(disp_ref, lanes)
-        own[:, lanes] = 2.0 * value - own_rows(prev_ref, lanes)
-        value = jnp.where(live > lanes.start // 256, value, 0.0)
-        return jnp.concatenate([value, tiles[:, lanes]], axis=0)
-
-    mass = sum_ref[:, WIDTH : WIDTH + 1] * (-1.0 / WIDTH)
+        return jnp.concatenate([own_ref[:, lanes], tiles[:, lanes]], axis=0)
 
     def emit(index, re, im):
         for part, value in ((0, re), (1, im)):
             lanes = block(index, part)
             value = mass * value
-            total = jnp.concatenate([own[:, lanes] + value[:OWN], value[OWN:]], axis=0)
-            sum_ref[:, lanes] = total
-            sent = dot(select_ref[place[0]], total.astype(BF16)).astype(BF16)
-            pair_ref[:, lanes] = sent[:16]
-            side_ref[:, lanes] = sent[16:32]
-            faces_ref[:, lanes] = sent[32:]
+            sum_ref[:OWN, lanes] = free_ref[:, lanes] + value[:OWN]
+            sum_ref[OWN:, lanes] = value[OWN:]
+        lanes = slice(256 * index, 256 * (index + 1))
+        sent = dot(select_ref[...], sum_ref[:, lanes].astype(BF16)).astype(BF16)
+        pair_ref[:, lanes] = sent[:16]
+        side_ref[:, lanes] = sent[16:32]
+        faces_ref[:, lanes] = sent[32:]
 
     forces(nodes, operator_ref, back_ref, table_ref, tback_ref, material_ref, both, strain, spectrum, emit)
 
 
-def column_kernel(place, faces_ref, pair_ref, side_ref, select_ref, pair_out, side_out):
-    select = select_ref[2 * place[0] + place[1]]
+def column_kernel(faces_ref, pair_ref, side_ref, select_ref, pair_out, side_out):
     for index in range(8):
         lanes = slice(256 * index, 256 * (index + 1))
         stacked = jnp.concatenate([faces_ref[:, lanes], pair_ref[:, lanes], side_ref[:, lanes]], axis=0)
-        sent = dot(select, stacked).astype(BF16)
+        sent = dot(select_ref[...], stacked).astype(BF16)
         pair_out[:, lanes] = sent[:16]
         side_out[:, lanes] = sent[16:]
 
 
 def step_two_kernel(
-    place, disp_ref, sum_ref, cpair_ref, cside_ref, dpair_ref, dside_ref,
+    own_ref, sum_ref, cpair_ref, cside_ref, dpair_ref, dside_ref,
     operator_ref, back_ref, table_ref, tback_ref, material_ref, select_ref,
     mid_ref, sum_out, row_out, col_out, corner_out,
     current, both, strain, spectrum,
 ):
-    select = select_ref[2 * place[0] + place[1]]
     live = sum_ref[:, WIDTH + 1 : WIDTH + 2]
     for index in range(8):
         lanes = slice(256 * index, 256 * (index + 1))
         arrived = jnp.concatenate([ref[:, lanes] for ref in (cpair_ref, cside_ref, dpair_ref, dside_ref)], axis=0)
-        value = jnp.where(live > index, sum_ref[:, lanes] + dot(select, arrived), 0.0)
+        value = jnp.where(live > index, sum_ref[:, lanes] + dot(select_ref[...], arrived), 0.0)
         current[:, lanes] = value
         mid_ref[:, lanes] = value[:OWN]
     mass = sum_ref[:, WIDTH : WIDTH + 1] * (-1.0 / WIDTH)
 
     def emit(index, re, im):
+        masked = jnp.where(live > index, mass, 0.0)
         for part, value in ((0, re), (1, im)):
             lanes = block(index, part)
-            value = mass * value
-            total = 2.0 * current[:OWN, lanes] - own_rows(disp_ref, lanes) + value[:OWN]
+            value = masked * value
+            total = 2.0 * current[:OWN, lanes] - own_ref[:, lanes] + value[:OWN]
             value = value.astype(BF16)
             for c in range(3):
                 for i in range(4):
@@ -427,28 +461,27 @@
     )
 
 
-def last_kernel(blocks_ref, sum_ref, row_ref, col_ref, corner_ref, out_ref):
-    for i in range(4):
-        live = node_column(lambda at: blocks_ref[at[0], at[1]].astype(F32), [(i, n) for n in range(4)])
-        first = lax.broadcasted_iota(jnp.int32, (4, 1), 0) == 0
-        for c in range(3):
-            for index in range(8):
-                lanes = slice(256 * index, 256 * (index + 1))
-                arrived = col_ref[c, i : i + 1, lanes].astype(F32)
-                if i == 0:
-                    arrived = arrived + corner_ref[c, :, lanes].astype(F32)
-                value = sum_ref[c, i, :, lanes] + jnp.where(first, arrived, 0.0)
-                if i == 0:
-                    value = value + row_ref[c, :, lanes].astype(F32)
-                out_ref[c, i, :, lanes] = jnp.where(live > index, value, 0.0)
-
-
-def call(kernel, outs, scratch=(), scalars=0, inputs=0, flops=0):
+def last_kernel(sum_ref, row_ref, col_ref, corner_ref, out_ref):
+    first = lax.broadcasted_iota(jnp.int32, (4, 1), 0) == 0
+    for c in range(3):
+        for i in range(4):
+            arrived = col_ref[c, i : i + 1].astype(F32)
+            if i == 0:
+                arrived = arrived + corner_ref[c].astype(F32)
+            value = sum_ref[c, i] + jnp.where(first, arrived, 0.0)
+            if i == 0:
+                value = value + row_ref[c].astype(F32)
+            out_ref[c, i] = value
+
+
+def call(kernel, outs, scratch=(), scalars=0, inputs=0, flops=0, far=0):
     vmem = pl.BlockSpec(memory_space=pltpu.VMEM)
     return pl.pallas_call(
         kernel,
         out_shape=outs,
-        in_specs=[pl.BlockSpec(memory_space=pltpu.SMEM)] * scalars + [vmem] * inputs,
+        in_specs=[pl.BlockSpec(memory_space=pltpu.HBM)] * far
+        + [pl.BlockSpec(memory_space=pltpu.SMEM)] * scalars
+        + [vmem] * inputs,
         out_specs=jax.tree.map(lambda _: vmem, outs),
         scratch_shapes=list(scratch),
         compiler_params=pltpu.CompilerParams(vmem_limit_bytes=VMEM_LIMIT),
@@ -462,7 +495,7 @@
 
 def solution(mesh):
     bands, layers = mesh.shape["colat"], mesh.shape["depth"]
-    parts, node_of = strain_terms()
+    parts, place_of = strain_terms()
     table, tback = sample_tables()
 
     def shifted(array, by_c, by_d):
@@ -483,22 +516,43 @@
         place = jnp.stack([at_c % 2, at_d % 2, at_c < bands - 1, at_d < layers - 1]).astype(jnp.int32)
         row_face = shape(3, 4, WIDTH + LANES, dtype=BF16)
         point = shape(3, 1, WIDTH + LANES, dtype=BF16)
-        row, col, corner = call(first_kernel, (row_face, row_face, point), scalars=2, inputs=1)(
-            node_blocks, inverse_mass, displacement
-        )
+        row, col, corner = call(
+            first_kernel,
+            (row_face, row_face, point),
+            [
+                pltpu.SMEM((4, 4), jnp.int32),
+                pltpu.SMEM((4, 4), F32),
+                pltpu.VMEM((3, 4, 4, WIDTH), F32),
+                pltpu.SemaphoreType.DMA((3,)),
+            ],
+            far=3,
+        )(node_blocks, inverse_mass, displacement)
         corner = shifted(corner, -1, -1)
         col = shifted(col, 0, -1)
         row = shifted(row, -1, 0)
 
-        factors = jnp.stack(
-            [item.reshape(25) for item in (jac_diag[0], jac_off[0], jac_off[1], jac_diag[1], inv_radius)]
+        operator, back, material, own, free, info, outgoing, column, arrival = call(
+            prepare_kernel,
+            (
+                shape(STRAINS, 2 * NODES, dtype=BF16),
+                shape(2 * NODES, STRAINS, dtype=BF16),
+                shape(RADIX, 56, LANES),
+                shape(OWN, WIDTH),
+                shape(OWN, WIDTH),
+                shape(OWN + 8, LANES),
+                shape(64, NODES, dtype=BF16),
+                shape(32, 64, dtype=BF16),
+                shape(NODES, 64, dtype=BF16),
+            ),
+            [pltpu.VMEM((2, 400, LANES), F32)],
+            scalars=3, inputs=13, flops=10**9,
+        )(
+            place, node_blocks, inverse_mass, displacement, previous,
+            jac_diag.reshape(2, 5, 5), jac_off.reshape(2, 5, 5), inv_radius.reshape(5, 5),
+            lame_l.reshape(400, LANES), lame_m.reshape(400, LANES),
+            jnp.asarray(parts), jnp.asarray(place_of), jnp.asarray(lane_shuffle()),
+            jnp.asarray(outgoing_select()), jnp.asarray(column_select()), jnp.asarray(arrival_select()),
         )
-        spread_factors = jnp.dot(factors, jnp.asarray(node_of.T), precision=lax.Precision.HIGHEST)
-        operator = jnp.sum(spread_factors[:, :, None] * jnp.asarray(parts), axis=0).astype(BF16)
-        back = jnp.sum(spread_factors[:, None, :] * jnp.asarray(parts.transpose(0, 2, 1)), axis=0).astype(BF16)
-        material = call(
-            material_kernel, shape(RADIX, 56, LANES), [pltpu.VMEM((16, 56, LANES), F32)], inputs=3
-        )(lame_l.reshape(5, 5, WIDTH), lame_m.reshape(5, 5, WIDTH), jnp.asarray(lane_shuffle()))
 
         work = [
             pltpu.VMEM((2 * NODES, WIDTH), BF16),
@@ -510,17 +564,12 @@
         total, pair, side, faces = call(
             step_one_kernel,
             (shape(NODES, WIDTH + LANES), tile, tile, shape(32, WIDTH, dtype=BF16)),
-            [pltpu.VMEM((OWN, WIDTH), F32), pltpu.VMEM((32, WIDTH + LANES), F32)] + work,
-            scalars=3, inputs=11, flops=10**9,
-        )(
-            place, node_blocks, inverse_mass, displacement, previous, row, col, corner,
-            *shared, jnp.asarray(outgoing_select()),
-        )
+            [pltpu.VMEM((32, WIDTH + LANES), F32)] + work,
+            inputs=12, flops=10**9,
+        )(own, free, info, row, col, corner, *shared, outgoing)
         cpair = swapped(pair, "colat", 0)
         cside = swapped(side, "colat", 1)
-        pair, side = call(column_kernel, (tile, tile), scalars=1, inputs=4)(
-            place, faces, cpair, cside, jnp.asarray(column_select())
-        )
+        pair, side = call(column_kernel, (tile, tile), inputs=4)(faces, cpair, cside, column)
         dpair = swapped(pair, "depth", 0)
         dside = swapped(side, "depth", 1)
         row_face = shape(3, 4, WIDTH, dtype=BF16)
@@ -531,14 +580,12 @@
                 shape(3, 1, WIDTH, dtype=BF16),
             ),
             [pltpu.VMEM((NODES, WIDTH), F32)] + work,
-            scalars=1, inputs=12, flops=10**9,
-        )(place, displacement, total, cpair, cside, dpair, dside, *shared, jnp.asarray(arrival_select()))
+            inputs=12, flops=10**9,
+        )(own, total, cpair, cside, dpair, dside, *shared, arrival)
         corner = shifted(corner, 1, 1)
         col = shifted(col, 0, 1)
         row = shifted(row, 1, 0)
-        final = call(last_kernel, shape(3, 4, 4, WIDTH), scalars=1, inputs=4)(
-            node_blocks, final, row, col, corner
-        )
+        final = call(last_kernel, shape(3, 4, 4, WIDTH), inputs=4)(final, row, col, corner)
         return middle.reshape(displacement.shape), final
 
     return jax.shard_map(

time: 57.6 us -> 57 us (0.990)
  local copies, waits for them, and re-layouts: 6.8 us -> 11 us
  other arithmetic: 2.3 us -> 0.08 us
  Pallas kernels: 11.9 us -> 10.1 us
  matrix products: 0.88 us -> 0 us
    unnamed x31 -> x43, local copies, waits for them, and re-layouts: 3.99 us -> 10.1 us
    reduce_sum x2 -> x0, other arithmetic: 1.53 us -> none  [the longest x1 1.35 us: per_device(): jnp.sum(spread_factors[:, :, None] * jnp.asarray(parts), axis=0)]
    slice x2 -> x0, local copies, waits for them, and re-layouts: 1.44 us -> none  [the longest x1 0.72 us: per_device(): jac_off[1]]
    pallas_call x1, Pallas kernels: 4.79 us -> 3.38 us  [per_device(): call(step_one_kernel, (shape(NODES, WIDTH + LANES), tile, tile, shape(32,...]
    pallas_call x1, Pallas kernels: 3.53 us -> 2.28 us  [per_device(): call(step_two_kernel, (shape(OWN, WIDTH), shape(3, 4, 4, WIDTH), row_face...]
    pallas_call x4, Pallas kernels: 3.56 us -> 4.48 us  [the longest x1 2.73 us: per_device(): call(prepare_kernel, (shape(STRAINS, 2 * NODES, dtype=BF16), shape(2 * NO...]
    dot_general x1 -> x0, matrix products: 0.88 us -> none  [per_device(): jnp.dot(factors, jnp.asarray(node_of.T), precision=lax.Precision.HIGHEST)]
    unnamed x1 -> x0, other arithmetic: 0.7 us -> none
  transfers between devices with their start and end apart: 10 -> 10, of which waited for: 5 -> 5; matrix products, arithmetic and copies ran while one was open for 13% -> 2% of each run, Pallas kernels for 1% -> 5%
where the time goes in v2:
time: 57 us; the launch traced here: 56.4 us
  waiting for transfers between devices  22.4 us (39%)
  starting transfers between devices  12.1 us (21%)
  local copies, waits for them, and re-layouts  11 us (19%)
  Pallas kernels  10.1 us (18%)
  between operations  0.81 us (1%)
    ppermute x4, waiting for transfers between devices, swapped(): return lax.ppermute(array, axis, pairs)  13.5 us
    ppermute x6, starting transfers between devices, shifted(): return lax.ppermute(array, ('colat', 'depth'), pairs)  10.6 us
    unnamed x43, local copies, waits for them, and re-layouts  10.1 us
    ppermute x6, waiting for transfers between devices, shifted(): return lax.ppermute(array, ('colat', 'depth'), pairs)  8.84 us
    pallas_call x1, Pallas kernels, per_device(): call(step_one_kernel, (shape(NODES, WIDTH + LANES), tile, tile, shape(32,...  3.38 us
    pallas_call x1, Pallas kernels, per_device(): call(prepare_kernel, (shape(STRAINS, 2 * NODES, dtype=BF16), shape(2 * NO...  2.73 us
    pallas_call x1, Pallas kernels, per_device(): call(step_two_kernel, (shape(OWN, WIDTH), shape(3, 4, 4, WIDTH), row_face...  2.28 us
    ppermute x4, starting transfers between devices, swapped(): return lax.ppermute(array, axis, pairs)  1.42 us
  transfers between devices with their start and end apart: 10, of which 5 were waited for; matrix products, arithmetic and copies ran while one was open for 2% of the time, Pallas kernels for 5%

profile of v2, /device:TPU:0, one launch (start us, length us, event | category | flops | bytes accessed | tf_op | source)
XLA Modules:
  0.0 56.4 jit_solution(256077800346722403)
XLA Ops:
  0.6 0.0 copy-start.2
  0.6 1.0 %copy-done.2 = f32[3,4,4,2048]{3,2,1,0:T(4,128)S(1)} copy-done((f32[3,4,4,2048]{3,2,1,0:T(4,128)S(1)}, f32[3,4,4,2048]{3,2,1,0:T(4,128)}, u32[]{:S(2)}) %copy-start.2) | copy-done | bytes 393240
  1.6 0.7 %copy-done.4 = s32[4,4]{1,0:T(4,128)S(1)} copy-done((s32[4,4]{1,0:T(4,128)S(1)}, s32[4,4]{1,0:T(4,128)}, u32[]{:S(2)}) %copy-start.4) | copy-done | bytes 88
  2.3 0.7 %copy-done.6 = f32[4,4]{1,0:T(4,128)S(1)} copy-done((f32[4,4]{1,0:T(4,128)S(1)}, f32[4,4]{1,0:T(4,128)}, u32[]{:S(2)}) %copy-start.6) | copy-done | bytes 88
  3.0 0.7 %shard_map.177 = (bf16[3,4,2176]{2,1,0:T(4,128)(2,1)S(1)}, bf16[3,4,2176]{2,1,0:T(4,128)(2,1)S(1)}, bf16[3,1,2176]{2,1,0:T(2,128)(2,1)S(1)}) custom-call(s32[4,4]{1,0:T(4,128)S(1)} %copy-done.4, f32[4,4]{1,0:T(4,128)S(1)} %copy-done.6, f32[3,4,4,2048]{3,2,1,0:T(4,128)S(1)} %copy-done.2), custom_call_target="tpu_custom_call" | custom-call | bytes 1048576 | tf_op jit(solution)/shard_map/pallas_call | solution.py:519
  3.7 0.0 copy-start.13
  3.7 8.3 %collective-permute-start.2 = (bf16[3,1,2176]{2,1,0:T(2,128)(2,1)S(1)}, bf16[3,1,2176]{2,1,0:T(2,128)(2,1)S(1)}, u32[]{:S(2)}, u32[]{:S(2)}) collective-permute-start(bf16[3,1,2176]{2,1,0:T(2,128)(2,1)S(1)} %get-tuple-element.30), channel_id=1, source_target_pairs={{0,127},{1,120},{2,121},{3,122},{4,123},{5,124},{6,125},{7,126},{8... | collective-permute-start | bytes 39176 | tf_op jit(solution)/shard_map/ppermute | solution.py:507
  12.0 1.1 %collective-permute-start = (bf16[3,4,2176]{2,1,0:T(4,128)(2,1)S(1)}, bf16[3,4,2176]{2,1,0:T(4,128)(2,1)S(1)}, u32[]{:S(2)}, u32[]{:S(2)}) collective-permute-start(bf16[3,4,2176]{2,1,0:T(4,128)(2,1)S(1)} %get-tuple-element.28), channel_id=1, source_target_pairs={{0,120},{1,121},{2,122},{3,123},{4,124},{5,125},{6,126},{7,127},{8... | collective-permute-start | bytes 156680 | tf_op jit(solution)/shard_map/ppermute | solution.py:507
  13.1 1.0 %collective-permute-start.1 = (bf16[3,4,2176]{2,1,0:T(4,128)(2,1)S(1)}, bf16[3,4,2176]{2,1,0:T(4,128)(2,1)S(1)}, u32[]{:S(2)}, u32[]{:S(2)}) collective-permute-start(bf16[3,4,2176]{2,1,0:T(4,128)(2,1)S(1)} %get-tuple-element.29), channel_id=1, source_target_pairs={{0,7},{1,0},{2,1},{3,2},{4,3},{5,4},{6,5},{7,6},{8,15},{9,8},{10,9... | collective-permute-start | bytes 156680 | tf_op jit(solution)/shard_map/ppermute | solution.py:507
  14.2 0.0 copy-done.19
  14.2 0.0 copy-done.17
  14.2 0.0 copy-start.14
  14.2 0.6 %copy-done.18 = f32[2,1,5,1,5]{4,3,2,1,0:T(1,128)S(1)} copy-done((f32[2,1,5,1,5]{4,3,2,1,0:T(1,128)S(1)}, f32[2,1,5,1,5]{4,3,2,1,0:T(1,128)}, u32[]{:S(2)}) %copy-start.18) | copy-done | bytes 224
  14.9 0.1 pad_add_fusion.place
  14.9 0.0 copy-done.3
  14.9 0.0 copy-done.13
  15.0 0.6 %copy-done.7 = f32[4,4]{1,0:T(4,128)S(1)} copy-done((f32[4,4]{1,0:T(4,128)S(1)}, f32[4,4]{1,0:T(4,128)}, u32[]{:S(2)}) %copy-start.7) | copy-done | bytes 88
  15.5 0.1 copy-done.5
  15.6 1.0 %copy-done.8 = f32[3,4,4,2048]{3,2,1,0:T(4,128)S(1)} copy-done((f32[3,4,4,2048]{3,2,1,0:T(4,128)S(1)}, f32[3,4,4,2048]{3,2,1,0:T(4,128)}, u32[]{:S(2)}) %copy-start.8) | copy-done | bytes 393240
  16.6 0.9 %copy-done.9 = f32[1,5,1,5,2048]{4,2,3,1,0:T(1,128)S(1)} copy-done((f32[1,5,1,5,2048]{4,2,3,1,0:T(1,128)S(1)}, f32[1,5,1,5,2048]{4,2,3,1,0:T(1,128)}, u32[]{:S(2)}) %copy-start.9) | copy-done | bytes 204824
  17.6 0.9 %copy-done.10 = f32[1,5,1,5,2048]{4,2,3,1,0:T(1,128)S(1)} copy-done((f32[1,5,1,5,2048]{4,2,3,1,0:T(1,128)S(1)}, f32[1,5,1,5,2048]{4,2,3,1,0:T(1,128)}, u32[]{:S(2)}) %copy-start.10) | copy-done | bytes 204824
  18.5 1.1 %copy-done.11 = f32[5,152,160]{2,1,0:T(8,128)S(1)} copy-done((f32[5,152,160]{2,1,0:T(8,128)S(1)}, f32[5,152,160]{2,1,0:T(8,128)}, u32[]{:S(2)}) %copy-start.11) | copy-done | bytes 486424
  19.6 0.9 %copy-done.12 = f32[2,152,5]{2,1,0:T(8,128)S(1)} copy-done((f32[2,152,5]{2,1,0:T(8,128)S(1)}, f32[2,152,5]{2,1,0:T(8,128)}, u32[]{:S(2)}) %copy-start.12) | copy-done | bytes 6104
  20.5 0.8 %copy-done.15 = bf16[2,64,80]{2,1,0:T(8,128)(2,1)S(1)} copy-done((bf16[2,64,80]{2,1,0:T(8,128)(2,1)S(1)}, bf16[2,64,80]{2,1,0:T(8,128)(2,1)}, u32[]{:S(2)}) %copy-start.15) | copy-done | bytes 20504
  21.3 0.8 %copy-done.16 = bf16[128,128]{1,0:T(8,128)(2,1)S(1)} copy-done((bf16[128,128]{1,0:T(8,128)(2,1)S(1)}, bf16[128,128]{1,0:T(8,128)(2,1)}, u32[]{:S(2)}) %copy-start.16) | copy-done | bytes 32792
  22.0 2.7 %shard_map.176 = (bf16[152,160]{1,0:T(8,128)(2,1)S(1)}, bf16[160,152]{1,0:T(8,128)(2,1)S(1)}, f32[16,56,128]{2,1,0:T(8,128)S(1)}, f32[48,2048]{1,0:T(8,128)S(1)}...) custom-call(s32[4]{0:T(128)S(1)} %pad_add_fusion.place, ...), custom_call_target="tpu_custom_call" | custom-call | flops 1000000000 | bytes 1048576 | tf_op jit(solution)/shard_map/pallas_call | solution.py:534
  24.8 0.0 collective-permute-done.2.corner_ref
  24.8 0.0 collective-permute-done.row_ref
  24.8 0.0 collective-permute-done.1.col_ref
  24.8 3.4 %shard_map.178 = (f32[80,2176]{1,0:T(8,128)S(1)}, bf16[16,2048]{1,0:T(8,128)(2,1)S(1)}, bf16[16,2048]{1,0:T(8,128)(2,1)S(1)}, bf16[32,2048]{1,0:T(8,128)(2,1)S(1)}) custom-call(f32[48,2048]{1,0:T(8,128)S(1)} %get-tuple-element.25.own_ref, f32[48,2048]{1,0:T(8,128)S(1)} %get-tuple-element.26.free_ref, f32[56,128]{1,0:T(8,128)S(1)} %get-tuple-element.27.info_ref, ...), custom_call_target="tpu_custom_call" | custom-call | flops 1000000000 | bytes 1048576 | tf_op jit(solution)/shard_map/pallas_call | solution.py:564
  28.2 0.1 collective-permute-start.3
  28.3 0.2 collective-permute-start.4
  28.5 1.0 %collective-permute-done.3.pair_ref.cpair_ref = bf16[16,2048]{1,0:T(8,128)(2,1)S(1)} collective-permute-done((bf16[16,2048]{1,0:T(8,128)(2,1)S(1)}, bf16[16,2048]{1,0:T(8,128)(2,1)S(1)}, u32[]{:S(2)}, u32[]{:S(2)}) %collective-permute-start.3) | collective-permute-done | bytes 65568 | tf_op jit(solution)/shard_map/ppermute | solution.py:512
  29.5 4.6 %collective-permute-done.4.side_ref.cside_ref = bf16[16,2048]{1,0:T(8,128)(2,1)S(1)} collective-permute-done((bf16[16,2048]{1,0:T(8,128)(2,1)S(1)}, bf16[16,2048]{1,0:T(8,128)(2,1)S(1)}, u32[]{:S(2)}, u32[]{:S(2)}) %collective-permute-start.4) | collective-permute-done | bytes 65568 | tf_op jit(solution)/shard_map/ppermute | solution.py:512
  34.2 0.2 shard_map.179
  34.4 1.1 %collective-permute-start.5 = (bf16[16,2048]{1,0:T(8,128)(2,1)S(1)}, bf16[16,2048]{1,0:T(8,128)(2,1)S(1)}, u32[]{:S(2)}, u32[]{:S(2)}) collective-permute-start(bf16[16,2048]{1,0:T(8,128)(2,1)S(1)} %get-tuple-element.40), channel_id=1, source_target_pairs={{0,1},{1,0},{2,3},{3,2},{4,5},{5,4},{6,7},{7,6},{8,9},{9,8},{10,11... | collective-permute-start | bytes 196616 | tf_op jit(solution)/shard_map/ppermute | solution.py:512
  35.4 0.0 collective-permute-start.6
  35.4 3.2 %collective-permute-done.5.dpair_ref = bf16[16,2048]{1,0:T(8,128)(2,1)S(1)} collective-permute-done((bf16[16,2048]{1,0:T(8,128)(2,1)S(1)}, bf16[16,2048]{1,0:T(8,128)(2,1)S(1)}, u32[]{:S(2)}, u32[]{:S(2)}) %collective-permute-start.5) | collective-permute-done | bytes 65568 | tf_op jit(solution)/shard_map/ppermute | solution.py:512
  38.7 4.6 %collective-permute-done.6.dside_ref = bf16[16,2048]{1,0:T(8,128)(2,1)S(1)} collective-permute-done((bf16[16,2048]{1,0:T(8,128)(2,1)S(1)}, bf16[16,2048]{1,0:T(8,128)(2,1)S(1)}, u32[]{:S(2)}, u32[]{:S(2)}) %collective-permute-start.6) | collective-permute-done | bytes 65568 | tf_op jit(solution)/shard_map/ppermute | solution.py:512
  43.3 2.3 %shard_map.180 = (f32[48,2048]{1,0:T(8,128)S(1)}, f32[3,4,4,2048]{3,2,1,0:T(4,128)S(1)}, bf16[3,4,2048]{2,1,0:T(4,128)(2,1)S(1)}, bf16[3,4,2048]{2,1,0:T(4,128)(2,1)S(1)}, bf16[3,1,2048]{2,1,0:T(2,128)(2,1)S(1)}) custom-call(f32[48,2048]{1,0:T(8,128)S(1)} %get-tuple-element.25.own_ref, f32[80,2176]{1,0:T(8,128)S(1)} %get-tuple-element.35.sum_ref, ...), custom_call_target="tpu_custom_call" | custom-call | flops 1000000000 | bytes 1048576 | tf_op jit(solution)/shard_map/pallas_call | solution.py:576
  45.6 0.1 collective-permute-start.7
  45.7 0.1 collective-permute-start.8
  45.8 0.1 collective-permute-start.9
  45.9 0.9 %reshape.27 = f32[3,4,4,2048]{3,2,1,0:T(4,128)} reshape(f32[48,2048]{1,0:T(8,128)S(1)} %get-tuple-element.43) | data formatting | bytes 786432 | tf_op jit(solution)/shard_map/reshape | solution.py:589
  46.7 8.8 %collective-permute-done.9.corner_ref = bf16[3,1,2048]{2,1,0:T(2,128)(2,1)S(1)} collective-permute-done((bf16[3,1,2048]{2,1,0:T(2,128)(2,1)S(1)}, bf16[3,1,2048]{2,1,0:T(2,128)(2,1)S(1)}, u32[]{:S(2)}, u32[]{:S(2)}) %collective-permute-start.9) | collective-permute-done | bytes 12320 | tf_op jit(solution)/shard_map/ppermute | solution.py:507
  55.6 0.0 collective-permute-done.7.row_ref
  55.6 0.0 collective-permute-done.8.col_ref
  55.6 0.9 %shard_map.181 = f32[3,4,4,2048]{3,2,1,0:T(4,128)} custom-call(f32[3,4,4,2048]{3,2,1,0:T(4,128)S(1)} %get-tuple-element.44.sum_ref, bf16[3,4,2048]{2,1,0:T(4,128)(2,1)S(1)} %collective-permute-done.7.row_ref, bf16[3,4,2048]{2,1,0:T(4,128)(2,1)S(1)} %collective-permute-done.8.col_ref, bf16[3,1,2048]{2,1,0:T(2,128)(2,1)S(1)} %collective-permute-done.9.corner_ref), custom_call_target="tpu_custom_call" | custom-call | bytes 1048576 | tf_op jit(solution)/shard_map/pallas_call | solution.py:588
  (25 shorter events, 0.1 us)
Async XLA Ops:
  0.6 1.0 %copy-start.2 = (f32[3,4,4,2048]{3,2,1,0:T(4,128)S(1)}, f32[3,4,4,2048]{3,2,1,0:T(4,128)}, u32[]{:S(2)}) copy-start(f32[3,4,4,2048]{3,2,1,0:T(4,128)} %disp_hbm.1) | copy-start | bytes 1179652
  1.6 0.7 %copy-start.4 = (s32[4,4]{1,0:T(4,128)S(1)}, s32[4,4]{1,0:T(4,128)}, u32[]{:S(2)}) copy-start(s32[4,4]{1,0:T(4,128)} %blocks_hbm.1) | copy-start | bytes 196
  2.3 0.7 %copy-start.6 = (f32[4,4]{1,0:T(4,128)S(1)}, f32[4,4]{1,0:T(4,128)}, u32[]{:S(2)}) copy-start(f32[4,4]{1,0:T(4,128)} %mass_hbm.1) | copy-start | bytes 196
  3.0 11.2 %copy-start.19 = (f32[1,5,1,5]{3,2,1,0:T(1,128)S(1)}, f32[1,5,1,5]{3,2,1,0:T(1,128)}, u32[]{:S(2)}) copy-start(f32[1,5,1,5]{3,2,1,0:T(1,128)} %param.23) | copy-start | bytes 304
  3.0 11.2 %copy-start.17 = (f32[2,1,5,1,5]{4,3,2,1,0:T(1,128)S(1)}, f32[2,1,5,1,5]{4,3,2,1,0:T(1,128)}, u32[]{:S(2)}) copy-start(f32[2,1,5,1,5]{4,3,2,1,0:T(1,128)} %param.21) | copy-start | bytes 604
  3.0 12.0 %copy-start.3 = (f32[3,4,4,2048]{3,2,1,0:T(4,128)S(1)}, f32[3,4,4,2048]{3,2,1,0:T(4,128)}, u32[]{:S(2)}) copy-start(f32[3,4,4,2048]{3,2,1,0:T(4,128)} %disp_hbm.1) | copy-start | bytes 1179652
  3.7 11.2 %copy-start.13 = (bf16[4,80,64]{2,1,0:T(8,128)(2,1)S(1)}, bf16[4,80,64]{2,1,0:T(8,128)(2,1)}, u32[]{:S(2)}) copy-start(bf16[4,80,64]{2,1,0:T(8,128)(2,1)} %constant.51.clone.arrival_ref) | copy-start | bytes 122884
  3.7 21.0 %collective-permute-start.2 = (bf16[3,1,2176]{2,1,0:T(2,128)(2,1)S(1)}, bf16[3,1,2176]{2,1,0:T(2,128)(2,1)S(1)}, u32[]{:S(2)}, u32[]{:S(2)}) collective-permute-start(bf16[3,1,2176]{2,1,0:T(2,128)(2,1)S(1)} %get-tuple-element.30), channel_id=1, source_target_pairs={{0,127},{1,120},{2,121},{3,122},{4,123},{5,124},{6,125},{7,126},{8... | collective-permute-start | bytes 39176 | tf_op jit(solution)/shard_map/ppermute | solution.py:507
  12.0 12.8 %collective-permute-start = (bf16[3,4,2176]{2,1,0:T(4,128)(2,1)S(1)}, bf16[3,4,2176]{2,1,0:T(4,128)(2,1)S(1)}, u32[]{:S(2)}, u32[]{:S(2)}) collective-permute-start(bf16[3,4,2176]{2,1,0:T(4,128)(2,1)S(1)} %get-tuple-element.28), channel_id=1, source_target_pairs={{0,120},{1,121},{2,122},{3,123},{4,124},{5,125},{6,126},{7,127},{8... | collective-permute-start | bytes 156680 | tf_op jit(solution)/shard_map/ppermute | solution.py:507
  13.1 11.7 %collective-permute-start.1 = (bf16[3,4,2176]{2,1,0:T(4,128)(2,1)S(1)}, bf16[3,4,2176]{2,1,0:T(4,128)(2,1)S(1)}, u32[]{:S(2)}, u32[]{:S(2)}) collective-permute-start(bf16[3,4,2176]{2,1,0:T(4,128)(2,1)S(1)} %get-tuple-element.29), channel_id=1, source_target_pairs={{0,7},{1,0},{2,1},{3,2},{4,3},{5,4},{6,5},{7,6},{8,15},{9,8},{10,9... | collective-permute-start | bytes 156680 | tf_op jit(solution)/shard_map/ppermute | solution.py:507
  14.2 0.7 %copy-start.18 = (f32[2,1,5,1,5]{4,3,2,1,0:T(1,128)S(1)}, f32[2,1,5,1,5]{4,3,2,1,0:T(1,128)}, u32[]{:S(2)}) copy-start(f32[2,1,5,1,5]{4,3,2,1,0:T(1,128)} %param.22) | copy-start | bytes 604
  14.2 0.8 %copy-start.14 = (bf16[4,32,64]{2,1,0:T(8,128)(2,1)S(1)}, bf16[4,32,64]{2,1,0:T(8,128)(2,1)}, u32[]{:S(2)}) copy-start(bf16[4,32,64]{2,1,0:T(8,128)(2,1)} %constant.50.clone.column_ref) | copy-start | bytes 49156
  14.9 0.7 %copy-start.7 = (f32[4,4]{1,0:T(4,128)S(1)}, f32[4,4]{1,0:T(4,128)}, u32[]{:S(2)}) copy-start(f32[4,4]{1,0:T(4,128)} %mass_hbm.1) | copy-start | bytes 196
  14.9 0.7 %copy-start.5 = (s32[4,4]{1,0:T(4,128)S(1)}, s32[4,4]{1,0:T(4,128)}, u32[]{:S(2)}) copy-start(s32[4,4]{1,0:T(4,128)} %blocks_hbm.1) | copy-start | bytes 196
  15.6 1.0 %copy-start.8 = (f32[3,4,4,2048]{3,2,1,0:T(4,128)S(1)}, f32[3,4,4,2048]{3,2,1,0:T(4,128)}, u32[]{:S(2)}) copy-start(f32[3,4,4,2048]{3,2,1,0:T(4,128)} %prev_ref.1) | copy-start | bytes 1179652
  16.6 0.9 %copy-start.9 = (f32[1,5,1,5,2048]{4,2,3,1,0:T(1,128)S(1)}, f32[1,5,1,5,2048]{4,2,3,1,0:T(1,128)}, u32[]{:S(2)}) copy-start(f32[1,5,1,5,2048]{4,2,3,1,0:T(1,128)} %param.24) | copy-start | bytes 614404
  17.6 0.9 %copy-start.10 = (f32[1,5,1,5,2048]{4,2,3,1,0:T(1,128)S(1)}, f32[1,5,1,5,2048]{4,2,3,1,0:T(1,128)}, u32[]{:S(2)}) copy-start(f32[1,5,1,5,2048]{4,2,3,1,0:T(1,128)} %param.25) | copy-start | bytes 614404
  18.5 1.1 %copy-start.11 = (f32[5,152,160]{2,1,0:T(8,128)S(1)}, f32[5,152,160]{2,1,0:T(8,128)}, u32[]{:S(2)}) copy-start(f32[5,152,160]{2,1,0:T(8,128)} %constant.46.clone.parts_ref) | copy-start | bytes 1459204
  19.6 0.9 %copy-start.12 = (f32[2,152,5]{2,1,0:T(8,128)S(1)}, f32[2,152,5]{2,1,0:T(8,128)}, u32[]{:S(2)}) copy-start(f32[2,152,5]{2,1,0:T(8,128)} %constant.47.clone.place_of_ref) | copy-start | bytes 18244
  20.5 0.8 %copy-start.15 = (bf16[2,64,80]{2,1,0:T(8,128)(2,1)S(1)}, bf16[2,64,80]{2,1,0:T(8,128)(2,1)}, u32[]{:S(2)}) copy-start(bf16[2,64,80]{2,1,0:T(8,128)(2,1)} %constant.49.clone.outgoing_ref) | copy-start | bytes 61444
  21.3 0.8 %copy-start.16 = (bf16[128,128]{1,0:T(8,128)(2,1)S(1)}, bf16[128,128]{1,0:T(8,128)(2,1)}, u32[]{:S(2)}) copy-start(bf16[128,128]{1,0:T(8,128)(2,1)} %constant.48.clone.shuffle_ref) | copy-start | bytes 98308
  22.0 2.8 %copy-start = (bf16[16,128,256]{2,1,0:T(8,128)(2,1)S(1)}, bf16[16,128,256]{2,1,0:T(8,128)(2,1)}, u32[]{:S(2)}) copy-start(bf16[16,128,256]{2,1,0:T(8,128)(2,1)} %constant.53.clone.tback_ref) | copy-start | bytes 3145732
  22.0 2.8 %copy-start.1 = (bf16[16,256,128]{2,1,0:T(8,128)(2,1)S(1)}, bf16[16,256,128]{2,1,0:T(8,128)(2,1)}, u32[]{:S(2)}) copy-start(bf16[16,256,128]{2,1,0:T(8,128)(2,1)} %constant.52.clone.table_ref) | copy-start | bytes 3145732
  28.2 1.3 %collective-permute-start.3 = (bf16[16,2048]{1,0:T(8,128)(2,1)S(1)}, bf16[16,2048]{1,0:T(8,128)(2,1)S(1)}, u32[]{:S(2)}, u32[]{:S(2)}) collective-permute-start(bf16[16,2048]{1,0:T(8,128)(2,1)S(1)} %get-tuple-element.36), channel_id=1, source_target_pairs={{0,8},{8,0},{16,24},{24,16},{32,40},{40,32},{48,56},{56,48},{64,72... | collective-permute-start | bytes 196616 | tf_op jit(solution)/shard_map/ppermute | solution.py:512
  28.3 5.9 %collective-permute-start.4 = (bf16[16,2048]{1,0:T(8,128)(2,1)S(1)}, bf16[16,2048]{1,0:T(8,128)(2,1)S(1)}, u32[]{:S(2)}, u32[]{:S(2)}) collective-permute-start(bf16[16,2048]{1,0:T(8,128)(2,1)S(1)} %get-tuple-element.37), channel_id=1, source_target_pairs={{0,120},{8,16},{16,8},{24,32},{32,24},{40,48},{48,40},{56,64},{64,... | collective-permute-start | bytes 196616 | tf_op jit(solution)/shard_map/ppermute | solution.py:512
  34.4 4.3 %collective-permute-start.5 = (bf16[16,2048]{1,0:T(8,128)(2,1)S(1)}, bf16[16,2048]{1,0:T(8,128)(2,1)S(1)}, u32[]{:S(2)}, u32[]{:S(2)}) collective-permute-start(bf16[16,2048]{1,0:T(8,128)(2,1)S(1)} %get-tuple-element.40), channel_id=1, source_target_pairs={{0,1},{1,0},{2,3},{3,2},{4,5},{5,4},{6,7},{7,6},{8,9},{9,8},{10,11... | collective-permute-start | bytes 196616 | tf_op jit(solution)/shard_map/ppermute | solution.py:512
  35.4 7.9 %collective-permute-start.6 = (bf16[16,2048]{1,0:T(8,128)(2,1)S(1)}, bf16[16,2048]{1,0:T(8,128)(2,1)S(1)}, u32[]{:S(2)}, u32[]{:S(2)}) collective-permute-start(bf16[16,2048]{1,0:T(8,128)(2,1)S(1)} %get-tuple-element.41), channel_id=1, source_target_pairs={{0,7},{1,2},{2,1},{3,4},{4,3},{5,6},{6,5},{7,0},{8,15},{9,10},{10,... | collective-permute-start | bytes 196616 | tf_op jit(solution)/shard_map/ppermute | solution.py:512
  45.6 9.9 %collective-permute-start.7 = (bf16[3,4,2048]{2,1,0:T(4,128)(2,1)S(1)}, bf16[3,4,2048]{2,1,0:T(4,128)(2,1)S(1)}, u32[]{:S(2)}, u32[]{:S(2)}) collective-permute-start(bf16[3,4,2048]{2,1,0:T(4,128)(2,1)S(1)} %get-tuple-element.45), channel_id=1, source_target_pairs={{0,8},{1,9},{2,10},{3,11},{4,12},{5,13},{6,14},{7,15},{8,16},{9,17... | collective-permute-start | bytes 147464 | tf_op jit(solution)/shard_map/ppermute | solution.py:507
  45.7 9.9 %collective-permute-start.8 = (bf16[3,4,2048]{2,1,0:T(4,128)(2,1)S(1)}, bf16[3,4,2048]{2,1,0:T(4,128)(2,1)S(1)}, u32[]{:S(2)}, u32[]{:S(2)}) collective-permute-start(bf16[3,4,2048]{2,1,0:T(4,128)(2,1)S(1)} %get-tuple-element.46), channel_id=1, source_target_pairs={{0,1},{1,2},{2,3},{3,4},{4,5},{5,6},{6,7},{7,0},{8,9},{9,10},{10,1... | collective-permute-start | bytes 147464 | tf_op jit(solution)/shard_map/ppermute | solution.py:507
  45.8 9.8 %collective-permute-start.9 = (bf16[3,1,2048]{2,1,0:T(2,128)(2,1)S(1)}, bf16[3,1,2048]{2,1,0:T(2,128)(2,1)S(1)}, u32[]{:S(2)}, u32[]{:S(2)}) collective-permute-start(bf16[3,1,2048]{2,1,0:T(2,128)(2,1)S(1)} %get-tuple-element.47), channel_id=1, source_target_pairs={{0,9},{1,10},{2,11},{3,12},{4,13},{5,14},{6,15},{7,8},{8,17},{9,18... | collective-permute-start | bytes 36872 | tf_op jit(solution)/shard_map/ppermute | solution.py:507

commit v3 on v2

--- a/solution.py
+++ b/solution.py
@@ -474,17 +474,17 @@
             out_ref[c, i] = value
 
 
-def call(kernel, outs, scratch=(), scalars=0, inputs=0, flops=0, far=0):
-    vmem = pl.BlockSpec(memory_space=pltpu.VMEM)
+def call(kernel, outs, scratch=(), scalars=0, inputs=0, flops=0, far=0, vmem=VMEM_LIMIT):
+    near = pl.BlockSpec(memory_space=pltpu.VMEM)
     return pl.pallas_call(
         kernel,
         out_shape=outs,
         in_specs=[pl.BlockSpec(memory_space=pltpu.HBM)] * far
         + [pl.BlockSpec(memory_space=pltpu.SMEM)] * scalars
-        + [vmem] * inputs,
-        out_specs=jax.tree.map(lambda _: vmem, outs),
+        + [near] * inputs,
+        out_specs=jax.tree.map(lambda _: near, outs),
         scratch_shapes=list(scratch),
-        compiler_params=pltpu.CompilerParams(vmem_limit_bytes=VMEM_LIMIT),
+        compiler_params=pltpu.CompilerParams(vmem_limit_bytes=vmem),
         cost_estimate=pl.CostEstimate(flops=flops, bytes_accessed=1 << 20, transcendentals=0),
     )
 
@@ -525,7 +525,7 @@
                 pltpu.VMEM((3, 4, 4, WIDTH), F32),
                 pltpu.SemaphoreType.DMA((3,)),
             ],
-            far=3,
+            far=3, flops=2 * 10**11, vmem=62 * 1024 * 1024,
         )(node_blocks, inverse_mass, displacement)
         corner = shifted(corner, -1, -1)
         col = shifted(col, 0, -1)

time: 57 us -> 52.5 us (0.921)
  local copies, waits for them, and re-layouts: 11 us -> 5.37 us
  Pallas kernels: 10.1 us -> 11.3 us
    unnamed x43 -> x33, local copies, waits for them, and re-layouts: 10.1 us -> 4.51 us
    pallas_call x1, Pallas kernels: 0.72 us -> 1.87 us  [per_device(): call(first_kernel, (row_face, row_face, point), [pltpu.SMEM((4, 4), jnp.i...]
  transfers between devices with their start and end apart: 10 -> 10, of which waited for: 5 -> 5; matrix products, arithmetic and copies ran while one was open for 2% -> 4% of each run, Pallas kernels for 5% -> 5%
where the time goes in v3:
time: 52.5 us; the launch traced here: 52 us
  waiting for transfers between devices  22.4 us (43%)
  starting transfers between devices  12.1 us (23%)
  Pallas kernels  11.3 us (22%)
  local copies, waits for them, and re-layouts  5.37 us (10%)
  between operations  0.87 us (2%)
    ppermute x4, waiting for transfers between devices, swapped(): return lax.ppermute(array, axis, pairs)  13.5 us
    ppermute x6, starting transfers between devices, shifted(): return lax.ppermute(array, ('colat', 'depth'), pairs)  10.6 us
    ppermute x6, waiting for transfers between devices, shifted(): return lax.ppermute(array, ('colat', 'depth'), pairs)  8.84 us
    unnamed x33, local copies, waits for them, and re-layouts  4.51 us
    pallas_call x1, Pallas kernels, per_device(): call(step_one_kernel, (shape(NODES, WIDTH + LANES), tile, tile, shape(32,...  3.37 us
    pallas_call x1, Pallas kernels, per_device(): call(prepare_kernel, (shape(STRAINS, 2 * NODES, dtype=BF16), shape(2 * NO...  2.73 us
    pallas_call x1, Pallas kernels, per_device(): call(step_two_kernel, (shape(OWN, WIDTH), shape(3, 4, 4, WIDTH), row_face...  2.29 us
    pallas_call x1, Pallas kernels, per_device(): call(first_kernel, (row_face, row_face, point), [pltpu.SMEM((4, 4), jnp.i...  1.87 us
  transfers between devices with their start and end apart: 10, of which 5 were waited for; matrix products, arithmetic and copies ran while one was open for 4% of the time, Pallas kernels for 5%

profile of v3, /device:TPU:0, one launch (start us, length us, event | category | flops | bytes accessed | tf_op | source)
XLA Modules:
  0.0 52.0 jit_solution(7715554739808787238)
XLA Ops:
  0.6 0.0 copy-start.2
  0.6 0.0 copy-start.3
  0.7 0.0 copy-start.4
  0.7 0.0 copy-start.5
  0.7 0.0 copy-start.8
  0.7 1.9 %shard_map.177 = (bf16[3,4,2176]{2,1,0:T(4,128)(2,1)}, bf16[3,4,2176]{2,1,0:T(4,128)(2,1)}, bf16[3,1,2176]{2,1,0:T(2,128)(2,1)}) custom-call(s32[4,4]{1,0:T(4,128)} %blocks_hbm.1, f32[4,4]{1,0:T(4,128)} %mass_hbm.1, f32[3,4,4,2048]{3,2,1,0:T(4,128)} %disp_hbm.1), custom_call_target="tpu_custom_call" | custom-call | flops 199999995904 | bytes 1048576 | tf_op jit(solution)/shard_map/pallas_call | solution.py:519
  2.6 0.0 copy-start.10
  2.6 8.3 %collective-permute-start.2 = (bf16[3,1,2176]{2,1,0:T(2,128)(2,1)}, bf16[3,1,2176]{2,1,0:T(2,128)(2,1)S(1)}, u32[]{:S(2)}, u32[]{:S(2)}) collective-permute-start(bf16[3,1,2176]{2,1,0:T(2,128)(2,1)} %get-tuple-element.30), channel_id=1, source_target_pairs={{0,127},{1,120},{2,121},{3,122},{4,123},{5,124},{6,125},{7,126},{8... | collective-permute-start | bytes 39176 | tf_op jit(solution)/shard_map/ppermute | solution.py:507
  10.8 1.1 %collective-permute-start = (bf16[3,4,2176]{2,1,0:T(4,128)(2,1)}, bf16[3,4,2176]{2,1,0:T(4,128)(2,1)S(1)}, u32[]{:S(2)}, u32[]{:S(2)}) collective-permute-start(bf16[3,4,2176]{2,1,0:T(4,128)(2,1)} %get-tuple-element.28), channel_id=1, source_target_pairs={{0,120},{1,121},{2,122},{3,123},{4,124},{5,125},{6,126},{7,127},{8... | collective-permute-start | bytes 156680 | tf_op jit(solution)/shard_map/ppermute | solution.py:507
  12.0 1.0 %collective-permute-start.1 = (bf16[3,4,2176]{2,1,0:T(4,128)(2,1)}, bf16[3,4,2176]{2,1,0:T(4,128)(2,1)S(1)}, u32[]{:S(2)}, u32[]{:S(2)}) collective-permute-start(bf16[3,4,2176]{2,1,0:T(4,128)(2,1)} %get-tuple-element.29), channel_id=1, source_target_pairs={{0,7},{1,0},{2,1},{3,2},{4,3},{5,4},{6,5},{7,6},{8,15},{9,8},{10,9... | collective-permute-start | bytes 156680 | tf_op jit(solution)/shard_map/ppermute | solution.py:507
  13.0 0.7 %copy.29 = f32[1,5,1,5]{3,1,2,0:T(8,128)S(1)} copy(f32[1,5,1,5]{3,2,1,0:T(1,128)} %param.23) | data formatting | bytes 200
  13.7 0.7 %copy.28 = f32[2,1,5,1,5]{4,0,2,3,1:T(2,128)S(1)} copy(f32[2,1,5,1,5]{4,3,2,1,0:T(1,128)} %param.21) | data formatting | bytes 400 | tf_op args[4]
  14.4 0.1 pad_add_fusion.place
  14.5 0.0 copy-done.2
  14.5 0.0 copy-done.3
  14.5 0.0 copy-done.4
  14.5 0.0 copy-done.5
  14.6 0.0 copy-done.8
  14.6 0.0 copy-done.10
  14.6 0.6 %copy-done.11 = bf16[4,32,64]{2,1,0:T(8,128)(2,1)S(1)} copy-done((bf16[4,32,64]{2,1,0:T(8,128)(2,1)S(1)}, bf16[4,32,64]{2,1,0:T(8,128)(2,1)}, u32[]{:S(2)}) %copy-start.11) | copy-done | bytes 16408
  15.1 0.1 copy-done.7
  15.2 0.0 copy-done.6
  15.2 0.9 %copy-done.9 = f32[2,152,5]{2,1,0:T(8,128)S(1)} copy-done((f32[2,152,5]{2,1,0:T(8,128)S(1)}, f32[2,152,5]{2,1,0:T(8,128)}, u32[]{:S(2)}) %copy-start.9) | copy-done | bytes 6104
  16.1 0.8 %copy-done.12 = bf16[2,64,80]{2,1,0:T(8,128)(2,1)S(1)} copy-done((bf16[2,64,80]{2,1,0:T(8,128)(2,1)S(1)}, bf16[2,64,80]{2,1,0:T(8,128)(2,1)}, u32[]{:S(2)}) %copy-start.12) | copy-done | bytes 20504
  16.9 0.8 %copy-done.13 = bf16[128,128]{1,0:T(8,128)(2,1)S(1)} copy-done((bf16[128,128]{1,0:T(8,128)(2,1)S(1)}, bf16[128,128]{1,0:T(8,128)(2,1)}, u32[]{:S(2)}) %copy-start.13) | copy-done | bytes 32792
  17.7 2.7 %shard_map.176 = (bf16[152,160]{1,0:T(8,128)(2,1)S(1)}, bf16[160,152]{1,0:T(8,128)(2,1)S(1)}, f32[16,56,128]{2,1,0:T(8,128)S(1)}, f32[48,2048]{1,0:T(8,128)S(1)}...) custom-call(s32[4]{0:T(128)S(1)} %pad_add_fusion.place, ...), custom_call_target="tpu_custom_call" | custom-call | flops 1000000000 | bytes 1048576 | tf_op jit(solution)/shard_map/pallas_call | solution.py:534
  20.4 0.0 collective-permute-done.2.corner_ref
  20.4 0.0 collective-permute-done.row_ref
  20.4 0.0 collective-permute-done.1.col_ref
  20.4 3.4 %shard_map.178 = (f32[80,2176]{1,0:T(8,128)S(1)}, bf16[16,2048]{1,0:T(8,128)(2,1)S(1)}, bf16[16,2048]{1,0:T(8,128)(2,1)S(1)}, bf16[32,2048]{1,0:T(8,128)(2,1)S(1)}) custom-call(f32[48,2048]{1,0:T(8,128)S(1)} %get-tuple-element.25.own_ref, f32[48,2048]{1,0:T(8,128)S(1)} %get-tuple-element.26.free_ref, f32[56,128]{1,0:T(8,128)S(1)} %get-tuple-element.27.info_ref, ...), custom_call_target="tpu_custom_call" | custom-call | flops 1000000000 | bytes 1048576 | tf_op jit(solution)/shard_map/pallas_call | solution.py:564
  23.8 0.1 collective-permute-start.3
  23.9 0.2 collective-permute-start.4
  24.1 1.0 %collective-permute-done.3.pair_ref.cpair_ref = bf16[16,2048]{1,0:T(8,128)(2,1)S(1)} collective-permute-done((bf16[16,2048]{1,0:T(8,128)(2,1)S(1)}, bf16[16,2048]{1,0:T(8,128)(2,1)S(1)}, u32[]{:S(2)}, u32[]{:S(2)}) %collective-permute-start.3) | collective-permute-done | bytes 65568 | tf_op jit(solution)/shard_map/ppermute | solution.py:512
  25.1 4.6 %collective-permute-done.4.side_ref.cside_ref = bf16[16,2048]{1,0:T(8,128)(2,1)S(1)} collective-permute-done((bf16[16,2048]{1,0:T(8,128)(2,1)S(1)}, bf16[16,2048]{1,0:T(8,128)(2,1)S(1)}, u32[]{:S(2)}, u32[]{:S(2)}) %collective-permute-start.4) | collective-permute-done | bytes 65568 | tf_op jit(solution)/shard_map/ppermute | solution.py:512
  29.8 0.2 shard_map.179
  30.0 1.1 %collective-permute-start.5 = (bf16[16,2048]{1,0:T(8,128)(2,1)S(1)}, bf16[16,2048]{1,0:T(8,128)(2,1)S(1)}, u32[]{:S(2)}, u32[]{:S(2)}) collective-permute-start(bf16[16,2048]{1,0:T(8,128)(2,1)S(1)} %get-tuple-element.40), channel_id=1, source_target_pairs={{0,1},{1,0},{2,3},{3,2},{4,5},{5,4},{6,7},{7,6},{8,9},{9,8},{10,11... | collective-permute-start | bytes 196616 | tf_op jit(solution)/shard_map/ppermute | solution.py:512
  31.1 0.0 collective-permute-start.6
  31.1 3.2 %collective-permute-done.5.dpair_ref = bf16[16,2048]{1,0:T(8,128)(2,1)S(1)} collective-permute-done((bf16[16,2048]{1,0:T(8,128)(2,1)S(1)}, bf16[16,2048]{1,0:T(8,128)(2,1)S(1)}, u32[]{:S(2)}, u32[]{:S(2)}) %collective-permute-start.5) | collective-permute-done | bytes 65568 | tf_op jit(solution)/shard_map/ppermute | solution.py:512
  34.3 4.6 %collective-permute-done.6.dside_ref = bf16[16,2048]{1,0:T(8,128)(2,1)S(1)} collective-permute-done((bf16[16,2048]{1,0:T(8,128)(2,1)S(1)}, bf16[16,2048]{1,0:T(8,128)(2,1)S(1)}, u32[]{:S(2)}, u32[]{:S(2)}) %collective-permute-start.6) | collective-permute-done | bytes 65568 | tf_op jit(solution)/shard_map/ppermute | solution.py:512
  38.9 2.3 %shard_map.180 = (f32[48,2048]{1,0:T(8,128)S(1)}, f32[3,4,4,2048]{3,2,1,0:T(4,128)S(1)}, bf16[3,4,2048]{2,1,0:T(4,128)(2,1)S(1)}, bf16[3,4,2048]{2,1,0:T(4,128)(2,1)S(1)}, bf16[3,1,2048]{2,1,0:T(2,128)(2,1)S(1)}) custom-call(f32[48,2048]{1,0:T(8,128)S(1)} %get-tuple-element.25.own_ref, f32[80,2176]{1,0:T(8,128)S(1)} %get-tuple-element.35.sum_ref, ...), custom_call_target="tpu_custom_call" | custom-call | flops 1000000000 | bytes 1048576 | tf_op jit(solution)/shard_map/pallas_call | solution.py:576
  41.2 0.1 collective-permute-start.7
  41.3 0.1 collective-permute-start.8
  41.4 0.1 collective-permute-start.9
  41.5 0.9 %reshape.27 = f32[3,4,4,2048]{3,2,1,0:T(4,128)} reshape(f32[48,2048]{1,0:T(8,128)S(1)} %get-tuple-element.43) | data formatting | bytes 786432 | tf_op jit(solution)/shard_map/reshape | solution.py:589
  42.3 8.8 %collective-permute-done.9.corner_ref = bf16[3,1,2048]{2,1,0:T(2,128)(2,1)S(1)} collective-permute-done((bf16[3,1,2048]{2,1,0:T(2,128)(2,1)S(1)}, bf16[3,1,2048]{2,1,0:T(2,128)(2,1)S(1)}, u32[]{:S(2)}, u32[]{:S(2)}) %collective-permute-start.9) | collective-permute-done | bytes 12320 | tf_op jit(solution)/shard_map/ppermute | solution.py:507
  51.2 0.0 collective-permute-done.7.row_ref
  51.2 0.0 collective-permute-done.8.col_ref
  51.2 0.9 %shard_map.181 = f32[3,4,4,2048]{3,2,1,0:T(4,128)} custom-call(f32[3,4,4,2048]{3,2,1,0:T(4,128)S(1)} %get-tuple-element.44.sum_ref, bf16[3,4,2048]{2,1,0:T(4,128)(2,1)S(1)} %collective-permute-done.7.row_ref, bf16[3,4,2048]{2,1,0:T(4,128)(2,1)S(1)} %collective-permute-done.8.col_ref, bf16[3,1,2048]{2,1,0:T(2,128)(2,1)S(1)} %collective-permute-done.9.corner_ref), custom_call_target="tpu_custom_call" | custom-call | bytes 1048576 | tf_op jit(solution)/shard_map/pallas_call | solution.py:588
  (15 shorter events, 0.0 us)
Async XLA Ops:
  0.6 13.9 %copy-start.2 = (f32[3,4,4,2048]{3,2,1,0:T(4,128)S(1)}, f32[3,4,4,2048]{3,2,1,0:T(4,128)}, u32[]{:S(2)}) copy-start(f32[3,4,4,2048]{3,2,1,0:T(4,128)} %disp_hbm.1) | copy-start | bytes 1179652
  0.6 13.9 %copy-start.3 = (f32[3,4,4,2048]{3,2,1,0:T(4,128)S(1)}, f32[3,4,4,2048]{3,2,1,0:T(4,128)}, u32[]{:S(2)}) copy-start(f32[3,4,4,2048]{3,2,1,0:T(4,128)} %prev_ref.1) | copy-start | bytes 1179652
  0.7 13.9 %copy-start.4 = (f32[1,5,1,5,2048]{4,2,3,1,0:T(1,128)S(1)}, f32[1,5,1,5,2048]{4,2,3,1,0:T(1,128)}, u32[]{:S(2)}) copy-start(f32[1,5,1,5,2048]{4,2,3,1,0:T(1,128)} %param.24) | copy-start | bytes 614404
  0.7 13.9 %copy-start.5 = (f32[1,5,1,5,2048]{4,2,3,1,0:T(1,128)S(1)}, f32[1,5,1,5,2048]{4,2,3,1,0:T(1,128)}, u32[]{:S(2)}) copy-start(f32[1,5,1,5,2048]{4,2,3,1,0:T(1,128)} %param.25) | copy-start | bytes 614404
  0.7 13.9 %copy-start.8 = (f32[5,152,160]{2,1,0:T(8,128)S(1)}, f32[5,152,160]{2,1,0:T(8,128)}, u32[]{:S(2)}) copy-start(f32[5,152,160]{2,1,0:T(8,128)} %constant.46.clone.parts_ref) | copy-start | bytes 1459204
  2.6 12.0 %copy-start.10 = (bf16[4,80,64]{2,1,0:T(8,128)(2,1)S(1)}, bf16[4,80,64]{2,1,0:T(8,128)(2,1)}, u32[]{:S(2)}) copy-start(bf16[4,80,64]{2,1,0:T(8,128)(2,1)} %constant.51.clone.arrival_ref) | copy-start | bytes 122884
  2.6 17.8 %collective-permute-start.2 = (bf16[3,1,2176]{2,1,0:T(2,128)(2,1)}, bf16[3,1,2176]{2,1,0:T(2,128)(2,1)S(1)}, u32[]{:S(2)}, u32[]{:S(2)}) collective-permute-start(bf16[3,1,2176]{2,1,0:T(2,128)(2,1)} %get-tuple-element.30), channel_id=1, source_target_pairs={{0,127},{1,120},{2,121},{3,122},{4,123},{5,124},{6,125},{7,126},{8... | collective-permute-start | bytes 39176 | tf_op jit(solution)/shard_map/ppermute | solution.py:507
  10.8 9.5 %collective-permute-start = (bf16[3,4,2176]{2,1,0:T(4,128)(2,1)}, bf16[3,4,2176]{2,1,0:T(4,128)(2,1)S(1)}, u32[]{:S(2)}, u32[]{:S(2)}) collective-permute-start(bf16[3,4,2176]{2,1,0:T(4,128)(2,1)} %get-tuple-element.28), channel_id=1, source_target_pairs={{0,120},{1,121},{2,122},{3,123},{4,124},{5,125},{6,126},{7,127},{8... | collective-permute-start | bytes 156680 | tf_op jit(solution)/shard_map/ppermute | solution.py:507
  12.0 8.4 %collective-permute-start.1 = (bf16[3,4,2176]{2,1,0:T(4,128)(2,1)}, bf16[3,4,2176]{2,1,0:T(4,128)(2,1)S(1)}, u32[]{:S(2)}, u32[]{:S(2)}) collective-permute-start(bf16[3,4,2176]{2,1,0:T(4,128)(2,1)} %get-tuple-element.29), channel_id=1, source_target_pairs={{0,7},{1,0},{2,1},{3,2},{4,3},{5,4},{6,5},{7,6},{8,15},{9,8},{10,9... | collective-permute-start | bytes 156680 | tf_op jit(solution)/shard_map/ppermute | solution.py:507
  13.7 0.7 %copy-start.14 = (f32[2,1,5,1,5]{4,3,2,1,0:T(1,128)S(1)}, f32[2,1,5,1,5]{4,3,2,1,0:T(1,128)}, u32[]{:S(2)}) copy-start(f32[2,1,5,1,5]{4,3,2,1,0:T(1,128)} %param.22) | copy-start | bytes 604
  14.4 0.8 %copy-start.11 = (bf16[4,32,64]{2,1,0:T(8,128)(2,1)S(1)}, bf16[4,32,64]{2,1,0:T(8,128)(2,1)}, u32[]{:S(2)}) copy-start(bf16[4,32,64]{2,1,0:T(8,128)(2,1)} %constant.50.clone.column_ref) | copy-start | bytes 49156
  14.5 0.7 %copy-start.7 = (f32[4,4]{1,0:T(4,128)S(1)}, f32[4,4]{1,0:T(4,128)}, u32[]{:S(2)}) copy-start(f32[4,4]{1,0:T(4,128)} %mass_hbm.1) | copy-start | bytes 196
  14.5 0.7 %copy-start.6 = (s32[4,4]{1,0:T(4,128)S(1)}, s32[4,4]{1,0:T(4,128)}, u32[]{:S(2)}) copy-start(s32[4,4]{1,0:T(4,128)} %blocks_hbm.1) | copy-start | bytes 196
  15.2 0.9 %copy-start.9 = (f32[2,152,5]{2,1,0:T(8,128)S(1)}, f32[2,152,5]{2,1,0:T(8,128)}, u32[]{:S(2)}) copy-start(f32[2,152,5]{2,1,0:T(8,128)} %constant.47.clone.place_of_ref) | copy-start | bytes 18244
  16.1 0.8 %copy-start.12 = (bf16[2,64,80]{2,1,0:T(8,128)(2,1)S(1)}, bf16[2,64,80]{2,1,0:T(8,128)(2,1)}, u32[]{:S(2)}) copy-start(bf16[2,64,80]{2,1,0:T(8,128)(2,1)} %constant.49.clone.outgoing_ref) | copy-start | bytes 61444
  16.9 0.8 %copy-start.13 = (bf16[128,128]{1,0:T(8,128)(2,1)S(1)}, bf16[128,128]{1,0:T(8,128)(2,1)}, u32[]{:S(2)}) copy-start(bf16[128,128]{1,0:T(8,128)(2,1)} %constant.48.clone.shuffle_ref) | copy-start | bytes 98308
  17.7 2.8 %copy-start = (bf16[16,128,256]{2,1,0:T(8,128)(2,1)S(1)}, bf16[16,128,256]{2,1,0:T(8,128)(2,1)}, u32[]{:S(2)}) copy-start(bf16[16,128,256]{2,1,0:T(8,128)(2,1)} %constant.53.clone.tback_ref) | copy-start | bytes 3145732
  17.7 2.8 %copy-start.1 = (bf16[16,256,128]{2,1,0:T(8,128)(2,1)S(1)}, bf16[16,256,128]{2,1,0:T(8,128)(2,1)}, u32[]{:S(2)}) copy-start(bf16[16,256,128]{2,1,0:T(8,128)(2,1)} %constant.52.clone.table_ref) | copy-start | bytes 3145732
  23.8 1.3 %collective-permute-start.3 = (bf16[16,2048]{1,0:T(8,128)(2,1)S(1)}, bf16[16,2048]{1,0:T(8,128)(2,1)S(1)}, u32[]{:S(2)}, u32[]{:S(2)}) collective-permute-start(bf16[16,2048]{1,0:T(8,128)(2,1)S(1)} %get-tuple-element.36), channel_id=1, source_target_pairs={{0,8},{8,0},{16,24},{24,16},{32,40},{40,32},{48,56},{56,48},{64,72... | collective-permute-start | bytes 196616 | tf_op jit(solution)/shard_map/ppermute | solution.py:512
  23.9 5.9 %collective-permute-start.4 = (bf16[16,2048]{1,0:T(8,128)(2,1)S(1)}, bf16[16,2048]{1,0:T(8,128)(2,1)S(1)}, u32[]{:S(2)}, u32[]{:S(2)}) collective-permute-start(bf16[16,2048]{1,0:T(8,128)(2,1)S(1)} %get-tuple-element.37), channel_id=1, source_target_pairs={{0,120},{8,16},{16,8},{24,32},{32,24},{40,48},{48,40},{56,64},{64,... | collective-permute-start | bytes 196616 | tf_op jit(solution)/shard_map/ppermute | solution.py:512
  30.0 4.3 %collective-permute-start.5 = (bf16[16,2048]{1,0:T(8,128)(2,1)S(1)}, bf16[16,2048]{1,0:T(8,128)(2,1)S(1)}, u32[]{:S(2)}, u32[]{:S(2)}) collective-permute-start(bf16[16,2048]{1,0:T(8,128)(2,1)S(1)} %get-tuple-element.40), channel_id=1, source_target_pairs={{0,1},{1,0},{2,3},{3,2},{4,5},{5,4},{6,7},{7,6},{8,9},{9,8},{10,11... | collective-permute-start | bytes 196616 | tf_op jit(solution)/shard_map/ppermute | solution.py:512
  31.1 7.9 %collective-permute-start.6 = (bf16[16,2048]{1,0:T(8,128)(2,1)S(1)}, bf16[16,2048]{1,0:T(8,128)(2,1)S(1)}, u32[]{:S(2)}, u32[]{:S(2)}) collective-permute-start(bf16[16,2048]{1,0:T(8,128)(2,1)S(1)} %get-tuple-element.41), channel_id=1, source_target_pairs={{0,7},{1,2},{2,1},{3,4},{4,3},{5,6},{6,5},{7,0},{8,15},{9,10},{10,... | collective-permute-start | bytes 196616 | tf_op jit(solution)/shard_map/ppermute | solution.py:512
  41.2 9.9 %collective-permute-start.7 = (bf16[3,4,2048]{2,1,0:T(4,128)(2,1)S(1)}, bf16[3,4,2048]{2,1,0:T(4,128)(2,1)S(1)}, u32[]{:S(2)}, u32[]{:S(2)}) collective-permute-start(bf16[3,4,2048]{2,1,0:T(4,128)(2,1)S(1)} %get-tuple-element.45), channel_id=1, source_target_pairs={{0,8},{1,9},{2,10},{3,11},{4,12},{5,13},{6,14},{7,15},{8,16},{9,17... | collective-permute-start | bytes 147464 | tf_op jit(solution)/shard_map/ppermute | solution.py:507
  41.3 9.9 %collective-permute-start.8 = (bf16[3,4,2048]{2,1,0:T(4,128)(2,1)S(1)}, bf16[3,4,2048]{2,1,0:T(4,128)(2,1)S(1)}, u32[]{:S(2)}, u32[]{:S(2)}) collective-permute-start(bf16[3,4,2048]{2,1,0:T(4,128)(2,1)S(1)} %get-tuple-element.46), channel_id=1, source_target_pairs={{0,1},{1,2},{2,3},{3,4},{4,5},{5,6},{6,7},{7,0},{8,9},{9,10},{10,1... | collective-permute-start | bytes 147464 | tf_op jit(solution)/shard_map/ppermute | solution.py:507
  41.4 9.8 %collective-permute-start.9 = (bf16[3,1,2048]{2,1,0:T(2,128)(2,1)S(1)}, bf16[3,1,2048]{2,1,0:T(2,128)(2,1)S(1)}, u32[]{:S(2)}, u32[]{:S(2)}) collective-permute-start(bf16[3,1,2048]{2,1,0:T(2,128)(2,1)S(1)} %get-tuple-element.47), channel_id=1, source_target_pairs={{0,9},{1,10},{2,11},{3,12},{4,13},{5,14},{6,15},{7,8},{8,17},{9,18... | collective-permute-start | bytes 36872 | tf_op jit(solution)/shard_map/ppermute | solution.py:507

commit v4 on v3

--- a/solution.py
+++ b/solution.py
@@ -274,15 +274,34 @@
     return jnp.dot(left, right, preferred_element_type=F32, precision=lax.Precision.HIGHEST)
 
 
+def packed_constants():
+    _, place_of = strain_terms()
+    pieces = {"shuffle": lane_shuffle()[None], "place": place_of, "outgoing": outgoing_select()}
+    pieces.update(column=column_select(), arrival=arrival_select())
+    rows, starts = [], {}
+    for name, piece in pieces.items():
+        starts[name] = sum(map(len, rows))
+        for matrix in np.asarray(piece, np.float32):
+            padded = np.zeros((-(-matrix.shape[0] // 16) * 16, LANES), np.float32)
+            padded[: matrix.shape[0], : matrix.shape[1]] = matrix
+            rows.append(padded)
+    return np.concatenate(rows).astype(ml_dtypes.bfloat16), starts
+
+
 def prepare_kernel(
-    place, blocks_ref, mass_ref, disp_ref, prev_ref, diag_ref, off_ref, radius_ref, lambda_ref, mu_ref,
-    parts_ref, place_of_ref, shuffle_ref, outgoing_ref, column_ref, arrival_ref,
+    starts, place, blocks_ref, mass_ref, disp_ref, prev_ref, diag_ref, off_ref, radius_ref, lambda_ref, mu_ref,
+    parts_ref, packed_ref,
     operator_out, back_out, material_out, own_out, free_out, info_out, outgoing_out, column_out, arrival_out,
     shuffled,
 ):
     operator = jnp.zeros((STRAINS, 2 * NODES), F32)
-    for term, factor in enumerate((diag_ref[0], off_ref[0], off_ref[1], diag_ref[1], radius_ref[...])):
-        spread_i = exact_dot(place_of_ref[0], factor) * place_of_ref[1]
+    first = starts["place"]
+    at_i = packed_ref[first : first + 160, :5].astype(F32)[:STRAINS]
+    at_j = packed_ref[first + 160 : first + 320, :5].astype(F32)[:STRAINS]
+    terms = ((diag_ref, 0), (off_ref, 0), (off_ref, 5), (diag_ref, 5), (radius_ref, 0))
+    for term, (ref, row) in enumerate(terms):
+        factor = jnp.concatenate([ref[row + i] for i in range(5)], axis=0)
+        spread_i = exact_dot(at_i, factor) * at_j
         operator = operator + parts_ref[term] * exact_dot(spread_i, jnp.ones((5, 2 * NODES), F32))
     operator_out[...] = operator.astype(BF16)
     back_out[...] = operator.T.astype(BF16)
@@ -301,15 +320,20 @@
         own_out[:, lanes] = value
         free_out[:, lanes] = jnp.where(live > index, 2.0 * value - own_rows(prev_ref, lanes), 0.0)
 
-    outgoing_out[...] = outgoing_ref[place[0]]
-    column_out[...] = column_ref[2 * place[0] + place[1]]
-    arrival_out[...] = arrival_ref[2 * place[0] + place[1]]
+    def packed(name, index, rows, columns):
+        first = pl.multiple_of(starts[name] + index * rows, 16)
+        return packed_ref[pl.ds(first, rows), :columns]
+
+    outgoing_out[...] = packed("outgoing", place[0], 64, NODES)
+    column_out[...] = packed("column", 2 * place[0] + place[1], 32, 64)
+    arrival_out[...] = packed("arrival", 2 * place[0] + place[1], NODES, 64)
+    shuffle = packed_ref[starts["shuffle"] : starts["shuffle"] + LANES]
 
     for which, (ref, factor) in enumerate(((lambda_ref, 1.0), (mu_ref, 2.0))):
         value = ref[...] * factor
         high = value.astype(BF16)
         low = (value - high.astype(F32)).astype(BF16)
-        shuffled[which] = dot(high, shuffle_ref[...]) + dot(low, shuffle_ref[...])
+        shuffled[which] = dot(high, shuffle) + dot(low, shuffle)
     group = lax.broadcasted_iota(jnp.int32, (8, LANES), 1) // 8
     row = lax.broadcasted_iota(jnp.int32, (8, LANES), 0)
     for rows in range(7):
@@ -376,7 +400,7 @@
 
 
 def step_one_kernel(
-    own_ref, free_ref, info_ref, row_ref, col_ref, corner_ref,
+    own_ref, free_ref, info_ref, col_ref, corner_ref, row_ref,
     operator_ref, back_ref, table_ref, tback_ref, material_ref, select_ref,
     sum_ref, pair_ref, side_ref, faces_ref,
     tiles, both, strain, spectrum,
@@ -415,7 +439,7 @@
     forces(nodes, operator_ref, back_ref, table_ref, tback_ref, material_ref, both, strain, spectrum, emit)
 
 
-def column_kernel(faces_ref, pair_ref, side_ref, select_ref, pair_out, side_out):
+def column_kernel(faces_ref, side_ref, pair_ref, select_ref, side_out, pair_out):
     for index in range(8):
         lanes = slice(256 * index, 256 * (index + 1))
         stacked = jnp.concatenate([faces_ref[:, lanes], pair_ref[:, lanes], side_ref[:, lanes]], axis=0)
@@ -425,7 +449,7 @@
 
 
 def step_two_kernel(
-    own_ref, sum_ref, cpair_ref, cside_ref, dpair_ref, dside_ref,
+    own_ref, sum_ref, cside_ref, cpair_ref, dside_ref, dpair_ref,
     operator_ref, back_ref, table_ref, tback_ref, material_ref, select_ref,
     mid_ref, sum_out, row_out, col_out, corner_out,
     current, both, strain, spectrum,
@@ -461,7 +485,7 @@
     )
 
 
-def last_kernel(sum_ref, row_ref, col_ref, corner_ref, out_ref):
+def last_kernel(sum_ref, col_ref, corner_ref, row_ref, out_ref):
     first = lax.broadcasted_iota(jnp.int32, (4, 1), 0) == 0
     for c in range(3):
         for i in range(4):
@@ -495,21 +519,26 @@
 
 def solution(mesh):
     bands, layers = mesh.shape["colat"], mesh.shape["depth"]
-    parts, place_of = strain_terms()
+    parts, _ = strain_terms()
+    packed, starts = packed_constants()
     table, tback = sample_tables()
 
+    def target(c, d, by_c, by_d):
+        past = not 0 <= d + by_d < layers
+        return (c + by_c + past * (bands // 2)) % bands * layers + (d + by_d) % layers
+
     def shifted(array, by_c, by_d):
-        pairs = [
-            (c * layers + d, (c + by_c) % bands * layers + (d + by_d) % layers)
-            for c in range(bands)
-            for d in range(layers)
-        ]
+        pairs = [(c * layers + d, target(c, d, by_c, by_d)) for c in range(bands) for d in range(layers)]
         return lax.ppermute(array, ("colat", "depth"), pairs)
 
     def swapped(array, axis, odd):
-        count = mesh.shape[axis]
-        pairs = [(n, (n + 1) % count if n % 2 == odd else (n - 1) % count) for n in range(count)]
-        return lax.ppermute(array, axis, pairs)
+        along_c = axis == "colat"
+        pairs = []
+        for c in range(bands):
+            for d in range(layers):
+                step = 1 if (c if along_c else d) % 2 == odd else -1
+                pairs.append((c * layers + d, target(c, d, step * along_c, step * (not along_c))))
+        return lax.ppermute(array, ("colat", "depth"), pairs)
 
     def per_device(displacement, previous, node_blocks, inverse_mass, jac_diag, jac_off, inv_radius, lame_l, lame_m):
         at_c, at_d = lax.axis_index("colat"), lax.axis_index("depth")
@@ -527,12 +556,12 @@
             ],
             far=3, flops=2 * 10**11, vmem=62 * 1024 * 1024,
         )(node_blocks, inverse_mass, displacement)
+        col = shifted(col, 0, -1)
         corner = shifted(corner, -1, -1)
-        col = shifted(col, 0, -1)
         row = shifted(row, -1, 0)
 
         operator, back, material, own, free, info, outgoing, column, arrival = call(
-            prepare_kernel,
+            functools.partial(prepare_kernel, starts),
             (
                 shape(STRAINS, 2 * NODES, dtype=BF16),
                 shape(2 * NODES, STRAINS, dtype=BF16),
@@ -545,13 +574,11 @@
                 shape(NODES, 64, dtype=BF16),
             ),
             [pltpu.VMEM((2, 400, LANES), F32)],
-            scalars=3, inputs=13, flops=10**9,
+            scalars=3, inputs=9, flops=10**9,
         )(
             place, node_blocks, inverse_mass, displacement, previous,
-            jac_diag.reshape(2, 5, 5), jac_off.reshape(2, 5, 5), inv_radius.reshape(5, 5),
-            lame_l.reshape(400, LANES), lame_m.reshape(400, LANES),
-            jnp.asarray(parts), jnp.asarray(place_of), jnp.asarray(lane_shuffle()),
-            jnp.asarray(outgoing_select()), jnp.asarray(column_select()), jnp.asarray(arrival_select()),
+            jac_diag.reshape(10, 1, 5), jac_off.reshape(10, 1, 5), inv_radius.reshape(5, 1, 5),
+            lame_l.reshape(400, LANES), lame_m.reshape(400, LANES), jnp.asarray(parts), jnp.asarray(packed),
         )
 
         work = [
@@ -566,12 +593,12 @@
             (shape(NODES, WIDTH + LANES), tile, tile, shape(32, WIDTH, dtype=BF16)),
             [pltpu.VMEM((32, WIDTH + LANES), F32)] + work,
             inputs=12, flops=10**9,
-        )(own, free, info, row, col, corner, *shared, outgoing)
+        )(own, free, info, col, corner, row, *shared, outgoing)
+        cside = swapped(side, "colat", 1)
         cpair = swapped(pair, "colat", 0)
-        cside = swapped(side, "colat", 1)
-        pair, side = call(column_kernel, (tile, tile), inputs=4)(faces, cpair, cside, column)
+        side, pair = call(column_kernel, (tile, tile), inputs=4)(faces, cside, cpair, column)
+        dside = swapped(side, "depth", 1)
         dpair = swapped(pair, "depth", 0)
-        dside = swapped(side, "depth", 1)
         row_face = shape(3, 4, WIDTH, dtype=BF16)
         middle, final, row, col, corner = call(
             step_two_kernel,
@@ -581,11 +608,11 @@
             ),
             [pltpu.VMEM((NODES, WIDTH), F32)] + work,
             inputs=12, flops=10**9,
-        )(own, total, cpair, cside, dpair, dside, *shared, arrival)
+        )(own, total, cside, cpair, dside, dpair, *shared, arrival)
+        col = shifted(col, 0, 1)
         corner = shifted(corner, 1, 1)
-        col = shifted(col, 0, 1)
         row = shifted(row, 1, 0)
-        final = call(last_kernel, shape(3, 4, 4, WIDTH), inputs=4)(final, row, col, corner)
+        final = call(last_kernel, shape(3, 4, 4, WIDTH), inputs=4)(final, col, corner, row)
         return middle.reshape(displacement.shape), final
 
     return jax.shard_map(

time: 52.5 us -> 47.5 us (0.905)
  waiting for transfers between devices: 22.4 us -> 18.8 us
  local copies, waits for them, and re-layouts: 5.37 us -> 2.5 us
  starting transfers between devices: 12.1 us -> 13.8 us
    ppermute x4, waiting for transfers between devices: 13.5 us -> 8.92 us  [swapped(): return lax.ppermute(array, ('colat', 'depth'), pairs)]
    ppermute x4, starting transfers between devices: 1.42 us -> 4.63 us  [swapped(): return lax.ppermute(array, ('colat', 'depth'), pairs)]
    unnamed x33 -> x26, local copies, waits for them, and re-layouts: 4.51 us -> 1.64 us
    ppermute x6, starting transfers between devices: 10.6 us -> 9.17 us  [shifted(): return lax.ppermute(array, ('colat', 'depth'), pairs)]
    ppermute x6, waiting for transfers between devices: 8.84 us -> 9.9 us  [shifted(): return lax.ppermute(array, ('colat', 'depth'), pairs)]
  transfers between devices with their start and end apart: 10 -> 10, of which waited for: 5 -> 3; matrix products, arithmetic and copies ran while one was open for 4% -> 2% of each run, Pallas kernels for 5% -> 6%
where the time goes in v4:
time: 47.5 us; the launch traced here: 47.3 us
  waiting for transfers between devices  18.8 us (40%)
  starting transfers between devices  13.8 us (29%)
  Pallas kernels  11.3 us (24%)
  local copies, waits for them, and re-layouts  2.5 us (5%)
  between operations  0.82 us (2%)
    ppermute x6, waiting for transfers between devices, shifted(): return lax.ppermute(array, ('colat', 'depth'), pairs)  9.9 us
    ppermute x6, starting transfers between devices, shifted(): return lax.ppermute(array, ('colat', 'depth'), pairs)  9.17 us
    ppermute x4, waiting for transfers between devices, swapped(): return lax.ppermute(array, ('colat', 'depth'), pairs)  8.92 us
    ppermute x4, starting transfers between devices, swapped(): return lax.ppermute(array, ('colat', 'depth'), pairs)  4.63 us
    pallas_call x1, Pallas kernels, per_device(): call(step_one_kernel, (shape(NODES, WIDTH + LANES), tile, tile, shape(32,...  3.36 us
    pallas_call x1, Pallas kernels, per_device(): call(functools.partial(prepare_kernel, starts), (shape(STRAINS, 2 * NODES...  2.74 us
    pallas_call x1, Pallas kernels, per_device(): call(step_two_kernel, (shape(OWN, WIDTH), shape(3, 4, 4, WIDTH), row_face...  2.28 us
    pallas_call x1, Pallas kernels, per_device(): call(first_kernel, (row_face, row_face, point), [pltpu.SMEM((4, 4), jnp.i...  1.87 us
  transfers between devices with their start and end apart: 10, of which 3 were waited for; matrix products, arithmetic and copies ran while one was open for 2% of the time, Pallas kernels for 6%

profile of v4, /device:TPU:0, one launch (start us, length us, event | category | flops | bytes accessed | tf_op | source)
XLA Modules:
  0.0 47.3 jit_solution(6262293298600529458)
XLA Ops:
  0.6 0.0 copy-start.2
  0.6 0.0 copy-start.3
  0.7 0.0 copy-start.4
  0.7 0.0 copy-start.5
  0.7 0.0 copy-start.11
  0.7 1.9 %shard_map.141 = (bf16[3,4,2176]{2,1,0:T(4,128)(2,1)}, bf16[3,4,2176]{2,1,0:T(4,128)(2,1)}, bf16[3,1,2176]{2,1,0:T(2,128)(2,1)}) custom-call(s32[4,4]{1,0:T(4,128)} %blocks_hbm.1, f32[4,4]{1,0:T(4,128)} %mass_hbm.1, f32[3,4,4,2048]{3,2,1,0:T(4,128)} %disp_hbm.1), custom_call_target="tpu_custom_call" | custom-call | flops 199999995904 | bytes 1048576 | tf_op jit(solution)/shard_map/pallas_call | solution.py:548
  2.6 8.5 %collective-permute-start.1 = (bf16[3,1,2176]{2,1,0:T(2,128)(2,1)}, bf16[3,1,2176]{2,1,0:T(2,128)(2,1)S(1)}, u32[]{:S(2)}, u32[]{:S(2)}) collective-permute-start(bf16[3,1,2176]{2,1,0:T(2,128)(2,1)} %get-tuple-element.29), channel_id=1, source_target_pairs={{0,63},{1,120},{2,121},{3,122},{4,123},{5,124},{6,125},{7,126},{8,... | collective-permute-start | bytes 39176 | tf_op jit(solution)/shard_map/ppermute | solution.py:532
  11.1 0.4 collective-permute-start
  11.5 0.0 collective-permute-start.2
  11.5 0.0 copy-start.10
  11.5 0.0 copy-start.7
  11.5 0.1 pad_add_fusion.place
  11.6 0.0 copy-done.2
  11.6 0.0 copy-done.3
  11.6 0.0 copy-done.4
  11.6 0.0 copy-done.5
  11.6 0.0 copy-done.11
  11.7 0.5 %copy-done.10 = f32[4,4]{1,0:T(4,128)S(1)} copy-done((f32[4,4]{1,0:T(4,128)S(1)}, f32[4,4]{1,0:T(4,128)}, u32[]{:S(2)}) %copy-start.10) | copy-done | bytes 88
  12.2 0.0 copy-done.9
  12.2 0.0 copy-done.8
  12.2 0.0 copy-done.7
  12.2 0.1 copy-done.6
  12.3 0.9 %copy-done.12 = bf16[1024,128]{1,0:T(8,128)(2,1)S(1)} copy-done((bf16[1024,128]{1,0:T(8,128)(2,1)S(1)}, bf16[1024,128]{1,0:T(8,128)(2,1)}, u32[]{:S(2)}) %copy-start.12) | copy-done | bytes 262168
  13.3 2.7 %shard_map.140 = (bf16[152,160]{1,0:T(8,128)(2,1)S(1)}, bf16[160,152]{1,0:T(8,128)(2,1)S(1)}, f32[16,56,128]{2,1,0:T(8,128)S(1)}, f32[48,2048]{1,0:T(8,128)S(1)}...) custom-call(s32[4]{0:T(128)S(1)} %pad_add_fusion.place, ...), custom_call_target="tpu_custom_call" | custom-call | flops 1000000000 | bytes 1048576 | tf_op jit(solution)/shard_map/pallas_call | solution.py:563
  16.0 0.0 collective-permute-done.1.corner_ref
  16.0 0.0 collective-permute-done.col_ref
  16.0 0.0 collective-permute-done.2.row_ref
  16.0 0.0 copy-done
  16.0 0.0 copy-done.1
  16.0 3.4 %shard_map.142 = (f32[80,2176]{1,0:T(8,128)S(1)}, bf16[16,2048]{1,0:T(8,128)(2,1)S(1)}, bf16[16,2048]{1,0:T(8,128)(2,1)S(1)}, bf16[32,2048]{1,0:T(8,128)(2,1)S(1)}) custom-call(f32[48,2048]{1,0:T(8,128)S(1)} %get-tuple-element.25.own_ref, f32[48,2048]{1,0:T(8,128)S(1)} %get-tuple-element.26.free_ref, f32[56,128]{1,0:T(8,128)S(1)} %get-tuple-element.27.info_ref, ...), custom_call_target="tpu_custom_call" | custom-call | flops 1000000000 | bytes 1048576 | tf_op jit(solution)/shard_map/pallas_call | solution.py:591
  19.4 1.4 %collective-permute-start.3 = (bf16[16,2048]{1,0:T(8,128)(2,1)S(1)}, bf16[16,2048]{1,0:T(8,128)(2,1)S(1)}, u32[]{:S(2)}, u32[]{:S(2)}) collective-permute-start(bf16[16,2048]{1,0:T(8,128)(2,1)S(1)} %get-tuple-element.36), channel_id=1, source_target_pairs={{0,120},{1,121},{2,122},{3,123},{4,124},{5,125},{6,126},{7,127},{8... | collective-permute-start | bytes 196616 | tf_op jit(solution)/shard_map/ppermute | solution.py:541
  20.8 0.0 collective-permute-start.4
  20.8 4.5 %collective-permute-done.3.side_ref.cside_ref = bf16[16,2048]{1,0:T(8,128)(2,1)S(1)} collective-permute-done((bf16[16,2048]{1,0:T(8,128)(2,1)S(1)}, bf16[16,2048]{1,0:T(8,128)(2,1)S(1)}, u32[]{:S(2)}, u32[]{:S(2)}) %collective-permute-start.3) | collective-permute-done | bytes 65568 | tf_op jit(solution)/shard_map/ppermute | solution.py:541
  25.3 0.0 collective-permute-done.4.pair_ref.cpair_ref
  25.3 0.2 shard_map.143
  25.5 3.2 %collective-permute-start.5 = (bf16[16,2048]{1,0:T(8,128)(2,1)S(1)}, bf16[16,2048]{1,0:T(8,128)(2,1)S(1)}, u32[]{:S(2)}, u32[]{:S(2)}) collective-permute-start(bf16[16,2048]{1,0:T(8,128)(2,1)S(1)} %get-tuple-element.40), channel_id=1, source_target_pairs={{0,71},{1,2},{2,1},{3,4},{4,3},{5,6},{6,5},{7,64},{8,79},{9,10},{1... | collective-permute-start | bytes 196616 | tf_op jit(solution)/shard_map/ppermute | solution.py:541
  28.7 0.0 collective-permute-start.6
  28.7 4.5 %collective-permute-done.5.dside_ref = bf16[16,2048]{1,0:T(8,128)(2,1)S(1)} collective-permute-done((bf16[16,2048]{1,0:T(8,128)(2,1)S(1)}, bf16[16,2048]{1,0:T(8,128)(2,1)S(1)}, u32[]{:S(2)}, u32[]{:S(2)}) %collective-permute-start.5) | collective-permute-done | bytes 65568 | tf_op jit(solution)/shard_map/ppermute | solution.py:541
  33.1 0.0 collective-permute-done.6.dpair_ref
  33.1 2.3 %shard_map.144 = (f32[48,2048]{1,0:T(8,128)S(1)}, f32[3,4,4,2048]{3,2,1,0:T(4,128)S(1)}, bf16[3,4,2048]{2,1,0:T(4,128)(2,1)S(1)}, bf16[3,4,2048]{2,1,0:T(4,128)(2,1)S(1)}, bf16[3,1,2048]{2,1,0:T(2,128)(2,1)S(1)}) custom-call(f32[48,2048]{1,0:T(8,128)S(1)} %get-tuple-element.25.own_ref, f32[80,2176]{1,0:T(8,128)S(1)} %get-tuple-element.35.sum_ref, ...), custom_call_target="tpu_custom_call" | custom-call | flops 1000000000 | bytes 1048576 | tf_op jit(solution)/shard_map/pallas_call | solution.py:603
  35.4 0.1 collective-permute-start.7
  35.5 0.1 collective-permute-start.9
  35.6 0.1 collective-permute-start.8
  35.7 0.9 %reshape.27 = f32[3,4,4,2048]{3,2,1,0:T(4,128)} reshape(f32[48,2048]{1,0:T(8,128)S(1)} %get-tuple-element.43) | data formatting | bytes 786432 | tf_op jit(solution)/shard_map/reshape | solution.py:616
  36.5 9.9 %collective-permute-done.8.corner_ref = bf16[3,1,2048]{2,1,0:T(2,128)(2,1)S(1)} collective-permute-done((bf16[3,1,2048]{2,1,0:T(2,128)(2,1)S(1)}, bf16[3,1,2048]{2,1,0:T(2,128)(2,1)S(1)}, u32[]{:S(2)}, u32[]{:S(2)}) %collective-permute-start.8) | collective-permute-done | bytes 12320 | tf_op jit(solution)/shard_map/ppermute | solution.py:532
  46.4 0.0 collective-permute-done.7.col_ref
  46.4 0.0 collective-permute-done.9.row_ref
  46.4 0.9 %shard_map.145 = f32[3,4,4,2048]{3,2,1,0:T(4,128)} custom-call(f32[3,4,4,2048]{3,2,1,0:T(4,128)S(1)} %get-tuple-element.44.sum_ref, bf16[3,4,2048]{2,1,0:T(4,128)(2,1)S(1)} %collective-permute-done.7.col_ref, bf16[3,1,2048]{2,1,0:T(2,128)(2,1)S(1)} %collective-permute-done.8.corner_ref, bf16[3,4,2048]{2,1,0:T(4,128)(2,1)S(1)} %collective-permute-done.9.row_ref), custom_call_target="tpu_custom_call" | custom-call | bytes 1048576 | tf_op jit(solution)/shard_map/pallas_call | solution.py:615
  (6 shorter events, 0.0 us)
Async XLA Ops:
  0.6 11.0 %copy-start.2 = (f32[3,4,4,2048]{3,2,1,0:T(4,128)S(1)}, f32[3,4,4,2048]{3,2,1,0:T(4,128)}, u32[]{:S(2)}) copy-start(f32[3,4,4,2048]{3,2,1,0:T(4,128)} %disp_hbm.1) | copy-start | bytes 1179652
  0.6 11.0 %copy-start.3 = (f32[3,4,4,2048]{3,2,1,0:T(4,128)S(1)}, f32[3,4,4,2048]{3,2,1,0:T(4,128)}, u32[]{:S(2)}) copy-start(f32[3,4,4,2048]{3,2,1,0:T(4,128)} %prev_ref.1) | copy-start | bytes 1179652
  0.7 11.0 %copy-start.4 = (f32[1,5,1,5,2048]{4,2,3,1,0:T(1,128)S(1)}, f32[1,5,1,5,2048]{4,2,3,1,0:T(1,128)}, u32[]{:S(2)}) copy-start(f32[1,5,1,5,2048]{4,2,3,1,0:T(1,128)} %param.20) | copy-start | bytes 614404
  0.7 11.0 %copy-start.5 = (f32[1,5,1,5,2048]{4,2,3,1,0:T(1,128)S(1)}, f32[1,5,1,5,2048]{4,2,3,1,0:T(1,128)}, u32[]{:S(2)}) copy-start(f32[1,5,1,5,2048]{4,2,3,1,0:T(1,128)} %param.21) | copy-start | bytes 614404
  0.7 11.0 %copy-start.11 = (f32[5,152,160]{2,1,0:T(8,128)S(1)}, f32[5,152,160]{2,1,0:T(8,128)}, u32[]{:S(2)}) copy-start(f32[5,152,160]{2,1,0:T(8,128)} %constant.38.clone.parts_ref) | copy-start | bytes 1459204
  2.6 13.4 %collective-permute-start.1 = (bf16[3,1,2176]{2,1,0:T(2,128)(2,1)}, bf16[3,1,2176]{2,1,0:T(2,128)(2,1)S(1)}, u32[]{:S(2)}, u32[]{:S(2)}) collective-permute-start(bf16[3,1,2176]{2,1,0:T(2,128)(2,1)} %get-tuple-element.29), channel_id=1, source_target_pairs={{0,63},{1,120},{2,121},{3,122},{4,123},{5,124},{6,125},{7,126},{8,... | collective-permute-start | bytes 39176 | tf_op jit(solution)/shard_map/ppermute | solution.py:532
  11.1 4.9 %collective-permute-start = (bf16[3,4,2176]{2,1,0:T(4,128)(2,1)}, bf16[3,4,2176]{2,1,0:T(4,128)(2,1)S(1)}, u32[]{:S(2)}, u32[]{:S(2)}) collective-permute-start(bf16[3,4,2176]{2,1,0:T(4,128)(2,1)} %get-tuple-element.28), channel_id=1, source_target_pairs={{0,71},{1,0},{2,1},{3,2},{4,3},{5,4},{6,5},{7,6},{8,79},{9,8},{10,... | collective-permute-start | bytes 156680 | tf_op jit(solution)/shard_map/ppermute | solution.py:532
  11.5 4.5 %collective-permute-start.2 = (bf16[3,4,2176]{2,1,0:T(4,128)(2,1)}, bf16[3,4,2176]{2,1,0:T(4,128)(2,1)S(1)}, u32[]{:S(2)}, u32[]{:S(2)}) collective-permute-start(bf16[3,4,2176]{2,1,0:T(4,128)(2,1)} %get-tuple-element.30), channel_id=1, source_target_pairs={{0,120},{1,121},{2,122},{3,123},{4,124},{5,125},{6,126},{7,127},{8... | collective-permute-start | bytes 156680 | tf_op jit(solution)/shard_map/ppermute | solution.py:532
  11.5 0.7 %copy-start.10 = (f32[4,4]{1,0:T(4,128)S(1)}, f32[4,4]{1,0:T(4,128)}, u32[]{:S(2)}) copy-start(f32[4,4]{1,0:T(4,128)} %mass_hbm.1) | copy-start | bytes 196
  11.5 0.7 %copy-start.9 = (s32[4,4]{1,0:T(4,128)S(1)}, s32[4,4]{1,0:T(4,128)}, u32[]{:S(2)}) copy-start(s32[4,4]{1,0:T(4,128)} %blocks_hbm.1) | copy-start | bytes 196
  11.5 0.7 %copy-start.8 = (f32[1,5,1,5]{3,2,1,0:T(1,128)S(1)}, f32[1,5,1,5]{3,2,1,0:T(1,128)}, u32[]{:S(2)}) copy-start(f32[1,5,1,5]{3,2,1,0:T(1,128)} %param.19) | copy-start | bytes 304
  11.5 0.7 %copy-start.7 = (f32[2,1,5,1,5]{4,3,2,1,0:T(1,128)S(1)}, f32[2,1,5,1,5]{4,3,2,1,0:T(1,128)}, u32[]{:S(2)}) copy-start(f32[2,1,5,1,5]{4,3,2,1,0:T(1,128)} %param.18) | copy-start | bytes 604
  11.6 0.7 %copy-start.6 = (f32[2,1,5,1,5]{4,3,2,1,0:T(1,128)S(1)}, f32[2,1,5,1,5]{4,3,2,1,0:T(1,128)}, u32[]{:S(2)}) copy-start(f32[2,1,5,1,5]{4,3,2,1,0:T(1,128)} %param.17) | copy-start | bytes 604
  12.3 0.9 %copy-start.12 = (bf16[1024,128]{1,0:T(8,128)(2,1)S(1)}, bf16[1024,128]{1,0:T(8,128)(2,1)}, u32[]{:S(2)}) copy-start(bf16[1024,128]{1,0:T(8,128)(2,1)} %constant.39.clone.packed_ref) | copy-start | bytes 786436
  13.3 2.8 %copy-start = (bf16[16,128,256]{2,1,0:T(8,128)(2,1)S(1)}, bf16[16,128,256]{2,1,0:T(8,128)(2,1)}, u32[]{:S(2)}) copy-start(bf16[16,128,256]{2,1,0:T(8,128)(2,1)} %constant.41.clone.tback_ref) | copy-start | bytes 3145732
  13.3 2.8 %copy-start.1 = (bf16[16,256,128]{2,1,0:T(8,128)(2,1)S(1)}, bf16[16,256,128]{2,1,0:T(8,128)(2,1)}, u32[]{:S(2)}) copy-start(bf16[16,256,128]{2,1,0:T(8,128)(2,1)} %constant.40.clone.table_ref) | copy-start | bytes 3145732
  19.4 5.9 %collective-permute-start.3 = (bf16[16,2048]{1,0:T(8,128)(2,1)S(1)}, bf16[16,2048]{1,0:T(8,128)(2,1)S(1)}, u32[]{:S(2)}, u32[]{:S(2)}) collective-permute-start(bf16[16,2048]{1,0:T(8,128)(2,1)S(1)} %get-tuple-element.36), channel_id=1, source_target_pairs={{0,120},{1,121},{2,122},{3,123},{4,124},{5,125},{6,126},{7,127},{8... | collective-permute-start | bytes 196616 | tf_op jit(solution)/shard_map/ppermute | solution.py:541
  20.8 4.5 %collective-permute-start.4 = (bf16[16,2048]{1,0:T(8,128)(2,1)S(1)}, bf16[16,2048]{1,0:T(8,128)(2,1)S(1)}, u32[]{:S(2)}, u32[]{:S(2)}) collective-permute-start(bf16[16,2048]{1,0:T(8,128)(2,1)S(1)} %get-tuple-element.37), channel_id=1, source_target_pairs={{0,8},{1,9},{2,10},{3,11},{4,12},{5,13},{6,14},{7,15},{8,0},{9,1},... | collective-permute-start | bytes 196616 | tf_op jit(solution)/shard_map/ppermute | solution.py:541
  25.5 7.7 %collective-permute-start.5 = (bf16[16,2048]{1,0:T(8,128)(2,1)S(1)}, bf16[16,2048]{1,0:T(8,128)(2,1)S(1)}, u32[]{:S(2)}, u32[]{:S(2)}) collective-permute-start(bf16[16,2048]{1,0:T(8,128)(2,1)S(1)} %get-tuple-element.40), channel_id=1, source_target_pairs={{0,71},{1,2},{2,1},{3,4},{4,3},{5,6},{6,5},{7,64},{8,79},{9,10},{1... | collective-permute-start | bytes 196616 | tf_op jit(solution)/shard_map/ppermute | solution.py:541
  28.7 4.5 %collective-permute-start.6 = (bf16[16,2048]{1,0:T(8,128)(2,1)S(1)}, bf16[16,2048]{1,0:T(8,128)(2,1)S(1)}, u32[]{:S(2)}, u32[]{:S(2)}) collective-permute-start(bf16[16,2048]{1,0:T(8,128)(2,1)S(1)} %get-tuple-element.41), channel_id=1, source_target_pairs={{0,1},{1,0},{2,3},{3,2},{4,5},{5,4},{6,7},{7,6},{8,9},{9,8},{10,11... | collective-permute-start | bytes 196616 | tf_op jit(solution)/shard_map/ppermute | solution.py:541
  35.4 11.0 %collective-permute-start.7 = (bf16[3,4,2048]{2,1,0:T(4,128)(2,1)S(1)}, bf16[3,4,2048]{2,1,0:T(4,128)(2,1)S(1)}, u32[]{:S(2)}, u32[]{:S(2)}) collective-permute-start(bf16[3,4,2048]{2,1,0:T(4,128)(2,1)S(1)} %get-tuple-element.45), channel_id=1, source_target_pairs={{0,1},{1,2},{2,3},{3,4},{4,5},{5,6},{6,7},{7,64},{8,9},{9,10},{10,... | collective-permute-start | bytes 147464 | tf_op jit(solution)/shard_map/ppermute | solution.py:532
  35.5 10.9 %collective-permute-start.9 = (bf16[3,4,2048]{2,1,0:T(4,128)(2,1)S(1)}, bf16[3,4,2048]{2,1,0:T(4,128)(2,1)S(1)}, u32[]{:S(2)}, u32[]{:S(2)}) collective-permute-start(bf16[3,4,2048]{2,1,0:T(4,128)(2,1)S(1)} %get-tuple-element.47), channel_id=1, source_target_pairs={{0,8},{1,9},{2,10},{3,11},{4,12},{5,13},{6,14},{7,15},{8,16},{9,17... | collective-permute-start | bytes 147464 | tf_op jit(solution)/shard_map/ppermute | solution.py:532
  35.6 10.8 %collective-permute-start.8 = (bf16[3,1,2048]{2,1,0:T(2,128)(2,1)S(1)}, bf16[3,1,2048]{2,1,0:T(2,128)(2,1)S(1)}, u32[]{:S(2)}, u32[]{:S(2)}) collective-permute-start(bf16[3,1,2048]{2,1,0:T(2,128)(2,1)S(1)} %get-tuple-element.46), channel_id=1, source_target_pairs={{0,9},{1,10},{2,11},{3,12},{4,13},{5,14},{6,15},{7,72},{8,17},{9,1... | collective-permute-start | bytes 36872 | tf_op jit(solution)/shard_map/ppermute | solution.py:532

commit v5 on v4

--- a/solution.py
+++ b/solution.py
@@ -275,59 +275,85 @@
 
 
 def packed_constants():
-    _, place_of = strain_terms()
-    pieces = {"shuffle": lane_shuffle()[None], "place": place_of, "outgoing": outgoing_select()}
-    pieces.update(column=column_select(), arrival=arrival_select())
-    rows, starts = [], {}
-    for name, piece in pieces.items():
-        starts[name] = sum(map(len, rows))
-        for matrix in np.asarray(piece, np.float32):
-            padded = np.zeros((-(-matrix.shape[0] // 16) * 16, LANES), np.float32)
-            padded[: matrix.shape[0], : matrix.shape[1]] = matrix
-            rows.append(padded)
-    return np.concatenate(rows).astype(ml_dtypes.bfloat16), starts
+    parts, place_of = strain_terms()
+    upper = np.zeros((3, STRAINS, 2 * LANES), np.float32)
+    for term in range(4):
+        upper[term // 2, :, NODES * (term % 2) : NODES * (term % 2 + 1)] = parts[term, :, :NODES]
+    upper[2, :, : 2 * NODES] = parts[4]
+    columns = (
+        {"arrival": arrival_select(), "outgoing": outgoing_select()},
+        {"shuffle": lane_shuffle()[None], "place": place_of, "column": column_select()},
+    )
+    lower, starts = np.zeros((3 * STRAINS + 560, 2 * LANES), np.float32), {}
+    lower[: 3 * STRAINS] = upper.reshape(-1, 2 * LANES)
+    for side, pieces in enumerate(columns):
+        first = 3 * STRAINS
+        for name, piece in pieces.items():
+            starts[name] = (first, LANES * side)
+            for matrix in np.asarray(piece, np.float32):
+                rows, width = matrix.shape
+                lower[first : first + rows, LANES * side : LANES * side + width] = matrix
+                first += rows
+    return lower, starts
 
 
 def prepare_kernel(
-    starts, place, blocks_ref, mass_ref, disp_ref, prev_ref, diag_ref, off_ref, radius_ref, lambda_ref, mu_ref,
-    parts_ref, packed_ref,
+    starts, place_ref, blocks_ref, mass_ref, disp_ref, prev_ref, diag_ref, off_ref, radius_ref, lambda_ref, mu_ref,
+    packed_ref,
     operator_out, back_out, material_out, own_out, free_out, info_out, outgoing_out, column_out, arrival_out,
     shuffled,
 ):
-    operator = jnp.zeros((STRAINS, 2 * NODES), F32)
-    first = starts["place"]
-    at_i = packed_ref[first : first + 160, :5].astype(F32)[:STRAINS]
-    at_j = packed_ref[first + 160 : first + 320, :5].astype(F32)[:STRAINS]
-    terms = ((diag_ref, 0), (off_ref, 0), (off_ref, 5), (diag_ref, 5), (radius_ref, 0))
-    for term, (ref, row) in enumerate(terms):
+    def constant(name, rows, columns, index=0):
+        first, lane = starts[name]
+        return packed_ref[first + rows * index : first + rows * (index + 1), lane : lane + columns]
+
+    at_i, at_j = constant("place", STRAINS, 5), constant("place", STRAINS, 5, 1)
+    factors = []
+    for ref, row in ((diag_ref, 0), (off_ref, 0), (off_ref, 5), (diag_ref, 5), (radius_ref, 0)):
         factor = jnp.concatenate([ref[row + i] for i in range(5)], axis=0)
         spread_i = exact_dot(at_i, factor) * at_j
-        operator = operator + parts_ref[term] * exact_dot(spread_i, jnp.ones((5, 2 * NODES), F32))
+        factors.append(jnp.sum(spread_i, axis=1, keepdims=True))
+    parts = [packed_ref[STRAINS * n : STRAINS * (n + 1)] for n in range(3)]
+    operator = parts[2][:, : 2 * NODES] * factors[4]
+    plain = sum(parts[t // 2][:, NODES * (t % 2) : NODES * (t % 2 + 1)] * factors[t] for t in range(4))
+    operator = operator + jnp.concatenate([plain, jnp.zeros_like(plain)], axis=1)
     operator_out[...] = operator.astype(BF16)
     back_out[...] = operator.T.astype(BF16)
 
-    nodes = [(i, j) for i in range(4) for j in range(4)]
-    live = jnp.concatenate([node_column(lambda at: blocks_ref[at[0], at[1]].astype(F32), nodes)] * 3, axis=0)
-    mass = jnp.concatenate([node_column(lambda at: mass_ref[at[0], at[1]], nodes)] * 3, axis=0)
+    def column(ref):
+        shape = (4, 4)
+        diagonal = lax.broadcasted_iota(jnp.int32, shape, 0) == lax.broadcasted_iota(jnp.int32, shape, 1)
+        value = ref[...].astype(F32)
+        pieces = [jnp.sum(jnp.where(diagonal, value[i : i + 1], 0.0), axis=1, keepdims=True) for i in range(4)]
+        return jnp.concatenate(pieces * 3, axis=0)
+
+    live, mass = column(blocks_ref), column(mass_ref)
     lane = lax.broadcasted_iota(jnp.int32, (OWN, LANES), 1)
     info_out[:OWN] = jnp.where(lane == 0, mass, jnp.where(lane == 1, live, 0.0))
-    lane = lax.broadcasted_iota(jnp.int32, (8, LANES), 1)
-    rests = jnp.where(lane == 0, place[2].astype(F32), jnp.where(lane == 1, place[3].astype(F32), 0.0))
-    info_out[OWN:] = rests
+    info_out[OWN:] = place_ref[...]
     for index in range(8):
         lanes = slice(256 * index, 256 * (index + 1))
         value = jnp.where(live > index, own_rows(disp_ref, lanes), 0.0)
         own_out[:, lanes] = value
         free_out[:, lanes] = jnp.where(live > index, 2.0 * value - own_rows(prev_ref, lanes), 0.0)
 
-    def packed(name, index, rows, columns):
-        first = pl.multiple_of(starts[name] + index * rows, 16)
-        return packed_ref[pl.ds(first, rows), :columns]
-
-    outgoing_out[...] = packed("outgoing", place[0], 64, NODES)
-    column_out[...] = packed("column", 2 * place[0] + place[1], 32, 64)
-    arrival_out[...] = packed("arrival", 2 * place[0] + place[1], NODES, 64)
-    shuffle = packed_ref[starts["shuffle"] : starts["shuffle"] + LANES]
+    def packed(name, rows, columns, *bits):
+        pieces = [constant(name, rows, columns, index) for index in range(2 ** len(bits))]
+        for bit in reversed(bits):
+            pieces = [jnp.where(bit > 0.5, one, zero) for zero, one in zip(pieces[0::2], pieces[1::2])]
+        return pieces[0]
+
+    def kept(matrix, first, flag):
+        column = lax.broadcasted_iota(jnp.int32, matrix.shape, 1)
+        dropped = jnp.logical_and(jnp.logical_and(column >= first, column < first + 16), flag < 0.5)
+        return jnp.where(dropped, 0.0, matrix)
+
+    odd_c, odd_d, side_c, side_d = (place_ref[0:1, n : n + 1] for n in range(2, 6))
+    outgoing_out[...] = packed("outgoing", 64, NODES, odd_c).astype(BF16)
+    column_out[...] = kept(packed("column", 32, 64, odd_c, odd_d), 48, side_c).astype(BF16)
+    arrived = kept(packed("arrival", NODES, 64, odd_c, odd_d), 16, side_c)
+    arrival_out[...] = kept(arrived, 48, side_d).astype(BF16)
+    shuffle = constant("shuffle", LANES, LANES).astype(BF16)
 
     for which, (ref, factor) in enumerate(((lambda_ref, 1.0), (mu_ref, 2.0))):
         value = ref[...] * factor
@@ -485,6 +511,13 @@
     )
 
 
+def middle_kernel(rows_ref, out_ref):
+    for c in range(3):
+        for i in range(4):
+            at = 16 * c + 4 * i
+            out_ref[c, i] = rows_ref[at : at + 4]
+
+
 def last_kernel(sum_ref, col_ref, corner_ref, row_ref, out_ref):
     first = lax.broadcasted_iota(jnp.int32, (4, 1), 0) == 0
     for c in range(3):
@@ -519,7 +552,6 @@
 
 def solution(mesh):
     bands, layers = mesh.shape["colat"], mesh.shape["depth"]
-    parts, _ = strain_terms()
     packed, starts = packed_constants()
     table, tback = sample_tables()
 
@@ -537,12 +569,23 @@
         for c in range(bands):
             for d in range(layers):
                 step = 1 if (c if along_c else d) % 2 == odd else -1
-                pairs.append((c * layers + d, target(c, d, step * along_c, step * (not along_c))))
+                to_c, to_d = c + step * along_c, d + step * (not along_c)
+                if not 0 <= to_c < bands:
+                    to_c, to_d = c, d ^ 1
+                if not 0 <= to_d < layers:
+                    to_c, to_d = c ^ 1, d
+                pairs.append((c * layers + d, to_c * layers + to_d))
         return lax.ppermute(array, ("colat", "depth"), pairs)
 
     def per_device(displacement, previous, node_blocks, inverse_mass, jac_diag, jac_off, inv_radius, lame_l, lame_m):
         at_c, at_d = lax.axis_index("colat"), lax.axis_index("depth")
-        place = jnp.stack([at_c % 2, at_d % 2, at_c < bands - 1, at_d < layers - 1]).astype(jnp.int32)
+        lane = lax.broadcasted_iota(jnp.int32, (8, LANES), 1)
+        place = jnp.zeros((8, LANES), F32)
+        has_side_c = jnp.where(at_c % 2 == 1, at_c < bands - 1, at_c > 0)
+        has_side_d = jnp.where(at_d % 2 == 1, at_d < layers - 1, at_d > 0)
+        flags = (at_c < bands - 1, at_d < layers - 1, at_c % 2, at_d % 2, has_side_c, has_side_d)
+        for at, value in enumerate(flags):
+            place = jnp.where(lane == at, value.astype(F32), place)
         row_face = shape(3, 4, WIDTH + LANES, dtype=BF16)
         point = shape(3, 1, WIDTH + LANES, dtype=BF16)
         row, col, corner = call(
@@ -554,7 +597,7 @@
                 pltpu.VMEM((3, 4, 4, WIDTH), F32),
                 pltpu.SemaphoreType.DMA((3,)),
             ],
-            far=3, flops=2 * 10**11, vmem=62 * 1024 * 1024,
+            far=3, flops=2 * 10**10, vmem=62 * 1024 * 1024,
         )(node_blocks, inverse_mass, displacement)
         col = shifted(col, 0, -1)
         corner = shifted(corner, -1, -1)
@@ -574,11 +617,11 @@
                 shape(NODES, 64, dtype=BF16),
             ),
             [pltpu.VMEM((2, 400, LANES), F32)],
-            scalars=3, inputs=9, flops=10**9,
+            inputs=11, flops=10**9,
         )(
             place, node_blocks, inverse_mass, displacement, previous,
             jac_diag.reshape(10, 1, 5), jac_off.reshape(10, 1, 5), inv_radius.reshape(5, 1, 5),
-            lame_l.reshape(400, LANES), lame_m.reshape(400, LANES), jnp.asarray(parts), jnp.asarray(packed),
+            lame_l.reshape(400, LANES), lame_m.reshape(400, LANES), jnp.asarray(packed),
         )
 
         work = [
@@ -612,8 +655,9 @@
         col = shifted(col, 0, 1)
         corner = shifted(corner, 1, 1)
         row = shifted(row, 1, 0)
+        middle = call(middle_kernel, shape(3, 4, 4, WIDTH), inputs=1, flops=2 * 10**10, vmem=4 * 1024 * 1024)(middle)
         final = call(last_kernel, shape(3, 4, 4, WIDTH), inputs=4)(final, col, corner, row)
-        return middle.reshape(displacement.shape), final
+        return middle, final
 
     return jax.shard_map(
         per_device,

time: 47.5 us -> 43.6 us (0.918)
  the two profiles are of different devices: /device:TPU:0 before, /device:TPU:6 now
where the time goes in v5:
time: 43.6 us; the launch traced here: 43.4 us
  starting transfers between devices  15.1 us (35%)
  waiting for transfers between devices  14.7 us (34%)
  Pallas kernels  10.6 us (24%)
  local copies, waits for them, and re-layouts  2.02 us (5%)
  between operations  0.9 us (2%)
    ppermute x6, waiting for transfers between devices, shifted(): return lax.ppermute(array, ('colat', 'depth'), pairs)  7.74 us
    ppermute x4, starting transfers between devices, swapped(): return lax.ppermute(array, ('colat', 'depth'), pairs)  7.7 us
    ppermute x6, starting transfers between devices, shifted(): return lax.ppermute(array, ('colat', 'depth'), pairs)  7.44 us
    ppermute x4, waiting for transfers between devices, swapped(): return lax.ppermute(array, ('colat', 'depth'), pairs)  6.92 us
    pallas_call x1, Pallas kernels, per_device(): call(step_one_kernel, (shape(NODES, WIDTH + LANES), tile, tile, shape(32,...  3.36 us
    pallas_call x1, Pallas kernels, per_device(): call(step_two_kernel, (shape(OWN, WIDTH), shape(3, 4, 4, WIDTH), row_face...  2.28 us
    unnamed x24, local copies, waits for them, and re-layouts  2.02 us
    pallas_call x1, Pallas kernels, per_device(): call(first_kernel, (row_face, row_face, point), [pltpu.SMEM((4, 4), jnp.i...  1.82 us
  transfers between devices with their start and end apart: 10, of which 4 were waited for; matrix products, arithmetic and copies ran while one was open for 0% of the time, Pallas kernels for 5%

profile of v5, /device:TPU:6, one launch (start us, length us, event | category | flops | bytes accessed | tf_op | source)
XLA Modules:
  0.0 43.4 jit_solution(4821972097443366539)
XLA Ops:
  0.6 0.0 copy-start.2
  0.6 0.0 copy-start.5
  0.7 0.0 copy-start.4
  0.7 0.0 copy-start.3
  0.7 0.0 copy-start.9
  0.7 0.0 copy-start.10
  0.7 1.8 %shard_map.132 = (bf16[3,4,2176]{2,1,0:T(4,128)(2,1)}, bf16[3,4,2176]{2,1,0:T(4,128)(2,1)}, bf16[3,1,2176]{2,1,0:T(2,128)(2,1)}) custom-call(s32[4,4]{1,0:T(4,128)} %blocks_hbm.1, f32[4,4]{1,0:T(4,128)} %mass_hbm.1, f32[3,4,4,2048]{3,2,1,0:T(4,128)} %disp_hbm.1), custom_call_target="tpu_custom_call" | custom-call | flops 20000000000 | bytes 1048576 | tf_op jit(solution)/shard_map/pallas_call | solution.py:591
  2.5 5.9 %collective-permute-start.1 = (bf16[3,1,2176]{2,1,0:T(2,128)(2,1)}, bf16[3,1,2176]{2,1,0:T(2,128)(2,1)S(1)}, u32[]{:S(2)}, u32[]{:S(2)}) collective-permute-start(bf16[3,1,2176]{2,1,0:T(2,128)(2,1)} %get-tuple-element.29), channel_id=1, source_target_pairs={{0,63},{1,120},{2,121},{3,122},{4,123},{5,124},{6,125},{7,126},{8,... | collective-permute-start | bytes 39176 | tf_op jit(solution)/shard_map/ppermute | solution.py:564
  8.4 1.3 %collective-permute-start = (bf16[3,4,2176]{2,1,0:T(4,128)(2,1)}, bf16[3,4,2176]{2,1,0:T(4,128)(2,1)S(1)}, u32[]{:S(2)}, u32[]{:S(2)}) collective-permute-start(bf16[3,4,2176]{2,1,0:T(4,128)(2,1)} %get-tuple-element.28), channel_id=1, source_target_pairs={{0,71},{1,0},{2,1},{3,2},{4,3},{5,4},{6,5},{7,6},{8,79},{9,8},{10,... | collective-permute-start | bytes 156680 | tf_op jit(solution)/shard_map/ppermute | solution.py:564
  9.7 0.0 collective-permute-start.2
  9.8 0.0 copy-start.7
  9.8 0.0 copy-start.6
  9.8 0.0 copy-start.8
  9.9 0.0 copy-done.2
  9.9 0.0 copy-done.5
  9.9 0.0 copy-done.4
  9.9 0.0 copy-done.3
  9.9 0.0 copy-done.9
  9.9 0.0 copy-done.10
  9.9 0.6 %copy-done.7 = f32[2,1,5,1,5]{4,3,2,1,0:T(1,128)S(1)} copy-done((f32[2,1,5,1,5]{4,3,2,1,0:T(1,128)S(1)}, f32[2,1,5,1,5]{4,3,2,1,0:T(1,128)}, u32[]{:S(2)}) %copy-start.7) | copy-done | bytes 224
  10.5 0.0 copy-done.6
  10.5 0.0 copy-done.8
  10.5 1.2 %copy-done.11 = f32[1016,256]{1,0:T(8,128)S(1)} copy-done((f32[1016,256]{1,0:T(8,128)S(1)}, f32[1016,256]{1,0:T(8,128)}, u32[]{:S(2)}) %copy-start.11) | copy-done | bytes 1040408
  11.8 1.4 %shard_map.131 = (bf16[152,160]{1,0:T(8,128)(2,1)S(1)}, bf16[160,152]{1,0:T(8,128)(2,1)S(1)}, f32[16,56,128]{2,1,0:T(8,128)S(1)}, f32[48,2048]{1,0:T(8,128)S(1)}...) custom-call(f32[8,128]{1,0:T(8,128)S(1)} %select_select_fusion.place, ...), custom_call_target="tpu_custom_call" | custom-call | flops 1000000000 | bytes 1048576 | tf_op jit(solution)/shard_map/pallas_call | solution.py:606
  13.1 0.0 collective-permute-done.1.corner_ref
  13.1 0.0 collective-permute-done.col_ref
  13.1 0.0 collective-permute-done.2.row_ref
  13.2 0.0 copy-done
  13.2 0.1 copy-done.1
  13.3 3.4 %shard_map.133 = (f32[80,2176]{1,0:T(8,128)S(1)}, bf16[16,2048]{1,0:T(8,128)(2,1)S(1)}, bf16[16,2048]{1,0:T(8,128)(2,1)S(1)}, bf16[32,2048]{1,0:T(8,128)(2,1)S(1)}) custom-call(f32[48,2048]{1,0:T(8,128)S(1)} %get-tuple-element.25.own_ref, f32[48,2048]{1,0:T(8,128)S(1)} %get-tuple-element.26.free_ref, f32[56,128]{1,0:T(8,128)S(1)} %get-tuple-element.27.info_ref, ...), custom_call_target="tpu_custom_call" | custom-call | flops 1000000000 | bytes 1048576 | tf_op jit(solution)/shard_map/pallas_call | solution.py:634
  16.7 3.2 %collective-permute-start.3 = (bf16[16,2048]{1,0:T(8,128)(2,1)S(1)}, bf16[16,2048]{1,0:T(8,128)(2,1)S(1)}, u32[]{:S(2)}, u32[]{:S(2)}) collective-permute-start(bf16[16,2048]{1,0:T(8,128)(2,1)S(1)} %get-tuple-element.36), channel_id=1, source_target_pairs={{0,1},{1,0},{2,3},{3,2},{4,5},{5,4},{6,7},{7,6},{8,16},{9,17},{10,... | collective-permute-start | bytes 196616 | tf_op jit(solution)/shard_map/ppermute | solution.py:578
  19.9 0.0 collective-permute-start.4
  19.9 2.7 %collective-permute-done.3.side_ref.cside_ref = bf16[16,2048]{1,0:T(8,128)(2,1)S(1)} collective-permute-done((bf16[16,2048]{1,0:T(8,128)(2,1)S(1)}, bf16[16,2048]{1,0:T(8,128)(2,1)S(1)}, u32[]{:S(2)}, u32[]{:S(2)}) %collective-permute-start.3) | collective-permute-done | bytes 65568 | tf_op jit(solution)/shard_map/ppermute | solution.py:578
  22.6 0.0 collective-permute-done.4.pair_ref.cpair_ref
  22.6 0.2 shard_map.134
  22.7 4.5 %collective-permute-start.5 = (bf16[16,2048]{1,0:T(8,128)(2,1)S(1)}, bf16[16,2048]{1,0:T(8,128)(2,1)S(1)}, u32[]{:S(2)}, u32[]{:S(2)}) collective-permute-start(bf16[16,2048]{1,0:T(8,128)(2,1)S(1)} %get-tuple-element.40), channel_id=1, source_target_pairs={{0,8},{1,2},{2,1},{3,4},{4,3},{5,6},{6,5},{7,15},{8,0},{9,10},{10,... | collective-permute-start | bytes 196616 | tf_op jit(solution)/shard_map/ppermute | solution.py:578
  27.2 0.0 collective-permute-start.6
  27.2 3.5 %collective-permute-done.5.dside_ref = bf16[16,2048]{1,0:T(8,128)(2,1)S(1)} collective-permute-done((bf16[16,2048]{1,0:T(8,128)(2,1)S(1)}, bf16[16,2048]{1,0:T(8,128)(2,1)S(1)}, u32[]{:S(2)}, u32[]{:S(2)}) %collective-permute-start.5) | collective-permute-done | bytes 65568 | tf_op jit(solution)/shard_map/ppermute | solution.py:578
  30.7 0.8 %collective-permute-done.6.dpair_ref = bf16[16,2048]{1,0:T(8,128)(2,1)S(1)} collective-permute-done((bf16[16,2048]{1,0:T(8,128)(2,1)S(1)}, bf16[16,2048]{1,0:T(8,128)(2,1)S(1)}, u32[]{:S(2)}, u32[]{:S(2)}) %collective-permute-start.6) | collective-permute-done | bytes 65568 | tf_op jit(solution)/shard_map/ppermute | solution.py:578
  31.5 2.3 %shard_map.135 = (f32[48,2048]{1,0:T(8,128)S(1)}, f32[3,4,4,2048]{3,2,1,0:T(4,128)S(1)}, bf16[3,4,2048]{2,1,0:T(4,128)(2,1)S(1)}, bf16[3,4,2048]{2,1,0:T(4,128)(2,1)S(1)}, bf16[3,1,2048]{2,1,0:T(2,128)(2,1)S(1)}) custom-call(f32[48,2048]{1,0:T(8,128)S(1)} %get-tuple-element.25.own_ref, f32[80,2176]{1,0:T(8,128)S(1)} %get-tuple-element.35.sum_ref, ...), custom_call_target="tpu_custom_call" | custom-call | flops 1000000000 | bytes 1048576 | tf_op jit(solution)/shard_map/pallas_call | solution.py:646
  33.8 0.1 collective-permute-start.8
  33.8 0.1 collective-permute-start.7
  33.9 0.1 collective-permute-start.9
  34.0 0.8 %shard_map.136 = f32[3,4,4,2048]{3,2,1,0:T(4,128)} custom-call(f32[48,2048]{1,0:T(8,128)S(1)} %get-tuple-element.43.rows_ref), custom_call_target="tpu_custom_call" | custom-call | flops 20000000000 | bytes 1048576 | tf_op jit(solution)/shard_map/pallas_call | solution.py:658
  34.8 7.7 %collective-permute-done.8.corner_ref = bf16[3,1,2048]{2,1,0:T(2,128)(2,1)S(1)} collective-permute-done((bf16[3,1,2048]{2,1,0:T(2,128)(2,1)S(1)}, bf16[3,1,2048]{2,1,0:T(2,128)(2,1)S(1)}, u32[]{:S(2)}, u32[]{:S(2)}) %collective-permute-start.8) | collective-permute-done | bytes 12320 | tf_op jit(solution)/shard_map/ppermute | solution.py:564
  42.5 0.0 collective-permute-done.7.col_ref
  42.5 0.0 collective-permute-done.9.row_ref
  42.5 0.9 %shard_map.137 = f32[3,4,4,2048]{3,2,1,0:T(4,128)} custom-call(f32[3,4,4,2048]{3,2,1,0:T(4,128)S(1)} %get-tuple-element.44.sum_ref, bf16[3,4,2048]{2,1,0:T(4,128)(2,1)S(1)} %collective-permute-done.7.col_ref, bf16[3,1,2048]{2,1,0:T(2,128)(2,1)S(1)} %collective-permute-done.8.corner_ref, bf16[3,4,2048]{2,1,0:T(4,128)(2,1)S(1)} %collective-permute-done.9.row_ref), custom_call_target="tpu_custom_call" | custom-call | bytes 1048576 | tf_op jit(solution)/shard_map/pallas_call | solution.py:659
  (8 shorter events, 0.0 us)
Async XLA Ops:
  0.6 9.2 %copy-start.2 = (f32[3,4,4,2048]{3,2,1,0:T(4,128)S(1)}, f32[3,4,4,2048]{3,2,1,0:T(4,128)}, u32[]{:S(2)}) copy-start(f32[3,4,4,2048]{3,2,1,0:T(4,128)} %disp_hbm.1) | copy-start | bytes 1179652
  0.6 9.2 %copy-start.5 = (f32[1,5,1,5,2048]{4,2,3,1,0:T(1,128)S(1)}, f32[1,5,1,5,2048]{4,2,3,1,0:T(1,128)}, u32[]{:S(2)}) copy-start(f32[1,5,1,5,2048]{4,2,3,1,0:T(1,128)} %param.20) | copy-start | bytes 614404
  0.7 9.2 %copy-start.4 = (f32[1,5,1,5,2048]{4,2,3,1,0:T(1,128)S(1)}, f32[1,5,1,5,2048]{4,2,3,1,0:T(1,128)}, u32[]{:S(2)}) copy-start(f32[1,5,1,5,2048]{4,2,3,1,0:T(1,128)} %param.19) | copy-start | bytes 614404
  0.7 9.2 %copy-start.3 = (f32[3,4,4,2048]{3,2,1,0:T(4,128)S(1)}, f32[3,4,4,2048]{3,2,1,0:T(4,128)}, u32[]{:S(2)}) copy-start(f32[3,4,4,2048]{3,2,1,0:T(4,128)} %prev_ref.1) | copy-start | bytes 1179652
  0.7 9.2 %copy-start.9 = (s32[4,4]{1,0:T(4,128)S(1)}, s32[4,4]{1,0:T(4,128)}, u32[]{:S(2)}) copy-start(s32[4,4]{1,0:T(4,128)} %blocks_hbm.1) | copy-start | bytes 196
  0.7 9.2 %copy-start.10 = (f32[4,4]{1,0:T(4,128)S(1)}, f32[4,4]{1,0:T(4,128)}, u32[]{:S(2)}) copy-start(f32[4,4]{1,0:T(4,128)} %mass_hbm.1) | copy-start | bytes 196
  2.5 10.6 %collective-permute-start.1 = (bf16[3,1,2176]{2,1,0:T(2,128)(2,1)}, bf16[3,1,2176]{2,1,0:T(2,128)(2,1)S(1)}, u32[]{:S(2)}, u32[]{:S(2)}) collective-permute-start(bf16[3,1,2176]{2,1,0:T(2,128)(2,1)} %get-tuple-element.29), channel_id=1, source_target_pairs={{0,63},{1,120},{2,121},{3,122},{4,123},{5,124},{6,125},{7,126},{8,... | collective-permute-start | bytes 39176 | tf_op jit(solution)/shard_map/ppermute | solution.py:564
  8.4 4.7 %collective-permute-start = (bf16[3,4,2176]{2,1,0:T(4,128)(2,1)}, bf16[3,4,2176]{2,1,0:T(4,128)(2,1)S(1)}, u32[]{:S(2)}, u32[]{:S(2)}) collective-permute-start(bf16[3,4,2176]{2,1,0:T(4,128)(2,1)} %get-tuple-element.28), channel_id=1, source_target_pairs={{0,71},{1,0},{2,1},{3,2},{4,3},{5,4},{6,5},{7,6},{8,79},{9,8},{10,... | collective-permute-start | bytes 156680 | tf_op jit(solution)/shard_map/ppermute | solution.py:564
  9.7 3.4 %collective-permute-start.2 = (bf16[3,4,2176]{2,1,0:T(4,128)(2,1)}, bf16[3,4,2176]{2,1,0:T(4,128)(2,1)S(1)}, u32[]{:S(2)}, u32[]{:S(2)}) collective-permute-start(bf16[3,4,2176]{2,1,0:T(4,128)(2,1)} %get-tuple-element.30), channel_id=1, source_target_pairs={{0,120},{1,121},{2,122},{3,123},{4,124},{5,125},{6,126},{7,127},{8... | collective-permute-start | bytes 156680 | tf_op jit(solution)/shard_map/ppermute | solution.py:564
  9.8 0.7 %copy-start.7 = (f32[2,1,5,1,5]{4,3,2,1,0:T(1,128)S(1)}, f32[2,1,5,1,5]{4,3,2,1,0:T(1,128)}, u32[]{:S(2)}) copy-start(f32[2,1,5,1,5]{4,3,2,1,0:T(1,128)} %param.17) | copy-start | bytes 604
  9.8 0.7 %copy-start.6 = (f32[2,1,5,1,5]{4,3,2,1,0:T(1,128)S(1)}, f32[2,1,5,1,5]{4,3,2,1,0:T(1,128)}, u32[]{:S(2)}) copy-start(f32[2,1,5,1,5]{4,3,2,1,0:T(1,128)} %param.16) | copy-start | bytes 604
  9.8 0.7 %copy-start.8 = (f32[1,5,1,5]{3,2,1,0:T(1,128)S(1)}, f32[1,5,1,5]{3,2,1,0:T(1,128)}, u32[]{:S(2)}) copy-start(f32[1,5,1,5]{3,2,1,0:T(1,128)} %param.18) | copy-start | bytes 304
  10.5 1.2 %copy-start.11 = (f32[1016,256]{1,0:T(8,128)S(1)}, f32[1016,256]{1,0:T(8,128)}, u32[]{:S(2)}) copy-start(f32[1016,256]{1,0:T(8,128)} %constant.53.clone.packed_ref) | copy-start | bytes 3121156
  11.8 1.4 %copy-start = (bf16[16,128,256]{2,1,0:T(8,128)(2,1)S(1)}, bf16[16,128,256]{2,1,0:T(8,128)(2,1)}, u32[]{:S(2)}) copy-start(bf16[16,128,256]{2,1,0:T(8,128)(2,1)} %constant.55.clone.tback_ref) | copy-start | bytes 3145732
  11.8 1.5 %copy-start.1 = (bf16[16,256,128]{2,1,0:T(8,128)(2,1)S(1)}, bf16[16,256,128]{2,1,0:T(8,128)(2,1)}, u32[]{:S(2)}) copy-start(bf16[16,256,128]{2,1,0:T(8,128)(2,1)} %constant.54.clone.table_ref) | copy-start | bytes 3145732
  16.7 5.9 %collective-permute-start.3 = (bf16[16,2048]{1,0:T(8,128)(2,1)S(1)}, bf16[16,2048]{1,0:T(8,128)(2,1)S(1)}, u32[]{:S(2)}, u32[]{:S(2)}) collective-permute-start(bf16[16,2048]{1,0:T(8,128)(2,1)S(1)} %get-tuple-element.36), channel_id=1, source_target_pairs={{0,1},{1,0},{2,3},{3,2},{4,5},{5,4},{6,7},{7,6},{8,16},{9,17},{10,... | collective-permute-start | bytes 196616 | tf_op jit(solution)/shard_map/ppermute | solution.py:578
  19.9 2.7 %collective-permute-start.4 = (bf16[16,2048]{1,0:T(8,128)(2,1)S(1)}, bf16[16,2048]{1,0:T(8,128)(2,1)S(1)}, u32[]{:S(2)}, u32[]{:S(2)}) collective-permute-start(bf16[16,2048]{1,0:T(8,128)(2,1)S(1)} %get-tuple-element.37), channel_id=1, source_target_pairs={{0,8},{1,9},{2,10},{3,11},{4,12},{5,13},{6,14},{7,15},{8,0},{9,1},... | collective-permute-start | bytes 196616 | tf_op jit(solution)/shard_map/ppermute | solution.py:578
  22.7 8.0 %collective-permute-start.5 = (bf16[16,2048]{1,0:T(8,128)(2,1)S(1)}, bf16[16,2048]{1,0:T(8,128)(2,1)S(1)}, u32[]{:S(2)}, u32[]{:S(2)}) collective-permute-start(bf16[16,2048]{1,0:T(8,128)(2,1)S(1)} %get-tuple-element.40), channel_id=1, source_target_pairs={{0,8},{1,2},{2,1},{3,4},{4,3},{5,6},{6,5},{7,15},{8,0},{9,10},{10,... | collective-permute-start | bytes 196616 | tf_op jit(solution)/shard_map/ppermute | solution.py:578
  27.2 4.3 %collective-permute-start.6 = (bf16[16,2048]{1,0:T(8,128)(2,1)S(1)}, bf16[16,2048]{1,0:T(8,128)(2,1)S(1)}, u32[]{:S(2)}, u32[]{:S(2)}) collective-permute-start(bf16[16,2048]{1,0:T(8,128)(2,1)S(1)} %get-tuple-element.41), channel_id=1, source_target_pairs={{0,1},{1,0},{2,3},{3,2},{4,5},{5,4},{6,7},{7,6},{8,9},{9,8},{10,11... | collective-permute-start | bytes 196616 | tf_op jit(solution)/shard_map/ppermute | solution.py:578
  33.8 8.8 %collective-permute-start.8 = (bf16[3,1,2048]{2,1,0:T(2,128)(2,1)S(1)}, bf16[3,1,2048]{2,1,0:T(2,128)(2,1)S(1)}, u32[]{:S(2)}, u32[]{:S(2)}) collective-permute-start(bf16[3,1,2048]{2,1,0:T(2,128)(2,1)S(1)} %get-tuple-element.46), channel_id=1, source_target_pairs={{0,9},{1,10},{2,11},{3,12},{4,13},{5,14},{6,15},{7,72},{8,17},{9,1... | collective-permute-start | bytes 36872 | tf_op jit(solution)/shard_map/ppermute | solution.py:564
  33.8 8.7 %collective-permute-start.7 = (bf16[3,4,2048]{2,1,0:T(4,128)(2,1)S(1)}, bf16[3,4,2048]{2,1,0:T(4,128)(2,1)S(1)}, u32[]{:S(2)}, u32[]{:S(2)}) collective-permute-start(bf16[3,4,2048]{2,1,0:T(4,128)(2,1)S(1)} %get-tuple-element.45), channel_id=1, source_target_pairs={{0,1},{1,2},{2,3},{3,4},{4,5},{5,6},{6,7},{7,64},{8,9},{9,10},{10,... | collective-permute-start | bytes 147464 | tf_op jit(solution)/shard_map/ppermute | solution.py:564
  33.9 8.6 %collective-permute-start.9 = (bf16[3,4,2048]{2,1,0:T(4,128)(2,1)S(1)}, bf16[3,4,2048]{2,1,0:T(4,128)(2,1)S(1)}, u32[]{:S(2)}, u32[]{:S(2)}) collective-permute-start(bf16[3,4,2048]{2,1,0:T(4,128)(2,1)S(1)} %get-tuple-element.47), channel_id=1, source_target_pairs={{0,8},{1,9},{2,10},{3,11},{4,12},{5,13},{6,14},{7,15},{8,16},{9,17... | collective-permute-start | bytes 147464 | tf_op jit(solution)/shard_map/ppermute | solution.py:564

commit v6 on v5

--- a/solution.py
+++ b/solution.py
@@ -244,13 +244,14 @@
     ]
     for load in loads:
         load.start()
-    for load in loads:
-        load.wait()
     faces = (
         (row_out, [(0, n) for n in range(4)]),
         (col_out, [(n, 0) for n in range(4)]),
         (corner_out, [(0, 0)]),
     )
+    loads[0].wait()
+    loads[1].wait()
+    columns = []
     for out, rows in faces:
         live = node_column(lambda at: blocks_ref[at[0], at[1]].astype(F32), rows)
         mass = node_column(lambda at: mass_ref[at[0], at[1]], rows)
@@ -258,16 +259,40 @@
         lane = lax.broadcasted_iota(jnp.int32, (len(rows), LANES), 1)
         info = jnp.where(lane == 0, high, jnp.where(lane == 1, mass - high, jnp.where(lane == 2, live, 0.0)))
         for c in range(3):
-            for index in range(8):
-                lanes = slice(256 * index, 256 * (index + 1))
+            out[c, :, WIDTH:] = info.astype(BF16)
+        columns.append(live)
+    loads[2].wait()
+    for (out, rows), live in zip(faces, columns):
+        for index in range(8):
+            lanes = slice(256 * index, 256 * (index + 1))
+            kept = live > index
+            for c in range(3):
                 if out is row_out:
                     value = disp_ref[c, 0, :, lanes]
                 elif out is col_out:
                     value = jnp.concatenate([disp_ref[c, n, 0:1, lanes] for n in range(4)], axis=0)
                 else:
                     value = disp_ref[c, 0, 0:1, lanes]
-                out[c, :, lanes] = jnp.where(live > index, value, 0.0).astype(BF16)
-            out[c, :, WIDTH:] = info.astype(BF16)
+                out[c, :, lanes] = jnp.where(kept, value, 0.0).astype(BF16)
+
+
+def own_kernel(place_ref, blocks_ref, mass_ref, disp_ref, prev_ref, own_out, free_out, info_out):
+    def column(ref):
+        shape = (4, 4)
+        diagonal = lax.broadcasted_iota(jnp.int32, shape, 0) == lax.broadcasted_iota(jnp.int32, shape, 1)
+        value = ref[...].astype(F32)
+        pieces = [jnp.sum(jnp.where(diagonal, value[i : i + 1], 0.0), axis=1, keepdims=True) for i in range(4)]
+        return jnp.concatenate(pieces * 3, axis=0)
+
+    live, mass = column(blocks_ref), column(mass_ref)
+    lane = lax.broadcasted_iota(jnp.int32, (OWN, LANES), 1)
+    info_out[:OWN] = jnp.where(lane == 0, mass, jnp.where(lane == 1, live, 0.0))
+    info_out[OWN:] = place_ref[...]
+    for index in range(8):
+        lanes = slice(256 * index, 256 * (index + 1))
+        value = jnp.where(live > index, own_rows(disp_ref, lanes), 0.0)
+        own_out[:, lanes] = value
+        free_out[:, lanes] = jnp.where(live > index, 2.0 * value - own_rows(prev_ref, lanes), 0.0)
 
 
 def exact_dot(left, right):
@@ -298,9 +323,8 @@
 
 
 def prepare_kernel(
-    starts, place_ref, blocks_ref, mass_ref, disp_ref, prev_ref, diag_ref, off_ref, radius_ref, lambda_ref, mu_ref,
-    packed_ref,
-    operator_out, back_out, material_out, own_out, free_out, info_out, outgoing_out, column_out, arrival_out,
+    starts, place_ref, diag_ref, off_ref, radius_ref, lambda_ref, mu_ref, packed_ref,
+    operator_out, back_out, material_out, outgoing_out, column_out, arrival_out,
     shuffled,
 ):
     def constant(name, rows, columns, index=0):
@@ -319,23 +343,6 @@
     operator = operator + jnp.concatenate([plain, jnp.zeros_like(plain)], axis=1)
     operator_out[...] = operator.astype(BF16)
     back_out[...] = operator.T.astype(BF16)
-
-    def column(ref):
-        shape = (4, 4)
-        diagonal = lax.broadcasted_iota(jnp.int32, shape, 0) == lax.broadcasted_iota(jnp.int32, shape, 1)
-        value = ref[...].astype(F32)
-        pieces = [jnp.sum(jnp.where(diagonal, value[i : i + 1], 0.0), axis=1, keepdims=True) for i in range(4)]
-        return jnp.concatenate(pieces * 3, axis=0)
-
-    live, mass = column(blocks_ref), column(mass_ref)
-    lane = lax.broadcasted_iota(jnp.int32, (OWN, LANES), 1)
-    info_out[:OWN] = jnp.where(lane == 0, mass, jnp.where(lane == 1, live, 0.0))
-    info_out[OWN:] = place_ref[...]
-    for index in range(8):
-        lanes = slice(256 * index, 256 * (index + 1))
-        value = jnp.where(live > index, own_rows(disp_ref, lanes), 0.0)
-        own_out[:, lanes] = value
-        free_out[:, lanes] = jnp.where(live > index, 2.0 * value - own_rows(prev_ref, lanes), 0.0)
 
     def packed(name, rows, columns, *bits):
         pieces = [constant(name, rows, columns, index) for index in range(2 ** len(bits))]
@@ -456,13 +463,15 @@
             value = mass * value
             sum_ref[:OWN, lanes] = free_ref[:, lanes] + value[:OWN]
             sum_ref[OWN:, lanes] = value[OWN:]
+
+    forces(nodes, operator_ref, back_ref, table_ref, tback_ref, material_ref, both, strain, spectrum, emit)
+
+    for index in range(8):
         lanes = slice(256 * index, 256 * (index + 1))
         sent = dot(select_ref[...], sum_ref[:, lanes].astype(BF16)).astype(BF16)
         pair_ref[:, lanes] = sent[:16]
         side_ref[:, lanes] = sent[16:32]
         faces_ref[:, lanes] = sent[32:]
-
-    forces(nodes, operator_ref, back_ref, table_ref, tback_ref, material_ref, both, strain, spectrum, emit)
 
 
 def column_kernel(faces_ref, side_ref, pair_ref, select_ref, side_out, pair_out):
@@ -603,23 +612,25 @@
         corner = shifted(corner, -1, -1)
         row = shifted(row, -1, 0)
 
-        operator, back, material, own, free, info, outgoing, column, arrival = call(
+        own, free, info = call(
+            own_kernel,
+            (shape(OWN, WIDTH), shape(OWN, WIDTH), shape(OWN + 8, LANES)),
+            inputs=5, flops=2 * 10**10, vmem=8 * 1024 * 1024,
+        )(place, node_blocks, inverse_mass, displacement, previous)
+        operator, back, material, outgoing, column, arrival = call(
             functools.partial(prepare_kernel, starts),
             (
                 shape(STRAINS, 2 * NODES, dtype=BF16),
                 shape(2 * NODES, STRAINS, dtype=BF16),
                 shape(RADIX, 56, LANES),
-                shape(OWN, WIDTH),
-                shape(OWN, WIDTH),
-                shape(OWN + 8, LANES),
                 shape(64, NODES, dtype=BF16),
                 shape(32, 64, dtype=BF16),
                 shape(NODES, 64, dtype=BF16),
             ),
             [pltpu.VMEM((2, 400, LANES), F32)],
-            inputs=11, flops=10**9,
+            inputs=7, flops=10**9, vmem=8 * 1024 * 1024,
         )(
-            place, node_blocks, inverse_mass, displacement, previous,
+            place,
             jac_diag.reshape(10, 1, 5), jac_off.reshape(10, 1, 5), inv_radius.reshape(5, 1, 5),
             lame_l.reshape(400, LANES), lame_m.reshape(400, LANES), jnp.asarray(packed),
         )

time: 43.6 us -> 42.4 us (0.972)
  Pallas kernels: 10.6 us -> 9.77 us
    pallas_call x1, Pallas kernels: 3.36 us -> 2.27 us  [per_device(): call(step_one_kernel, (shape(NODES, WIDTH + LANES), tile, tile, shape(32,...]
  transfers between devices with their start and end apart: 10 -> 10, of which waited for: 4 -> 4; matrix products, arithmetic and copies ran while one was open for 0% -> 0% of each run, Pallas kernels for 5% -> 6%
where the time goes in v6:
time: 42.4 us; the launch traced here: 42.3 us
  waiting for transfers between devices  14.9 us (35%)
  starting transfers between devices  14.7 us (35%)
  Pallas kernels  9.77 us (23%)
  local copies, waits for them, and re-layouts  1.99 us (5%)
  between operations  0.86 us (2%)
    ppermute x6, waiting for transfers between devices, shifted(): return lax.ppermute(array, ('colat', 'depth'), pairs)  7.74 us
    ppermute x6, starting transfers between devices, shifted(): return lax.ppermute(array, ('colat', 'depth'), pairs)  7.44 us
    ppermute x4, starting transfers between devices, swapped(): return lax.ppermute(array, ('colat', 'depth'), pairs)  7.3 us
    ppermute x4, waiting for transfers between devices, swapped(): return lax.ppermute(array, ('colat', 'depth'), pairs)  7.12 us
    pallas_call x1, Pallas kernels, per_device(): call(step_two_kernel, (shape(OWN, WIDTH), shape(3, 4, 4, WIDTH), row_face...  2.28 us
    pallas_call x1, Pallas kernels, per_device(): call(step_one_kernel, (shape(NODES, WIDTH + LANES), tile, tile, shape(32,...  2.27 us
    unnamed x24, local copies, waits for them, and re-layouts  1.99 us
    pallas_call x1, Pallas kernels, per_device(): call(first_kernel, (row_face, row_face, point), [pltpu.SMEM((4, 4), jnp.i...  1.81 us
  transfers between devices with their start and end apart: 10, of which 4 were waited for; matrix products, arithmetic and copies ran while one was open for 0% of the time, Pallas kernels for 6%

profile of v6, /device:TPU:6, one launch (start us, length us, event | category | flops | bytes accessed | tf_op | source)
XLA Modules:
  0.0 42.3 jit_solution(6576954330083467212)
XLA Ops:
  0.6 0.0 copy-start.2
  0.6 0.0 copy-start.3
  0.6 1.8 %shard_map.132 = (bf16[3,4,2176]{2,1,0:T(4,128)(2,1)}, bf16[3,4,2176]{2,1,0:T(4,128)(2,1)}, bf16[3,1,2176]{2,1,0:T(2,128)(2,1)}) custom-call(s32[4,4]{1,0:T(4,128)} %blocks_hbm.1, f32[4,4]{1,0:T(4,128)} %mass_hbm.1, f32[3,4,4,2048]{3,2,1,0:T(4,128)} %disp_hbm.1), custom_call_target="tpu_custom_call" | custom-call | flops 20000000000 | bytes 1048576 | tf_op jit(solution)/shard_map/pallas_call | solution.py:600
  2.5 5.9 %collective-permute-start.1 = (bf16[3,1,2176]{2,1,0:T(2,128)(2,1)}, bf16[3,1,2176]{2,1,0:T(2,128)(2,1)S(1)}, u32[]{:S(2)}, u32[]{:S(2)}) collective-permute-start(bf16[3,1,2176]{2,1,0:T(2,128)(2,1)} %get-tuple-element.29), channel_id=1, source_target_pairs={{0,63},{1,120},{2,121},{3,122},{4,123},{5,124},{6,125},{7,126},{8,... | collective-permute-start | bytes 39176 | tf_op jit(solution)/shard_map/ppermute | solution.py:573
  8.4 1.3 %collective-permute-start = (bf16[3,4,2176]{2,1,0:T(4,128)(2,1)}, bf16[3,4,2176]{2,1,0:T(4,128)(2,1)S(1)}, u32[]{:S(2)}, u32[]{:S(2)}) collective-permute-start(bf16[3,4,2176]{2,1,0:T(4,128)(2,1)} %get-tuple-element.28), channel_id=1, source_target_pairs={{0,71},{1,0},{2,1},{3,2},{4,3},{5,4},{6,5},{7,6},{8,79},{9,8},{10,... | collective-permute-start | bytes 156680 | tf_op jit(solution)/shard_map/ppermute | solution.py:573
  9.7 0.0 collective-permute-start.2
  9.7 0.0 copy-start.9
  9.8 0.0 copy-start.10
  9.8 0.0 copy-done.2
  9.8 0.0 copy-done.3
  9.8 0.6 %copy-done.9 = s32[4,4]{1,0:T(4,128)S(1)} copy-done((s32[4,4]{1,0:T(4,128)S(1)}, s32[4,4]{1,0:T(4,128)}, u32[]{:S(2)}) %copy-start.9) | copy-done | bytes 88
  10.4 0.0 copy-done.10
  10.4 0.0 copy-start.4
  10.5 0.0 copy-start.5
  10.5 0.2 shard_map.131
  10.7 0.0 copy-start.6
  10.7 0.0 copy-start.8
  10.7 0.7 %copy-done.4 = f32[1,5,1,5,2048]{4,2,3,1,0:T(1,128)S(1)} copy-done((f32[1,5,1,5,2048]{4,2,3,1,0:T(1,128)S(1)}, f32[1,5,1,5,2048]{4,2,3,1,0:T(1,128)}, u32[]{:S(2)}) %copy-start.4) | copy-done | bytes 204824
  11.4 0.1 copy-done.5
  11.5 0.0 copy-done.7
  11.5 0.4 %copy-done.11 = f32[1016,256]{1,0:T(8,128)S(1)} copy-done((f32[1016,256]{1,0:T(8,128)S(1)}, f32[1016,256]{1,0:T(8,128)}, u32[]{:S(2)}) %copy-start.11) | copy-done | bytes 1040408
  11.9 0.0 copy-done.6
  11.9 0.0 copy-done.8
  11.9 1.3 %shard_map.133 = (bf16[152,160]{1,0:T(8,128)(2,1)S(1)}, bf16[160,152]{1,0:T(8,128)(2,1)S(1)}, f32[16,56,128]{2,1,0:T(8,128)S(1)}, bf16[64,80]{1,0:T(8,128)(2,1)S...) custom-call(f32[8,128]{1,0:T(8,128)S(1)} %select_select_fusion.place_ref, f32[10,1,5]{2,1,0:T(1,128)S(1)} %bitcast.7, ...), custom_call_target="tpu_custom_call" | custom-call | flops 1000000000 | bytes 1048576 | tf_op jit(solution)/shard_map/pallas_call | solution.py:620
  13.3 0.0 collective-permute-done.1.corner_ref
  13.3 0.0 collective-permute-done.col_ref
  13.3 0.0 collective-permute-done.2.row_ref
  13.3 0.0 copy-done
  13.3 0.1 copy-done.1
  13.5 2.3 %shard_map.134 = (f32[80,2176]{1,0:T(8,128)S(1)}, bf16[16,2048]{1,0:T(8,128)(2,1)S(1)}, bf16[16,2048]{1,0:T(8,128)(2,1)S(1)}, bf16[32,2048]{1,0:T(8,128)(2,1)S(1)}) custom-call(f32[48,2048]{1,0:T(8,128)S(1)} %get-tuple-element.25.own_ref, f32[48,2048]{1,0:T(8,128)S(1)} %get-tuple-element.26.free_ref, f32[56,128]{1,0:T(8,128)S(1)} %get-tuple-element.27.info_ref, ...), custom_call_target="tpu_custom_call" | custom-call | flops 1000000000 | bytes 1048576 | tf_op jit(solution)/shard_map/pallas_call | solution.py:645
  15.7 3.0 %collective-permute-start.3 = (bf16[16,2048]{1,0:T(8,128)(2,1)S(1)}, bf16[16,2048]{1,0:T(8,128)(2,1)S(1)}, u32[]{:S(2)}, u32[]{:S(2)}) collective-permute-start(bf16[16,2048]{1,0:T(8,128)(2,1)S(1)} %get-tuple-element.36), channel_id=1, source_target_pairs={{0,1},{1,0},{2,3},{3,2},{4,5},{5,4},{6,7},{7,6},{8,16},{9,17},{10,... | collective-permute-start | bytes 196616 | tf_op jit(solution)/shard_map/ppermute | solution.py:587
  18.8 0.0 collective-permute-start.4
  18.8 2.9 %collective-permute-done.3.side_ref.cside_ref = bf16[16,2048]{1,0:T(8,128)(2,1)S(1)} collective-permute-done((bf16[16,2048]{1,0:T(8,128)(2,1)S(1)}, bf16[16,2048]{1,0:T(8,128)(2,1)S(1)}, u32[]{:S(2)}, u32[]{:S(2)}) %collective-permute-start.3) | collective-permute-done | bytes 65568 | tf_op jit(solution)/shard_map/ppermute | solution.py:587
  21.6 0.0 collective-permute-done.4.pair_ref.cpair_ref
  21.6 0.2 shard_map.135
  21.8 4.3 %collective-permute-start.5 = (bf16[16,2048]{1,0:T(8,128)(2,1)S(1)}, bf16[16,2048]{1,0:T(8,128)(2,1)S(1)}, u32[]{:S(2)}, u32[]{:S(2)}) collective-permute-start(bf16[16,2048]{1,0:T(8,128)(2,1)S(1)} %get-tuple-element.40), channel_id=1, source_target_pairs={{0,8},{1,2},{2,1},{3,4},{4,3},{5,6},{6,5},{7,15},{8,0},{9,10},{10,... | collective-permute-start | bytes 196616 | tf_op jit(solution)/shard_map/ppermute | solution.py:587
  26.1 0.0 collective-permute-start.6
  26.1 3.7 %collective-permute-done.5.dside_ref = bf16[16,2048]{1,0:T(8,128)(2,1)S(1)} collective-permute-done((bf16[16,2048]{1,0:T(8,128)(2,1)S(1)}, bf16[16,2048]{1,0:T(8,128)(2,1)S(1)}, u32[]{:S(2)}, u32[]{:S(2)}) %collective-permute-start.5) | collective-permute-done | bytes 65568 | tf_op jit(solution)/shard_map/ppermute | solution.py:587
  29.7 0.6 %collective-permute-done.6.dpair_ref = bf16[16,2048]{1,0:T(8,128)(2,1)S(1)} collective-permute-done((bf16[16,2048]{1,0:T(8,128)(2,1)S(1)}, bf16[16,2048]{1,0:T(8,128)(2,1)S(1)}, u32[]{:S(2)}, u32[]{:S(2)}) %collective-permute-start.6) | collective-permute-done | bytes 65568 | tf_op jit(solution)/shard_map/ppermute | solution.py:587
  30.3 2.3 %shard_map.136 = (f32[48,2048]{1,0:T(8,128)S(1)}, f32[3,4,4,2048]{3,2,1,0:T(4,128)S(1)}, bf16[3,4,2048]{2,1,0:T(4,128)(2,1)S(1)}, bf16[3,4,2048]{2,1,0:T(4,128)(2,1)S(1)}, bf16[3,1,2048]{2,1,0:T(2,128)(2,1)S(1)}) custom-call(f32[48,2048]{1,0:T(8,128)S(1)} %get-tuple-element.25.own_ref, f32[80,2176]{1,0:T(8,128)S(1)} %get-tuple-element.35.sum_ref, ...), custom_call_target="tpu_custom_call" | custom-call | flops 1000000000 | bytes 1048576 | tf_op jit(solution)/shard_map/pallas_call | solution.py:657
  32.6 0.1 collective-permute-start.8
  32.7 0.1 collective-permute-start.7
  32.8 0.1 collective-permute-start.9
  32.9 0.8 %shard_map.137 = f32[3,4,4,2048]{3,2,1,0:T(4,128)} custom-call(f32[48,2048]{1,0:T(8,128)S(1)} %get-tuple-element.43.rows_ref), custom_call_target="tpu_custom_call" | custom-call | flops 20000000000 | bytes 1048576 | tf_op jit(solution)/shard_map/pallas_call | solution.py:669
  33.6 7.7 %collective-permute-done.8.corner_ref = bf16[3,1,2048]{2,1,0:T(2,128)(2,1)S(1)} collective-permute-done((bf16[3,1,2048]{2,1,0:T(2,128)(2,1)S(1)}, bf16[3,1,2048]{2,1,0:T(2,128)(2,1)S(1)}, u32[]{:S(2)}, u32[]{:S(2)}) %collective-permute-start.8) | collective-permute-done | bytes 12320 | tf_op jit(solution)/shard_map/ppermute | solution.py:573
  41.4 0.0 collective-permute-done.7.col_ref
  41.4 0.0 collective-permute-done.9.row_ref
  41.4 0.9 %shard_map.138 = f32[3,4,4,2048]{3,2,1,0:T(4,128)} custom-call(f32[3,4,4,2048]{3,2,1,0:T(4,128)S(1)} %get-tuple-element.44.sum_ref, bf16[3,4,2048]{2,1,0:T(4,128)(2,1)S(1)} %collective-permute-done.7.col_ref, bf16[3,1,2048]{2,1,0:T(2,128)(2,1)S(1)} %collective-permute-done.8.corner_ref, bf16[3,4,2048]{2,1,0:T(4,128)(2,1)S(1)} %collective-permute-done.9.row_ref), custom_call_target="tpu_custom_call" | custom-call | bytes 1048576 | tf_op jit(solution)/shard_map/pallas_call | solution.py:670
  (9 shorter events, 0.0 us)
Async XLA Ops:
  0.6 9.2 %copy-start.2 = (f32[3,4,4,2048]{3,2,1,0:T(4,128)S(1)}, f32[3,4,4,2048]{3,2,1,0:T(4,128)}, u32[]{:S(2)}) copy-start(f32[3,4,4,2048]{3,2,1,0:T(4,128)} %disp_hbm.1) | copy-start | bytes 1179652
  0.6 9.2 %copy-start.3 = (f32[3,4,4,2048]{3,2,1,0:T(4,128)S(1)}, f32[3,4,4,2048]{3,2,1,0:T(4,128)}, u32[]{:S(2)}) copy-start(f32[3,4,4,2048]{3,2,1,0:T(4,128)} %prev_ref.1) | copy-start | bytes 1179652
  2.5 10.8 %collective-permute-start.1 = (bf16[3,1,2176]{2,1,0:T(2,128)(2,1)}, bf16[3,1,2176]{2,1,0:T(2,128)(2,1)S(1)}, u32[]{:S(2)}, u32[]{:S(2)}) collective-permute-start(bf16[3,1,2176]{2,1,0:T(2,128)(2,1)} %get-tuple-element.29), channel_id=1, source_target_pairs={{0,63},{1,120},{2,121},{3,122},{4,123},{5,124},{6,125},{7,126},{8,... | collective-permute-start | bytes 39176 | tf_op jit(solution)/shard_map/ppermute | solution.py:573
  8.4 4.9 %collective-permute-start = (bf16[3,4,2176]{2,1,0:T(4,128)(2,1)}, bf16[3,4,2176]{2,1,0:T(4,128)(2,1)S(1)}, u32[]{:S(2)}, u32[]{:S(2)}) collective-permute-start(bf16[3,4,2176]{2,1,0:T(4,128)(2,1)} %get-tuple-element.28), channel_id=1, source_target_pairs={{0,71},{1,0},{2,1},{3,2},{4,3},{5,4},{6,5},{7,6},{8,79},{9,8},{10,... | collective-permute-start | bytes 156680 | tf_op jit(solution)/shard_map/ppermute | solution.py:573
  9.7 3.6 %collective-permute-start.2 = (bf16[3,4,2176]{2,1,0:T(4,128)(2,1)}, bf16[3,4,2176]{2,1,0:T(4,128)(2,1)S(1)}, u32[]{:S(2)}, u32[]{:S(2)}) collective-permute-start(bf16[3,4,2176]{2,1,0:T(4,128)(2,1)} %get-tuple-element.30), channel_id=1, source_target_pairs={{0,120},{1,121},{2,122},{3,123},{4,124},{5,125},{6,126},{7,127},{8... | collective-permute-start | bytes 156680 | tf_op jit(solution)/shard_map/ppermute | solution.py:573
  9.7 0.7 %copy-start.9 = (s32[4,4]{1,0:T(4,128)S(1)}, s32[4,4]{1,0:T(4,128)}, u32[]{:S(2)}) copy-start(s32[4,4]{1,0:T(4,128)} %blocks_hbm.1) | copy-start | bytes 196
  9.8 0.7 %copy-start.10 = (f32[4,4]{1,0:T(4,128)S(1)}, f32[4,4]{1,0:T(4,128)}, u32[]{:S(2)}) copy-start(f32[4,4]{1,0:T(4,128)} %mass_hbm.1) | copy-start | bytes 196
  10.4 0.9 %copy-start.4 = (f32[1,5,1,5,2048]{4,2,3,1,0:T(1,128)S(1)}, f32[1,5,1,5,2048]{4,2,3,1,0:T(1,128)}, u32[]{:S(2)}) copy-start(f32[1,5,1,5,2048]{4,2,3,1,0:T(1,128)} %param.19) | copy-start | bytes 614404
  10.5 1.0 %copy-start.5 = (f32[1,5,1,5,2048]{4,2,3,1,0:T(1,128)S(1)}, f32[1,5,1,5,2048]{4,2,3,1,0:T(1,128)}, u32[]{:S(2)}) copy-start(f32[1,5,1,5,2048]{4,2,3,1,0:T(1,128)} %param.20) | copy-start | bytes 614404
  10.5 1.0 %copy-start.7 = (f32[2,1,5,1,5]{4,3,2,1,0:T(1,128)S(1)}, f32[2,1,5,1,5]{4,3,2,1,0:T(1,128)}, u32[]{:S(2)}) copy-start(f32[2,1,5,1,5]{4,3,2,1,0:T(1,128)} %param.17) | copy-start | bytes 604
  10.5 1.4 %copy-start.11 = (f32[1016,256]{1,0:T(8,128)S(1)}, f32[1016,256]{1,0:T(8,128)}, u32[]{:S(2)}) copy-start(f32[1016,256]{1,0:T(8,128)} %constant.53.clone.packed_ref) | copy-start | bytes 3121156
  10.7 1.2 %copy-start.6 = (f32[2,1,5,1,5]{4,3,2,1,0:T(1,128)S(1)}, f32[2,1,5,1,5]{4,3,2,1,0:T(1,128)}, u32[]{:S(2)}) copy-start(f32[2,1,5,1,5]{4,3,2,1,0:T(1,128)} %param.16) | copy-start | bytes 604
  10.7 1.2 %copy-start.8 = (f32[1,5,1,5]{3,2,1,0:T(1,128)S(1)}, f32[1,5,1,5]{3,2,1,0:T(1,128)}, u32[]{:S(2)}) copy-start(f32[1,5,1,5]{3,2,1,0:T(1,128)} %param.18) | copy-start | bytes 304
  11.9 1.4 %copy-start = (bf16[16,128,256]{2,1,0:T(8,128)(2,1)S(1)}, bf16[16,128,256]{2,1,0:T(8,128)(2,1)}, u32[]{:S(2)}) copy-start(bf16[16,128,256]{2,1,0:T(8,128)(2,1)} %constant.55.clone.tback_ref) | copy-start | bytes 3145732
  11.9 1.5 %copy-start.1 = (bf16[16,256,128]{2,1,0:T(8,128)(2,1)S(1)}, bf16[16,256,128]{2,1,0:T(8,128)(2,1)}, u32[]{:S(2)}) copy-start(bf16[16,256,128]{2,1,0:T(8,128)(2,1)} %constant.54.clone.table_ref) | copy-start | bytes 3145732
  15.7 5.9 %collective-permute-start.3 = (bf16[16,2048]{1,0:T(8,128)(2,1)S(1)}, bf16[16,2048]{1,0:T(8,128)(2,1)S(1)}, u32[]{:S(2)}, u32[]{:S(2)}) collective-permute-start(bf16[16,2048]{1,0:T(8,128)(2,1)S(1)} %get-tuple-element.36), channel_id=1, source_target_pairs={{0,1},{1,0},{2,3},{3,2},{4,5},{5,4},{6,7},{7,6},{8,16},{9,17},{10,... | collective-permute-start | bytes 196616 | tf_op jit(solution)/shard_map/ppermute | solution.py:587
  18.8 2.9 %collective-permute-start.4 = (bf16[16,2048]{1,0:T(8,128)(2,1)S(1)}, bf16[16,2048]{1,0:T(8,128)(2,1)S(1)}, u32[]{:S(2)}, u32[]{:S(2)}) collective-permute-start(bf16[16,2048]{1,0:T(8,128)(2,1)S(1)} %get-tuple-element.37), channel_id=1, source_target_pairs={{0,8},{1,9},{2,10},{3,11},{4,12},{5,13},{6,14},{7,15},{8,0},{9,1},... | collective-permute-start | bytes 196616 | tf_op jit(solution)/shard_map/ppermute | solution.py:587
  21.8 8.0 %collective-permute-start.5 = (bf16[16,2048]{1,0:T(8,128)(2,1)S(1)}, bf16[16,2048]{1,0:T(8,128)(2,1)S(1)}, u32[]{:S(2)}, u32[]{:S(2)}) collective-permute-start(bf16[16,2048]{1,0:T(8,128)(2,1)S(1)} %get-tuple-element.40), channel_id=1, source_target_pairs={{0,8},{1,2},{2,1},{3,4},{4,3},{5,6},{6,5},{7,15},{8,0},{9,10},{10,... | collective-permute-start | bytes 196616 | tf_op jit(solution)/shard_map/ppermute | solution.py:587
  26.1 4.3 %collective-permute-start.6 = (bf16[16,2048]{1,0:T(8,128)(2,1)S(1)}, bf16[16,2048]{1,0:T(8,128)(2,1)S(1)}, u32[]{:S(2)}, u32[]{:S(2)}) collective-permute-start(bf16[16,2048]{1,0:T(8,128)(2,1)S(1)} %get-tuple-element.41), channel_id=1, source_target_pairs={{0,1},{1,0},{2,3},{3,2},{4,5},{5,4},{6,7},{7,6},{8,9},{9,8},{10,11... | collective-permute-start | bytes 196616 | tf_op jit(solution)/shard_map/ppermute | solution.py:587
  32.6 8.8 %collective-permute-start.8 = (bf16[3,1,2048]{2,1,0:T(2,128)(2,1)S(1)}, bf16[3,1,2048]{2,1,0:T(2,128)(2,1)S(1)}, u32[]{:S(2)}, u32[]{:S(2)}) collective-permute-start(bf16[3,1,2048]{2,1,0:T(2,128)(2,1)S(1)} %get-tuple-element.46), channel_id=1, source_target_pairs={{0,9},{1,10},{2,11},{3,12},{4,13},{5,14},{6,15},{7,72},{8,17},{9,1... | collective-permute-start | bytes 36872 | tf_op jit(solution)/shard_map/ppermute | solution.py:573
  32.7 8.7 %collective-permute-start.7 = (bf16[3,4,2048]{2,1,0:T(4,128)(2,1)S(1)}, bf16[3,4,2048]{2,1,0:T(4,128)(2,1)S(1)}, u32[]{:S(2)}, u32[]{:S(2)}) collective-permute-start(bf16[3,4,2048]{2,1,0:T(4,128)(2,1)S(1)} %get-tuple-element.45), channel_id=1, source_target_pairs={{0,1},{1,2},{2,3},{3,4},{4,5},{5,6},{6,7},{7,64},{8,9},{9,10},{10,... | collective-permute-start | bytes 147464 | tf_op jit(solution)/shard_map/ppermute | solution.py:573
  32.8 8.6 %collective-permute-start.9 = (bf16[3,4,2048]{2,1,0:T(4,128)(2,1)S(1)}, bf16[3,4,2048]{2,1,0:T(4,128)(2,1)S(1)}, u32[]{:S(2)}, u32[]{:S(2)}) collective-permute-start(bf16[3,4,2048]{2,1,0:T(4,128)(2,1)S(1)} %get-tuple-element.47), channel_id=1, source_target_pairs={{0,8},{1,9},{2,10},{3,11},{4,12},{5,13},{6,14},{7,15},{8,16},{9,17... | collective-permute-start | bytes 147464 | tf_op jit(solution)/shard_map/ppermute | solution.py:573

commit v7 on v6

--- a/solution.py
+++ b/solution.py
@@ -615,7 +615,7 @@
         own, free, info = call(
             own_kernel,
             (shape(OWN, WIDTH), shape(OWN, WIDTH), shape(OWN + 8, LANES)),
-            inputs=5, flops=2 * 10**10, vmem=8 * 1024 * 1024,
+            inputs=5, flops=10**8, vmem=8 * 1024 * 1024,
         )(place, node_blocks, inverse_mass, displacement, previous)
         operator, back, material, outgoing, column, arrival = call(
             functools.partial(prepare_kernel, starts),

time: 42.4 us -> 42.5 us (level)
  starting transfers between devices: 14.7 us -> 16.2 us
  local copies, waits for them, and re-layouts: 1.99 us -> 0.71 us
    ppermute x4, starting transfers between devices: 7.3 us -> 8.74 us  [swapped(): return lax.ppermute(array, ('colat', 'depth'), pairs)]
    unnamed x24, local copies, waits for them, and re-layouts: 1.99 us -> 0.71 us
    ppermute x4, waiting for transfers between devices: 7.12 us -> 6.4 us  [swapped(): return lax.ppermute(array, ('colat', 'depth'), pairs)]
    ppermute x6, waiting for transfers between devices: 7.74 us -> 8.28 us  [shifted(): return lax.ppermute(array, ('colat', 'depth'), pairs)]
  transfers between devices with their start and end apart: 10 -> 10, of which waited for: 4 -> 5; matrix products, arithmetic and copies ran while one was open for 0% -> 0% of each run, Pallas kernels for 6% -> 6%
where the time goes in v7:
time: 42.5 us; the launch traced here: 42.3 us
  starting transfers between devices  16.2 us (38%)
  waiting for transfers between devices  14.7 us (35%)
  Pallas kernels  9.81 us (23%)
  between operations  0.88 us (2%)
  local copies, waits for them, and re-layouts  0.71 us (2%)
    ppermute x4, starting transfers between devices, swapped(): return lax.ppermute(array, ('colat', 'depth'), pairs)  8.74 us
    ppermute x6, waiting for transfers between devices, shifted(): return lax.ppermute(array, ('colat', 'depth'), pairs)  8.28 us
    ppermute x6, starting transfers between devices, shifted(): return lax.ppermute(array, ('colat', 'depth'), pairs)  7.44 us
    ppermute x4, waiting for transfers between devices, swapped(): return lax.ppermute(array, ('colat', 'depth'), pairs)  6.4 us
    pallas_call x1, Pallas kernels, per_device(): call(step_one_kernel, (shape(NODES, WIDTH + LANES), tile, tile, shape(32,...  2.28 us
    pallas_call x1, Pallas kernels, per_device(): call(step_two_kernel, (shape(OWN, WIDTH), shape(3, 4, 4, WIDTH), row_face...  2.27 us
    pallas_call x1, Pallas kernels, per_device(): call(first_kernel, (row_face, row_face, point), [pltpu.SMEM((4, 4), jnp.i...  1.85 us
    pallas_call x1, Pallas kernels, per_device(): call(functools.partial(prepare_kernel, starts), (shape(STRAINS, 2 * NODES...  1.34 us
  transfers between devices with their start and end apart: 10, of which 5 were waited for; matrix products, arithmetic and copies ran while one was open for 0% of the time, Pallas kernels for 6%

profile of v7, /device:TPU:6, one launch (start us, length us, event | category | flops | bytes accessed | tf_op | source)
XLA Modules:
  0.0 42.3 jit_solution(8574360195630655762)
XLA Ops:
  0.6 0.0 copy-start.11
  0.6 0.0 copy-start.7
  0.7 0.0 copy-start.6
  0.7 1.9 %shard_map.132 = (bf16[3,4,2176]{2,1,0:T(4,128)(2,1)}, bf16[3,4,2176]{2,1,0:T(4,128)(2,1)}, bf16[3,1,2176]{2,1,0:T(2,128)(2,1)}) custom-call(s32[4,4]{1,0:T(4,128)} %blocks_hbm.1, f32[4,4]{1,0:T(4,128)} %mass_hbm.1, f32[3,4,4,2048]{3,2,1,0:T(4,128)} %disp_hbm.1), custom_call_target="tpu_custom_call" | custom-call | flops 20000000000 | bytes 1048576 | tf_op jit(solution)/shard_map/pallas_call | solution.py:600
  2.5 5.9 %collective-permute-start.1 = (bf16[3,1,2176]{2,1,0:T(2,128)(2,1)}, bf16[3,1,2176]{2,1,0:T(2,128)(2,1)S(1)}, u32[]{:S(2)}, u32[]{:S(2)}) collective-permute-start(bf16[3,1,2176]{2,1,0:T(2,128)(2,1)} %get-tuple-element.29), channel_id=1, source_target_pairs={{0,63},{1,120},{2,121},{3,122},{4,123},{5,124},{6,125},{7,126},{8,... | collective-permute-start | bytes 39176 | tf_op jit(solution)/shard_map/ppermute | solution.py:573
  8.4 1.3 %collective-permute-start = (bf16[3,4,2176]{2,1,0:T(4,128)(2,1)}, bf16[3,4,2176]{2,1,0:T(4,128)(2,1)S(1)}, u32[]{:S(2)}, u32[]{:S(2)}) collective-permute-start(bf16[3,4,2176]{2,1,0:T(4,128)(2,1)} %get-tuple-element.28), channel_id=1, source_target_pairs={{0,71},{1,0},{2,1},{3,2},{4,3},{5,4},{6,5},{7,6},{8,79},{9,8},{10,... | collective-permute-start | bytes 156680 | tf_op jit(solution)/shard_map/ppermute | solution.py:573
  9.7 0.0 collective-permute-start.2
  9.8 0.0 copy-start.9
  9.8 0.0 copy-start.8
  9.8 0.0 copy-start.10
  9.9 0.0 copy-done.11
  9.9 0.0 copy-done.7
  9.9 0.0 copy-done.6
  9.9 0.6 %copy-done.9 = f32[2,1,5,1,5]{4,3,2,1,0:T(1,128)S(1)} copy-done((f32[2,1,5,1,5]{4,3,2,1,0:T(1,128)S(1)}, f32[2,1,5,1,5]{4,3,2,1,0:T(1,128)}, u32[]{:S(2)}) %copy-start.9) | copy-done | bytes 224
  10.5 0.0 copy-done.8
  10.5 0.0 copy-done.10
  10.6 0.0 copy-start
  10.6 0.0 copy-start.1
  10.6 1.3 %shard_map.133 = (bf16[152,160]{1,0:T(8,128)(2,1)S(1)}, bf16[160,152]{1,0:T(8,128)(2,1)S(1)}, f32[16,56,128]{2,1,0:T(8,128)S(1)}, bf16[64,80]{1,0:T(8,128)(2,1)S...) custom-call(f32[8,128]{1,0:T(8,128)S(1)} %select_select_fusion.place_ref, f32[10,1,5]{2,1,0:T(1,128)S(1)} %bitcast.7, ...), custom_call_target="tpu_custom_call" | custom-call | flops 1000000000 | bytes 1048576 | tf_op jit(solution)/shard_map/pallas_call | solution.py:620
  11.9 0.0 copy-done.2
  11.9 0.0 copy-done.3
  11.9 0.0 copy-done.4
  11.9 0.0 copy-done.5
  12.0 0.2 shard_map.131
  12.2 0.0 collective-permute-done.1.corner_ref
  12.2 0.5 %collective-permute-done.col_ref = bf16[3,4,2176]{2,1,0:T(4,128)(2,1)S(1)} collective-permute-done((bf16[3,4,2176]{2,1,0:T(4,128)(2,1)}, bf16[3,4,2176]{2,1,0:T(4,128)(2,1)S(1)}, u32[]{:S(2)}, u32[]{:S(2)}) %collective-permute-start) | collective-permute-done | bytes 52256 | tf_op jit(solution)/shard_map/ppermute | solution.py:573
  12.8 0.0 collective-permute-done.2.row_ref
  12.8 0.0 copy-done
  12.8 0.0 copy-done.1
  12.8 2.3 %shard_map.134 = (f32[80,2176]{1,0:T(8,128)S(1)}, bf16[16,2048]{1,0:T(8,128)(2,1)S(1)}, bf16[16,2048]{1,0:T(8,128)(2,1)S(1)}, bf16[32,2048]{1,0:T(8,128)(2,1)S(1)}) custom-call(f32[48,2048]{1,0:T(8,128)S(1)} %get-tuple-element.25.own_ref, f32[48,2048]{1,0:T(8,128)S(1)} %get-tuple-element.26.free_ref, f32[56,128]{1,0:T(8,128)S(1)} %get-tuple-element.27.info_ref, ...), custom_call_target="tpu_custom_call" | custom-call | flops 1000000000 | bytes 1048576 | tf_op jit(solution)/shard_map/pallas_call | solution.py:645
  15.1 3.7 %collective-permute-start.3 = (bf16[16,2048]{1,0:T(8,128)(2,1)S(1)}, bf16[16,2048]{1,0:T(8,128)(2,1)S(1)}, u32[]{:S(2)}, u32[]{:S(2)}) collective-permute-start(bf16[16,2048]{1,0:T(8,128)(2,1)S(1)} %get-tuple-element.36), channel_id=1, source_target_pairs={{0,1},{1,0},{2,3},{3,2},{4,5},{5,4},{6,7},{7,6},{8,16},{9,17},{10,... | collective-permute-start | bytes 196616 | tf_op jit(solution)/shard_map/ppermute | solution.py:587
  18.8 0.0 collective-permute-start.4
  18.8 2.1 %collective-permute-done.3.side_ref.cside_ref = bf16[16,2048]{1,0:T(8,128)(2,1)S(1)} collective-permute-done((bf16[16,2048]{1,0:T(8,128)(2,1)S(1)}, bf16[16,2048]{1,0:T(8,128)(2,1)S(1)}, u32[]{:S(2)}, u32[]{:S(2)}) %collective-permute-start.3) | collective-permute-done | bytes 65568 | tf_op jit(solution)/shard_map/ppermute | solution.py:587
  20.9 0.0 collective-permute-done.4.pair_ref.cpair_ref
  20.9 0.2 shard_map.135
  21.1 5.0 %collective-permute-start.5 = (bf16[16,2048]{1,0:T(8,128)(2,1)S(1)}, bf16[16,2048]{1,0:T(8,128)(2,1)S(1)}, u32[]{:S(2)}, u32[]{:S(2)}) collective-permute-start(bf16[16,2048]{1,0:T(8,128)(2,1)S(1)} %get-tuple-element.40), channel_id=1, source_target_pairs={{0,8},{1,2},{2,1},{3,4},{4,3},{5,6},{6,5},{7,15},{8,0},{9,10},{10,... | collective-permute-start | bytes 196616 | tf_op jit(solution)/shard_map/ppermute | solution.py:587
  26.1 0.0 collective-permute-start.6
  26.1 3.0 %collective-permute-done.5.dside_ref = bf16[16,2048]{1,0:T(8,128)(2,1)S(1)} collective-permute-done((bf16[16,2048]{1,0:T(8,128)(2,1)S(1)}, bf16[16,2048]{1,0:T(8,128)(2,1)S(1)}, u32[]{:S(2)}, u32[]{:S(2)}) %collective-permute-start.5) | collective-permute-done | bytes 65568 | tf_op jit(solution)/shard_map/ppermute | solution.py:587
  29.1 1.3 %collective-permute-done.6.dpair_ref = bf16[16,2048]{1,0:T(8,128)(2,1)S(1)} collective-permute-done((bf16[16,2048]{1,0:T(8,128)(2,1)S(1)}, bf16[16,2048]{1,0:T(8,128)(2,1)S(1)}, u32[]{:S(2)}, u32[]{:S(2)}) %collective-permute-start.6) | collective-permute-done | bytes 65568 | tf_op jit(solution)/shard_map/ppermute | solution.py:587
  30.4 2.3 %shard_map.136 = (f32[48,2048]{1,0:T(8,128)S(1)}, f32[3,4,4,2048]{3,2,1,0:T(4,128)S(1)}, bf16[3,4,2048]{2,1,0:T(4,128)(2,1)S(1)}, bf16[3,4,2048]{2,1,0:T(4,128)(2,1)S(1)}, bf16[3,1,2048]{2,1,0:T(2,128)(2,1)S(1)}) custom-call(f32[48,2048]{1,0:T(8,128)S(1)} %get-tuple-element.25.own_ref, f32[80,2176]{1,0:T(8,128)S(1)} %get-tuple-element.35.sum_ref, ...), custom_call_target="tpu_custom_call" | custom-call | flops 1000000000 | bytes 1048576 | tf_op jit(solution)/shard_map/pallas_call | solution.py:657
  32.7 0.1 collective-permute-start.8
  32.7 0.1 collective-permute-start.7
  32.8 0.1 collective-permute-start.9
  32.9 0.8 %shard_map.137 = f32[3,4,4,2048]{3,2,1,0:T(4,128)} custom-call(f32[48,2048]{1,0:T(8,128)S(1)} %get-tuple-element.43.rows_ref), custom_call_target="tpu_custom_call" | custom-call | flops 20000000000 | bytes 1048576 | tf_op jit(solution)/shard_map/pallas_call | solution.py:669
  33.7 7.7 %collective-permute-done.8.corner_ref = bf16[3,1,2048]{2,1,0:T(2,128)(2,1)S(1)} collective-permute-done((bf16[3,1,2048]{2,1,0:T(2,128)(2,1)S(1)}, bf16[3,1,2048]{2,1,0:T(2,128)(2,1)S(1)}, u32[]{:S(2)}, u32[]{:S(2)}) %collective-permute-start.8) | collective-permute-done | bytes 12320 | tf_op jit(solution)/shard_map/ppermute | solution.py:573
  41.4 0.0 collective-permute-done.7.col_ref
  41.4 0.0 collective-permute-done.9.row_ref
  41.4 0.9 %shard_map.138 = f32[3,4,4,2048]{3,2,1,0:T(4,128)} custom-call(f32[3,4,4,2048]{3,2,1,0:T(4,128)S(1)} %get-tuple-element.44.sum_ref, bf16[3,4,2048]{2,1,0:T(4,128)(2,1)S(1)} %collective-permute-done.7.col_ref, bf16[3,1,2048]{2,1,0:T(2,128)(2,1)S(1)} %collective-permute-done.8.corner_ref, bf16[3,4,2048]{2,1,0:T(4,128)(2,1)S(1)} %collective-permute-done.9.row_ref), custom_call_target="tpu_custom_call" | custom-call | bytes 1048576 | tf_op jit(solution)/shard_map/pallas_call | solution.py:670
  (9 shorter events, 0.0 us)
Async XLA Ops:
  0.6 9.2 %copy-start.11 = (f32[1016,256]{1,0:T(8,128)S(1)}, f32[1016,256]{1,0:T(8,128)}, u32[]{:S(2)}) copy-start(f32[1016,256]{1,0:T(8,128)} %constant.53.clone.packed_ref) | copy-start | bytes 3121156
  0.6 9.2 %copy-start.7 = (f32[1,5,1,5,2048]{4,2,3,1,0:T(1,128)S(1)}, f32[1,5,1,5,2048]{4,2,3,1,0:T(1,128)}, u32[]{:S(2)}) copy-start(f32[1,5,1,5,2048]{4,2,3,1,0:T(1,128)} %param.20) | copy-start | bytes 614404
  0.7 9.2 %copy-start.6 = (f32[1,5,1,5,2048]{4,2,3,1,0:T(1,128)S(1)}, f32[1,5,1,5,2048]{4,2,3,1,0:T(1,128)}, u32[]{:S(2)}) copy-start(f32[1,5,1,5,2048]{4,2,3,1,0:T(1,128)} %param.19) | copy-start | bytes 614404
  2.5 9.7 %collective-permute-start.1 = (bf16[3,1,2176]{2,1,0:T(2,128)(2,1)}, bf16[3,1,2176]{2,1,0:T(2,128)(2,1)S(1)}, u32[]{:S(2)}, u32[]{:S(2)}) collective-permute-start(bf16[3,1,2176]{2,1,0:T(2,128)(2,1)} %get-tuple-element.29), channel_id=1, source_target_pairs={{0,63},{1,120},{2,121},{3,122},{4,123},{5,124},{6,125},{7,126},{8,... | collective-permute-start | bytes 39176 | tf_op jit(solution)/shard_map/ppermute | solution.py:573
  8.4 4.3 %collective-permute-start = (bf16[3,4,2176]{2,1,0:T(4,128)(2,1)}, bf16[3,4,2176]{2,1,0:T(4,128)(2,1)S(1)}, u32[]{:S(2)}, u32[]{:S(2)}) collective-permute-start(bf16[3,4,2176]{2,1,0:T(4,128)(2,1)} %get-tuple-element.28), channel_id=1, source_target_pairs={{0,71},{1,0},{2,1},{3,2},{4,3},{5,4},{6,5},{7,6},{8,79},{9,8},{10,... | collective-permute-start | bytes 156680 | tf_op jit(solution)/shard_map/ppermute | solution.py:573
  9.7 3.0 %collective-permute-start.2 = (bf16[3,4,2176]{2,1,0:T(4,128)(2,1)}, bf16[3,4,2176]{2,1,0:T(4,128)(2,1)S(1)}, u32[]{:S(2)}, u32[]{:S(2)}) collective-permute-start(bf16[3,4,2176]{2,1,0:T(4,128)(2,1)} %get-tuple-element.30), channel_id=1, source_target_pairs={{0,120},{1,121},{2,122},{3,123},{4,124},{5,125},{6,126},{7,127},{8... | collective-permute-start | bytes 156680 | tf_op jit(solution)/shard_map/ppermute | solution.py:573
  9.8 0.7 %copy-start.9 = (f32[2,1,5,1,5]{4,3,2,1,0:T(1,128)S(1)}, f32[2,1,5,1,5]{4,3,2,1,0:T(1,128)}, u32[]{:S(2)}) copy-start(f32[2,1,5,1,5]{4,3,2,1,0:T(1,128)} %param.17) | copy-start | bytes 604
  9.8 0.7 %copy-start.8 = (f32[2,1,5,1,5]{4,3,2,1,0:T(1,128)S(1)}, f32[2,1,5,1,5]{4,3,2,1,0:T(1,128)}, u32[]{:S(2)}) copy-start(f32[2,1,5,1,5]{4,3,2,1,0:T(1,128)} %param.16) | copy-start | bytes 604
  9.8 0.7 %copy-start.10 = (f32[1,5,1,5]{3,2,1,0:T(1,128)S(1)}, f32[1,5,1,5]{3,2,1,0:T(1,128)}, u32[]{:S(2)}) copy-start(f32[1,5,1,5]{3,2,1,0:T(1,128)} %param.18) | copy-start | bytes 304
  10.5 1.4 %copy-start.2 = (f32[3,4,4,2048]{3,2,1,0:T(4,128)S(1)}, f32[3,4,4,2048]{3,2,1,0:T(4,128)}, u32[]{:S(2)}) copy-start(f32[3,4,4,2048]{3,2,1,0:T(4,128)} %disp_hbm.1) | copy-start | bytes 1179652
  10.5 1.4 %copy-start.3 = (f32[3,4,4,2048]{3,2,1,0:T(4,128)S(1)}, f32[3,4,4,2048]{3,2,1,0:T(4,128)}, u32[]{:S(2)}) copy-start(f32[3,4,4,2048]{3,2,1,0:T(4,128)} %prev_ref.1) | copy-start | bytes 1179652
  10.5 1.4 %copy-start.4 = (s32[4,4]{1,0:T(4,128)S(1)}, s32[4,4]{1,0:T(4,128)}, u32[]{:S(2)}) copy-start(s32[4,4]{1,0:T(4,128)} %blocks_hbm.1) | copy-start | bytes 196
  10.5 1.4 %copy-start.5 = (f32[4,4]{1,0:T(4,128)S(1)}, f32[4,4]{1,0:T(4,128)}, u32[]{:S(2)}) copy-start(f32[4,4]{1,0:T(4,128)} %mass_hbm.1) | copy-start | bytes 196
  10.6 2.2 %copy-start = (bf16[16,128,256]{2,1,0:T(8,128)(2,1)S(1)}, bf16[16,128,256]{2,1,0:T(8,128)(2,1)}, u32[]{:S(2)}) copy-start(bf16[16,128,256]{2,1,0:T(8,128)(2,1)} %constant.55.clone.tback_ref) | copy-start | bytes 3145732
  10.6 2.2 %copy-start.1 = (bf16[16,256,128]{2,1,0:T(8,128)(2,1)S(1)}, bf16[16,256,128]{2,1,0:T(8,128)(2,1)}, u32[]{:S(2)}) copy-start(bf16[16,256,128]{2,1,0:T(8,128)(2,1)} %constant.54.clone.table_ref) | copy-start | bytes 3145732
  15.1 5.9 %collective-permute-start.3 = (bf16[16,2048]{1,0:T(8,128)(2,1)S(1)}, bf16[16,2048]{1,0:T(8,128)(2,1)S(1)}, u32[]{:S(2)}, u32[]{:S(2)}) collective-permute-start(bf16[16,2048]{1,0:T(8,128)(2,1)S(1)} %get-tuple-element.36), channel_id=1, source_target_pairs={{0,1},{1,0},{2,3},{3,2},{4,5},{5,4},{6,7},{7,6},{8,16},{9,17},{10,... | collective-permute-start | bytes 196616 | tf_op jit(solution)/shard_map/ppermute | solution.py:587
  18.8 2.1 %collective-permute-start.4 = (bf16[16,2048]{1,0:T(8,128)(2,1)S(1)}, bf16[16,2048]{1,0:T(8,128)(2,1)S(1)}, u32[]{:S(2)}, u32[]{:S(2)}) collective-permute-start(bf16[16,2048]{1,0:T(8,128)(2,1)S(1)} %get-tuple-element.37), channel_id=1, source_target_pairs={{0,8},{1,9},{2,10},{3,11},{4,12},{5,13},{6,14},{7,15},{8,0},{9,1},... | collective-permute-start | bytes 196616 | tf_op jit(solution)/shard_map/ppermute | solution.py:587
  21.1 8.0 %collective-permute-start.5 = (bf16[16,2048]{1,0:T(8,128)(2,1)S(1)}, bf16[16,2048]{1,0:T(8,128)(2,1)S(1)}, u32[]{:S(2)}, u32[]{:S(2)}) collective-permute-start(bf16[16,2048]{1,0:T(8,128)(2,1)S(1)} %get-tuple-element.40), channel_id=1, source_target_pairs={{0,8},{1,2},{2,1},{3,4},{4,3},{5,6},{6,5},{7,15},{8,0},{9,10},{10,... | collective-permute-start | bytes 196616 | tf_op jit(solution)/shard_map/ppermute | solution.py:587
  26.1 4.3 %collective-permute-start.6 = (bf16[16,2048]{1,0:T(8,128)(2,1)S(1)}, bf16[16,2048]{1,0:T(8,128)(2,1)S(1)}, u32[]{:S(2)}, u32[]{:S(2)}) collective-permute-start(bf16[16,2048]{1,0:T(8,128)(2,1)S(1)} %get-tuple-element.41), channel_id=1, source_target_pairs={{0,1},{1,0},{2,3},{3,2},{4,5},{5,4},{6,7},{7,6},{8,9},{9,8},{10,11... | collective-permute-start | bytes 196616 | tf_op jit(solution)/shard_map/ppermute | solution.py:587
  32.7 8.8 %collective-permute-start.8 = (bf16[3,1,2048]{2,1,0:T(2,128)(2,1)S(1)}, bf16[3,1,2048]{2,1,0:T(2,128)(2,1)S(1)}, u32[]{:S(2)}, u32[]{:S(2)}) collective-permute-start(bf16[3,1,2048]{2,1,0:T(2,128)(2,1)S(1)} %get-tuple-element.46), channel_id=1, source_target_pairs={{0,9},{1,10},{2,11},{3,12},{4,13},{5,14},{6,15},{7,72},{8,17},{9,1... | collective-permute-start | bytes 36872 | tf_op jit(solution)/shard_map/ppermute | solution.py:573
  32.7 8.7 %collective-permute-start.7 = (bf16[3,4,2048]{2,1,0:T(4,128)(2,1)S(1)}, bf16[3,4,2048]{2,1,0:T(4,128)(2,1)S(1)}, u32[]{:S(2)}, u32[]{:S(2)}) collective-permute-start(bf16[3,4,2048]{2,1,0:T(4,128)(2,1)S(1)} %get-tuple-element.45), channel_id=1, source_target_pairs={{0,1},{1,2},{2,3},{3,4},{4,5},{5,6},{6,7},{7,64},{8,9},{9,10},{10,... | collective-permute-start | bytes 147464 | tf_op jit(solution)/shard_map/ppermute | solution.py:573
  32.8 8.6 %collective-permute-start.9 = (bf16[3,4,2048]{2,1,0:T(4,128)(2,1)S(1)}, bf16[3,4,2048]{2,1,0:T(4,128)(2,1)S(1)}, u32[]{:S(2)}, u32[]{:S(2)}) collective-permute-start(bf16[3,4,2048]{2,1,0:T(4,128)(2,1)S(1)} %get-tuple-element.47), channel_id=1, source_target_pairs={{0,8},{1,9},{2,10},{3,11},{4,12},{5,13},{6,14},{7,15},{8,16},{9,17... | collective-permute-start | bytes 147464 | tf_op jit(solution)/shard_map/ppermute | solution.py:573

commit v8 on v6

--- a/solution.py
+++ b/solution.py
@@ -527,8 +527,9 @@
             out_ref[c, i] = rows_ref[at : at + 4]
 
 
-def last_kernel(sum_ref, col_ref, corner_ref, row_ref, out_ref):
+def last_kernel(sum_ref, col_ref, corner_ref, row_ref, out_hbm, out_ref, sems):
     first = lax.broadcasted_iota(jnp.int32, (4, 1), 0) == 0
+    stores = [pltpu.make_async_copy(out_ref.at[c], out_hbm.at[c], sems.at[c]) for c in range(3)]
     for c in range(3):
         for i in range(4):
             arrived = col_ref[c, i : i + 1].astype(F32)
@@ -538,9 +539,12 @@
             if i == 0:
                 value = value + row_ref[c].astype(F32)
             out_ref[c, i] = value
-
-
-def call(kernel, outs, scratch=(), scalars=0, inputs=0, flops=0, far=0, vmem=VMEM_LIMIT):
+        stores[c].start()
+    for store in stores:
+        store.wait()
+
+
+def call(kernel, outs, scratch=(), scalars=0, inputs=0, flops=0, far=0, vmem=VMEM_LIMIT, outside=False):
     near = pl.BlockSpec(memory_space=pltpu.VMEM)
     return pl.pallas_call(
         kernel,
@@ -548,7 +552,7 @@
         in_specs=[pl.BlockSpec(memory_space=pltpu.HBM)] * far
         + [pl.BlockSpec(memory_space=pltpu.SMEM)] * scalars
         + [near] * inputs,
-        out_specs=jax.tree.map(lambda _: near, outs),
+        out_specs=jax.tree.map(lambda _: pl.BlockSpec(memory_space=pltpu.HBM) if outside else near, outs),
         scratch_shapes=list(scratch),
         compiler_params=pltpu.CompilerParams(vmem_limit_bytes=vmem),
         cost_estimate=pl.CostEstimate(flops=flops, bytes_accessed=1 << 20, transcendentals=0),
@@ -667,7 +671,12 @@
         corner = shifted(corner, 1, 1)
         row = shifted(row, 1, 0)
         middle = call(middle_kernel, shape(3, 4, 4, WIDTH), inputs=1, flops=2 * 10**10, vmem=4 * 1024 * 1024)(middle)
-        final = call(last_kernel, shape(3, 4, 4, WIDTH), inputs=4)(final, col, corner, row)
+        final = call(
+            last_kernel,
+            shape(3, 4, 4, WIDTH),
+            [pltpu.VMEM((3, 4, 4, WIDTH), F32), pltpu.SemaphoreType.DMA((3,))],
+            inputs=4, outside=True,
+        )(final, col, corner, row)
         return middle, final
 
     return jax.shard_map(

time: 42.4 us -> 42.4 us (level)
  no operation moved by 1% of the time
where the time goes in v8:
time: 42.4 us; the launch traced here: 42.2 us
  waiting for transfers between devices  14.9 us (35%)
  starting transfers between devices  14.7 us (35%)
  Pallas kernels  9.71 us (23%)
  local copies, waits for them, and re-layouts  1.99 us (5%)
  between operations  0.86 us (2%)
    ppermute x6, waiting for transfers between devices, shifted(): return lax.ppermute(array, ('colat', 'depth'), pairs)  7.74 us
    ppermute x6, starting transfers between devices, shifted(): return lax.ppermute(array, ('colat', 'depth'), pairs)  7.44 us
    ppermute x4, starting transfers between devices, swapped(): return lax.ppermute(array, ('colat', 'depth'), pairs)  7.3 us
    ppermute x4, waiting for transfers between devices, swapped(): return lax.ppermute(array, ('colat', 'depth'), pairs)  7.12 us
    pallas_call x1, Pallas kernels, per_device(): call(step_two_kernel, (shape(OWN, WIDTH), shape(3, 4, 4, WIDTH), row_face...  2.28 us
    pallas_call x1, Pallas kernels, per_device(): call(step_one_kernel, (shape(NODES, WIDTH + LANES), tile, tile, shape(32,...  2.27 us
    unnamed x24, local copies, waits for them, and re-layouts  1.99 us
    pallas_call x1, Pallas kernels, per_device(): call(first_kernel, (row_face, row_face, point), [pltpu.SMEM((4, 4), jnp.i...  1.81 us
  transfers between devices with their start and end apart: 10, of which 4 were waited for; matrix products, arithmetic and copies ran while one was open for 0% of the time, Pallas kernels for 6%

profile of v8, /device:TPU:6, one launch (start us, length us, event | category | flops | bytes accessed | tf_op | source)
XLA Modules:
  0.0 42.2 jit_solution(8230189167015522723)
XLA Ops:
  0.6 0.0 copy-start.2
  0.6 0.0 copy-start.3
  0.6 1.8 %shard_map.132 = (bf16[3,4,2176]{2,1,0:T(4,128)(2,1)}, bf16[3,4,2176]{2,1,0:T(4,128)(2,1)}, bf16[3,1,2176]{2,1,0:T(2,128)(2,1)}) custom-call(s32[4,4]{1,0:T(4,128)} %blocks_hbm.1, f32[4,4]{1,0:T(4,128)} %mass_hbm.1, f32[3,4,4,2048]{3,2,1,0:T(4,128)} %disp_hbm.1), custom_call_target="tpu_custom_call" | custom-call | flops 20000000000 | bytes 1048576 | tf_op jit(solution)/shard_map/pallas_call | solution.py:604
  2.5 5.9 %collective-permute-start.1 = (bf16[3,1,2176]{2,1,0:T(2,128)(2,1)}, bf16[3,1,2176]{2,1,0:T(2,128)(2,1)S(1)}, u32[]{:S(2)}, u32[]{:S(2)}) collective-permute-start(bf16[3,1,2176]{2,1,0:T(2,128)(2,1)} %get-tuple-element.29), channel_id=1, source_target_pairs={{0,63},{1,120},{2,121},{3,122},{4,123},{5,124},{6,125},{7,126},{8,... | collective-permute-start | bytes 39176 | tf_op jit(solution)/shard_map/ppermute | solution.py:577
  8.4 1.3 %collective-permute-start = (bf16[3,4,2176]{2,1,0:T(4,128)(2,1)}, bf16[3,4,2176]{2,1,0:T(4,128)(2,1)S(1)}, u32[]{:S(2)}, u32[]{:S(2)}) collective-permute-start(bf16[3,4,2176]{2,1,0:T(4,128)(2,1)} %get-tuple-element.28), channel_id=1, source_target_pairs={{0,71},{1,0},{2,1},{3,2},{4,3},{5,4},{6,5},{7,6},{8,79},{9,8},{10,... | collective-permute-start | bytes 156680 | tf_op jit(solution)/shard_map/ppermute | solution.py:577
  9.7 0.0 collective-permute-start.2
  9.7 0.0 copy-start.9
  9.8 0.0 copy-start.10
  9.8 0.0 copy-done.2
  9.8 0.0 copy-done.3
  9.8 0.6 %copy-done.9 = s32[4,4]{1,0:T(4,128)S(1)} copy-done((s32[4,4]{1,0:T(4,128)S(1)}, s32[4,4]{1,0:T(4,128)}, u32[]{:S(2)}) %copy-start.9) | copy-done | bytes 88
  10.4 0.0 copy-done.10
  10.4 0.0 copy-start.4
  10.5 0.0 copy-start.5
  10.5 0.2 shard_map.131
  10.7 0.0 copy-start.6
  10.7 0.0 copy-start.8
  10.7 0.7 %copy-done.4 = f32[1,5,1,5,2048]{4,2,3,1,0:T(1,128)S(1)} copy-done((f32[1,5,1,5,2048]{4,2,3,1,0:T(1,128)S(1)}, f32[1,5,1,5,2048]{4,2,3,1,0:T(1,128)}, u32[]{:S(2)}) %copy-start.4) | copy-done | bytes 204824
  11.4 0.1 copy-done.5
  11.5 0.0 copy-done.7
  11.5 0.4 %copy-done.11 = f32[1016,256]{1,0:T(8,128)S(1)} copy-done((f32[1016,256]{1,0:T(8,128)S(1)}, f32[1016,256]{1,0:T(8,128)}, u32[]{:S(2)}) %copy-start.11) | copy-done | bytes 1040408
  11.9 0.0 copy-done.6
  11.9 0.0 copy-done.8
  11.9 1.3 %shard_map.133 = (bf16[152,160]{1,0:T(8,128)(2,1)S(1)}, bf16[160,152]{1,0:T(8,128)(2,1)S(1)}, f32[16,56,128]{2,1,0:T(8,128)S(1)}, bf16[64,80]{1,0:T(8,128)(2,1)S...) custom-call(f32[8,128]{1,0:T(8,128)S(1)} %select_select_fusion.place_ref, f32[10,1,5]{2,1,0:T(1,128)S(1)} %bitcast.7, ...), custom_call_target="tpu_custom_call" | custom-call | flops 1000000000 | bytes 1048576 | tf_op jit(solution)/shard_map/pallas_call | solution.py:624
  13.3 0.0 collective-permute-done.1.corner_ref
  13.3 0.0 collective-permute-done.col_ref
  13.3 0.0 collective-permute-done.2.row_ref
  13.3 0.0 copy-done
  13.3 0.1 copy-done.1
  13.5 2.3 %shard_map.134 = (f32[80,2176]{1,0:T(8,128)S(1)}, bf16[16,2048]{1,0:T(8,128)(2,1)S(1)}, bf16[16,2048]{1,0:T(8,128)(2,1)S(1)}, bf16[32,2048]{1,0:T(8,128)(2,1)S(1)}) custom-call(f32[48,2048]{1,0:T(8,128)S(1)} %get-tuple-element.25.own_ref, f32[48,2048]{1,0:T(8,128)S(1)} %get-tuple-element.26.free_ref, f32[56,128]{1,0:T(8,128)S(1)} %get-tuple-element.27.info_ref, ...), custom_call_target="tpu_custom_call" | custom-call | flops 1000000000 | bytes 1048576 | tf_op jit(solution)/shard_map/pallas_call | solution.py:649
  15.7 3.0 %collective-permute-start.3 = (bf16[16,2048]{1,0:T(8,128)(2,1)S(1)}, bf16[16,2048]{1,0:T(8,128)(2,1)S(1)}, u32[]{:S(2)}, u32[]{:S(2)}) collective-permute-start(bf16[16,2048]{1,0:T(8,128)(2,1)S(1)} %get-tuple-element.36), channel_id=1, source_target_pairs={{0,1},{1,0},{2,3},{3,2},{4,5},{5,4},{6,7},{7,6},{8,16},{9,17},{10,... | collective-permute-start | bytes 196616 | tf_op jit(solution)/shard_map/ppermute | solution.py:591
  18.8 0.0 collective-permute-start.4
  18.8 2.9 %collective-permute-done.3.side_ref.cside_ref = bf16[16,2048]{1,0:T(8,128)(2,1)S(1)} collective-permute-done((bf16[16,2048]{1,0:T(8,128)(2,1)S(1)}, bf16[16,2048]{1,0:T(8,128)(2,1)S(1)}, u32[]{:S(2)}, u32[]{:S(2)}) %collective-permute-start.3) | collective-permute-done | bytes 65568 | tf_op jit(solution)/shard_map/ppermute | solution.py:591
  21.6 0.0 collective-permute-done.4.pair_ref.cpair_ref
  21.6 0.2 shard_map.135
  21.8 4.3 %collective-permute-start.5 = (bf16[16,2048]{1,0:T(8,128)(2,1)S(1)}, bf16[16,2048]{1,0:T(8,128)(2,1)S(1)}, u32[]{:S(2)}, u32[]{:S(2)}) collective-permute-start(bf16[16,2048]{1,0:T(8,128)(2,1)S(1)} %get-tuple-element.40), channel_id=1, source_target_pairs={{0,8},{1,2},{2,1},{3,4},{4,3},{5,6},{6,5},{7,15},{8,0},{9,10},{10,... | collective-permute-start | bytes 196616 | tf_op jit(solution)/shard_map/ppermute | solution.py:591
  26.1 0.0 collective-permute-start.6
  26.1 3.7 %collective-permute-done.5.dside_ref = bf16[16,2048]{1,0:T(8,128)(2,1)S(1)} collective-permute-done((bf16[16,2048]{1,0:T(8,128)(2,1)S(1)}, bf16[16,2048]{1,0:T(8,128)(2,1)S(1)}, u32[]{:S(2)}, u32[]{:S(2)}) %collective-permute-start.5) | collective-permute-done | bytes 65568 | tf_op jit(solution)/shard_map/ppermute | solution.py:591
  29.7 0.6 %collective-permute-done.6.dpair_ref = bf16[16,2048]{1,0:T(8,128)(2,1)S(1)} collective-permute-done((bf16[16,2048]{1,0:T(8,128)(2,1)S(1)}, bf16[16,2048]{1,0:T(8,128)(2,1)S(1)}, u32[]{:S(2)}, u32[]{:S(2)}) %collective-permute-start.6) | collective-permute-done | bytes 65568 | tf_op jit(solution)/shard_map/ppermute | solution.py:591
  30.3 2.3 %shard_map.136 = (f32[48,2048]{1,0:T(8,128)S(1)}, f32[3,4,4,2048]{3,2,1,0:T(4,128)S(1)}, bf16[3,4,2048]{2,1,0:T(4,128)(2,1)S(1)}, bf16[3,4,2048]{2,1,0:T(4,128)(2,1)S(1)}, bf16[3,1,2048]{2,1,0:T(2,128)(2,1)S(1)}) custom-call(f32[48,2048]{1,0:T(8,128)S(1)} %get-tuple-element.25.own_ref, f32[80,2176]{1,0:T(8,128)S(1)} %get-tuple-element.35.sum_ref, ...), custom_call_target="tpu_custom_call" | custom-call | flops 1000000000 | bytes 1048576 | tf_op jit(solution)/shard_map/pallas_call | solution.py:661
  32.6 0.1 collective-permute-start.8
  32.7 0.1 collective-permute-start.7
  32.8 0.1 collective-permute-start.9
  32.9 0.8 %shard_map.137 = f32[3,4,4,2048]{3,2,1,0:T(4,128)} custom-call(f32[48,2048]{1,0:T(8,128)S(1)} %get-tuple-element.43.rows_ref), custom_call_target="tpu_custom_call" | custom-call | flops 20000000000 | bytes 1048576 | tf_op jit(solution)/shard_map/pallas_call | solution.py:673
  33.6 7.7 %collective-permute-done.8.corner_ref = bf16[3,1,2048]{2,1,0:T(2,128)(2,1)S(1)} collective-permute-done((bf16[3,1,2048]{2,1,0:T(2,128)(2,1)S(1)}, bf16[3,1,2048]{2,1,0:T(2,128)(2,1)S(1)}, u32[]{:S(2)}, u32[]{:S(2)}) %collective-permute-start.8) | collective-permute-done | bytes 12320 | tf_op jit(solution)/shard_map/ppermute | solution.py:577
  41.4 0.0 collective-permute-done.7.col_ref
  41.4 0.0 collective-permute-done.9.row_ref
  41.4 0.8 %shard_map.138 = f32[3,4,4,2048]{3,2,1,0:T(4,128)} custom-call(f32[3,4,4,2048]{3,2,1,0:T(4,128)S(1)} %get-tuple-element.44.sum_ref, bf16[3,4,2048]{2,1,0:T(4,128)(2,1)S(1)} %collective-permute-done.7.col_ref, bf16[3,1,2048]{2,1,0:T(2,128)(2,1)S(1)} %collective-permute-done.8.corner_ref, bf16[3,4,2048]{2,1,0:T(4,128)(2,1)S(1)} %collective-permute-done.9.row_ref), custom_call_target="tpu_custom_call" | custom-call | bytes 1048576 | tf_op jit(solution)/shard_map/pallas_call | solution.py:674
  (9 shorter events, 0.0 us)
Async XLA Ops:
  0.6 9.2 %copy-start.2 = (f32[3,4,4,2048]{3,2,1,0:T(4,128)S(1)}, f32[3,4,4,2048]{3,2,1,0:T(4,128)}, u32[]{:S(2)}) copy-start(f32[3,4,4,2048]{3,2,1,0:T(4,128)} %disp_hbm.1) | copy-start | bytes 1179652
  0.6 9.2 %copy-start.3 = (f32[3,4,4,2048]{3,2,1,0:T(4,128)S(1)}, f32[3,4,4,2048]{3,2,1,0:T(4,128)}, u32[]{:S(2)}) copy-start(f32[3,4,4,2048]{3,2,1,0:T(4,128)} %prev_ref.1) | copy-start | bytes 1179652
  2.5 10.8 %collective-permute-start.1 = (bf16[3,1,2176]{2,1,0:T(2,128)(2,1)}, bf16[3,1,2176]{2,1,0:T(2,128)(2,1)S(1)}, u32[]{:S(2)}, u32[]{:S(2)}) collective-permute-start(bf16[3,1,2176]{2,1,0:T(2,128)(2,1)} %get-tuple-element.29), channel_id=1, source_target_pairs={{0,63},{1,120},{2,121},{3,122},{4,123},{5,124},{6,125},{7,126},{8,... | collective-permute-start | bytes 39176 | tf_op jit(solution)/shard_map/ppermute | solution.py:577
  8.4 4.9 %collective-permute-start = (bf16[3,4,2176]{2,1,0:T(4,128)(2,1)}, bf16[3,4,2176]{2,1,0:T(4,128)(2,1)S(1)}, u32[]{:S(2)}, u32[]{:S(2)}) collective-permute-start(bf16[3,4,2176]{2,1,0:T(4,128)(2,1)} %get-tuple-element.28), channel_id=1, source_target_pairs={{0,71},{1,0},{2,1},{3,2},{4,3},{5,4},{6,5},{7,6},{8,79},{9,8},{10,... | collective-permute-start | bytes 156680 | tf_op jit(solution)/shard_map/ppermute | solution.py:577
  9.7 3.6 %collective-permute-start.2 = (bf16[3,4,2176]{2,1,0:T(4,128)(2,1)}, bf16[3,4,2176]{2,1,0:T(4,128)(2,1)S(1)}, u32[]{:S(2)}, u32[]{:S(2)}) collective-permute-start(bf16[3,4,2176]{2,1,0:T(4,128)(2,1)} %get-tuple-element.30), channel_id=1, source_target_pairs={{0,120},{1,121},{2,122},{3,123},{4,124},{5,125},{6,126},{7,127},{8... | collective-permute-start | bytes 156680 | tf_op jit(solution)/shard_map/ppermute | solution.py:577
  9.7 0.7 %copy-start.9 = (s32[4,4]{1,0:T(4,128)S(1)}, s32[4,4]{1,0:T(4,128)}, u32[]{:S(2)}) copy-start(s32[4,4]{1,0:T(4,128)} %blocks_hbm.1) | copy-start | bytes 196
  9.8 0.7 %copy-start.10 = (f32[4,4]{1,0:T(4,128)S(1)}, f32[4,4]{1,0:T(4,128)}, u32[]{:S(2)}) copy-start(f32[4,4]{1,0:T(4,128)} %mass_hbm.1) | copy-start | bytes 196
  10.4 0.9 %copy-start.4 = (f32[1,5,1,5,2048]{4,2,3,1,0:T(1,128)S(1)}, f32[1,5,1,5,2048]{4,2,3,1,0:T(1,128)}, u32[]{:S(2)}) copy-start(f32[1,5,1,5,2048]{4,2,3,1,0:T(1,128)} %param.19) | copy-start | bytes 614404
  10.5 1.0 %copy-start.5 = (f32[1,5,1,5,2048]{4,2,3,1,0:T(1,128)S(1)}, f32[1,5,1,5,2048]{4,2,3,1,0:T(1,128)}, u32[]{:S(2)}) copy-start(f32[1,5,1,5,2048]{4,2,3,1,0:T(1,128)} %param.20) | copy-start | bytes 614404
  10.5 1.0 %copy-start.7 = (f32[2,1,5,1,5]{4,3,2,1,0:T(1,128)S(1)}, f32[2,1,5,1,5]{4,3,2,1,0:T(1,128)}, u32[]{:S(2)}) copy-start(f32[2,1,5,1,5]{4,3,2,1,0:T(1,128)} %param.17) | copy-start | bytes 604
  10.5 1.4 %copy-start.11 = (f32[1016,256]{1,0:T(8,128)S(1)}, f32[1016,256]{1,0:T(8,128)}, u32[]{:S(2)}) copy-start(f32[1016,256]{1,0:T(8,128)} %constant.53.clone.packed_ref) | copy-start | bytes 3121156
  10.7 1.2 %copy-start.6 = (f32[2,1,5,1,5]{4,3,2,1,0:T(1,128)S(1)}, f32[2,1,5,1,5]{4,3,2,1,0:T(1,128)}, u32[]{:S(2)}) copy-start(f32[2,1,5,1,5]{4,3,2,1,0:T(1,128)} %param.16) | copy-start | bytes 604
  10.7 1.2 %copy-start.8 = (f32[1,5,1,5]{3,2,1,0:T(1,128)S(1)}, f32[1,5,1,5]{3,2,1,0:T(1,128)}, u32[]{:S(2)}) copy-start(f32[1,5,1,5]{3,2,1,0:T(1,128)} %param.18) | copy-start | bytes 304
  11.9 1.4 %copy-start = (bf16[16,128,256]{2,1,0:T(8,128)(2,1)S(1)}, bf16[16,128,256]{2,1,0:T(8,128)(2,1)}, u32[]{:S(2)}) copy-start(bf16[16,128,256]{2,1,0:T(8,128)(2,1)} %constant.55.clone.tback_ref) | copy-start | bytes 3145732
  11.9 1.5 %copy-start.1 = (bf16[16,256,128]{2,1,0:T(8,128)(2,1)S(1)}, bf16[16,256,128]{2,1,0:T(8,128)(2,1)}, u32[]{:S(2)}) copy-start(bf16[16,256,128]{2,1,0:T(8,128)(2,1)} %constant.54.clone.table_ref) | copy-start | bytes 3145732
  15.7 5.9 %collective-permute-start.3 = (bf16[16,2048]{1,0:T(8,128)(2,1)S(1)}, bf16[16,2048]{1,0:T(8,128)(2,1)S(1)}, u32[]{:S(2)}, u32[]{:S(2)}) collective-permute-start(bf16[16,2048]{1,0:T(8,128)(2,1)S(1)} %get-tuple-element.36), channel_id=1, source_target_pairs={{0,1},{1,0},{2,3},{3,2},{4,5},{5,4},{6,7},{7,6},{8,16},{9,17},{10,... | collective-permute-start | bytes 196616 | tf_op jit(solution)/shard_map/ppermute | solution.py:591
  18.8 2.9 %collective-permute-start.4 = (bf16[16,2048]{1,0:T(8,128)(2,1)S(1)}, bf16[16,2048]{1,0:T(8,128)(2,1)S(1)}, u32[]{:S(2)}, u32[]{:S(2)}) collective-permute-start(bf16[16,2048]{1,0:T(8,128)(2,1)S(1)} %get-tuple-element.37), channel_id=1, source_target_pairs={{0,8},{1,9},{2,10},{3,11},{4,12},{5,13},{6,14},{7,15},{8,0},{9,1},... | collective-permute-start | bytes 196616 | tf_op jit(solution)/shard_map/ppermute | solution.py:591
  21.8 8.0 %collective-permute-start.5 = (bf16[16,2048]{1,0:T(8,128)(2,1)S(1)}, bf16[16,2048]{1,0:T(8,128)(2,1)S(1)}, u32[]{:S(2)}, u32[]{:S(2)}) collective-permute-start(bf16[16,2048]{1,0:T(8,128)(2,1)S(1)} %get-tuple-element.40), channel_id=1, source_target_pairs={{0,8},{1,2},{2,1},{3,4},{4,3},{5,6},{6,5},{7,15},{8,0},{9,10},{10,... | collective-permute-start | bytes 196616 | tf_op jit(solution)/shard_map/ppermute | solution.py:591
  26.1 4.3 %collective-permute-start.6 = (bf16[16,2048]{1,0:T(8,128)(2,1)S(1)}, bf16[16,2048]{1,0:T(8,128)(2,1)S(1)}, u32[]{:S(2)}, u32[]{:S(2)}) collective-permute-start(bf16[16,2048]{1,0:T(8,128)(2,1)S(1)} %get-tuple-element.41), channel_id=1, source_target_pairs={{0,1},{1,0},{2,3},{3,2},{4,5},{5,4},{6,7},{7,6},{8,9},{9,8},{10,11... | collective-permute-start | bytes 196616 | tf_op jit(solution)/shard_map/ppermute | solution.py:591
  32.6 8.8 %collective-permute-start.8 = (bf16[3,1,2048]{2,1,0:T(2,128)(2,1)S(1)}, bf16[3,1,2048]{2,1,0:T(2,128)(2,1)S(1)}, u32[]{:S(2)}, u32[]{:S(2)}) collective-permute-start(bf16[3,1,2048]{2,1,0:T(2,128)(2,1)S(1)} %get-tuple-element.46), channel_id=1, source_target_pairs={{0,9},{1,10},{2,11},{3,12},{4,13},{5,14},{6,15},{7,72},{8,17},{9,1... | collective-permute-start | bytes 36872 | tf_op jit(solution)/shard_map/ppermute | solution.py:577
  32.7 8.7 %collective-permute-start.7 = (bf16[3,4,2048]{2,1,0:T(4,128)(2,1)S(1)}, bf16[3,4,2048]{2,1,0:T(4,128)(2,1)S(1)}, u32[]{:S(2)}, u32[]{:S(2)}) collective-permute-start(bf16[3,4,2048]{2,1,0:T(4,128)(2,1)S(1)} %get-tuple-element.45), channel_id=1, source_target_pairs={{0,1},{1,2},{2,3},{3,4},{4,5},{5,6},{6,7},{7,64},{8,9},{9,10},{10,... | collective-permute-start | bytes 147464 | tf_op jit(solution)/shard_map/ppermute | solution.py:577
  32.8 8.6 %collective-permute-start.9 = (bf16[3,4,2048]{2,1,0:T(4,128)(2,1)S(1)}, bf16[3,4,2048]{2,1,0:T(4,128)(2,1)S(1)}, u32[]{:S(2)}, u32[]{:S(2)}) collective-permute-start(bf16[3,4,2048]{2,1,0:T(4,128)(2,1)S(1)} %get-tuple-element.47), channel_id=1, source_target_pairs={{0,8},{1,9},{2,10},{3,11},{4,12},{5,13},{6,14},{7,15},{8,16},{9,17... | collective-permute-start | bytes 147464 | tf_op jit(solution)/shard_map/ppermute | solution.py:577

commit v9 on v8

--- a/solution.py
+++ b/solution.py
@@ -433,7 +433,7 @@
 
 
 def step_one_kernel(
-    own_ref, free_ref, info_ref, col_ref, corner_ref, row_ref,
+    own_ref, free_ref, info_ref, row_ref, col_ref, corner_ref,
     operator_ref, back_ref, table_ref, tback_ref, material_ref, select_ref,
     sum_ref, pair_ref, side_ref, faces_ref,
     tiles, both, strain, spectrum,
@@ -651,7 +651,7 @@
             (shape(NODES, WIDTH + LANES), tile, tile, shape(32, WIDTH, dtype=BF16)),
             [pltpu.VMEM((32, WIDTH + LANES), F32)] + work,
             inputs=12, flops=10**9,
-        )(own, free, info, col, corner, row, *shared, outgoing)
+        )(own, free, info, row, col, corner, *shared, outgoing)
         cside = swapped(side, "colat", 1)
         cpair = swapped(pair, "colat", 0)
         side, pair = call(column_kernel, (tile, tile), inputs=4)(faces, cside, cpair, column)

time: 42.4 us -> 43.3 us (1.021)
  waiting for transfers between devices: 14.9 us -> 16.4 us
  starting transfers between devices: 14.7 us -> 14.1 us
    ppermute x4, starting transfers between devices: 7.3 us -> 5.83 us  [swapped(): return lax.ppermute(array, ('colat', 'depth'), pairs)]
    ppermute x4, waiting for transfers between devices: 7.12 us -> 8.58 us  [swapped(): return lax.ppermute(array, ('colat', 'depth'), pairs)]
    ppermute x6, starting transfers between devices: 7.44 us -> 8.28 us  [shifted(): return lax.ppermute(array, ('colat', 'depth'), pairs)]
  transfers between devices with their start and end apart: 10 -> 10, of which waited for: 4 -> 4; matrix products, arithmetic and copies ran while one was open for 0% -> 0% of each run, Pallas kernels for 6% -> 5%
where the time goes in v9:
time: 43.3 us; the launch traced here: 43.1 us
  waiting for transfers between devices  16.4 us (38%)
  starting transfers between devices  14.1 us (33%)
  Pallas kernels  9.71 us (22%)
  local copies, waits for them, and re-layouts  1.99 us (5%)
  between operations  0.86 us (2%)
    ppermute x4, waiting for transfers between devices, swapped(): return lax.ppermute(array, ('colat', 'depth'), pairs)  8.58 us
    ppermute x6, starting transfers between devices, shifted(): return lax.ppermute(array, ('colat', 'depth'), pairs)  8.28 us
    ppermute x6, waiting for transfers between devices, shifted(): return lax.ppermute(array, ('colat', 'depth'), pairs)  7.82 us
    ppermute x4, starting transfers between devices, swapped(): return lax.ppermute(array, ('colat', 'depth'), pairs)  5.83 us
    pallas_call x1, Pallas kernels, per_device(): call(step_two_kernel, (shape(OWN, WIDTH), shape(3, 4, 4, WIDTH), row_face...  2.28 us
    pallas_call x1, Pallas kernels, per_device(): call(step_one_kernel, (shape(NODES, WIDTH + LANES), tile, tile, shape(32,...  2.27 us
    unnamed x24, local copies, waits for them, and re-layouts  1.99 us
    pallas_call x1, Pallas kernels, per_device(): call(first_kernel, (row_face, row_face, point), [pltpu.SMEM((4, 4), jnp.i...  1.81 us
  transfers between devices with their start and end apart: 10, of which 4 were waited for; matrix products, arithmetic and copies ran while one was open for 0% of the time, Pallas kernels for 5%

profile of v9, /device:TPU:6, one launch (start us, length us, event | category | flops | bytes accessed | tf_op | source)
XLA Modules:
  0.0 43.1 jit_solution(14193587752041767364)
XLA Ops:
  0.6 0.0 copy-start.2
  0.6 0.0 copy-start.3
  0.6 1.8 %shard_map.132 = (bf16[3,4,2176]{2,1,0:T(4,128)(2,1)}, bf16[3,4,2176]{2,1,0:T(4,128)(2,1)}, bf16[3,1,2176]{2,1,0:T(2,128)(2,1)}) custom-call(s32[4,4]{1,0:T(4,128)} %blocks_hbm.1, f32[4,4]{1,0:T(4,128)} %mass_hbm.1, f32[3,4,4,2048]{3,2,1,0:T(4,128)} %disp_hbm.1), custom_call_target="tpu_custom_call" | custom-call | flops 20000000000 | bytes 1048576 | tf_op jit(solution)/shard_map/pallas_call | solution.py:604
  2.5 5.9 %collective-permute-start.2 = (bf16[3,1,2176]{2,1,0:T(2,128)(2,1)}, bf16[3,1,2176]{2,1,0:T(2,128)(2,1)S(1)}, u32[]{:S(2)}, u32[]{:S(2)}) collective-permute-start(bf16[3,1,2176]{2,1,0:T(2,128)(2,1)} %get-tuple-element.30), channel_id=1, source_target_pairs={{0,63},{1,120},{2,121},{3,122},{4,123},{5,124},{6,125},{7,126},{8,... | collective-permute-start | bytes 39176 | tf_op jit(solution)/shard_map/ppermute | solution.py:577
  8.4 1.1 %collective-permute-start = (bf16[3,4,2176]{2,1,0:T(4,128)(2,1)}, bf16[3,4,2176]{2,1,0:T(4,128)(2,1)S(1)}, u32[]{:S(2)}, u32[]{:S(2)}) collective-permute-start(bf16[3,4,2176]{2,1,0:T(4,128)(2,1)} %get-tuple-element.28), channel_id=1, source_target_pairs={{0,120},{1,121},{2,122},{3,123},{4,124},{5,125},{6,126},{7,127},{8... | collective-permute-start | bytes 156680 | tf_op jit(solution)/shard_map/ppermute | solution.py:577
  9.5 1.0 %collective-permute-start.1 = (bf16[3,4,2176]{2,1,0:T(4,128)(2,1)}, bf16[3,4,2176]{2,1,0:T(4,128)(2,1)S(1)}, u32[]{:S(2)}, u32[]{:S(2)}) collective-permute-start(bf16[3,4,2176]{2,1,0:T(4,128)(2,1)} %get-tuple-element.29), channel_id=1, source_target_pairs={{0,71},{1,0},{2,1},{3,2},{4,3},{5,4},{6,5},{7,6},{8,79},{9,8},{10,... | collective-permute-start | bytes 156680 | tf_op jit(solution)/shard_map/ppermute | solution.py:577
  10.6 0.0 copy-start.9
  10.6 0.0 copy-start.10
  10.6 0.0 copy-done.2
  10.6 0.0 copy-done.3
  10.7 0.6 %copy-done.9 = s32[4,4]{1,0:T(4,128)S(1)} copy-done((s32[4,4]{1,0:T(4,128)S(1)}, s32[4,4]{1,0:T(4,128)}, u32[]{:S(2)}) %copy-start.9) | copy-done | bytes 88
  11.3 0.0 copy-done.10
  11.3 0.0 copy-start.4
  11.3 0.0 copy-start.5
  11.3 0.2 shard_map.131
  11.5 0.0 copy-start.6
  11.6 0.0 copy-start.8
  11.6 0.7 %copy-done.4 = f32[1,5,1,5,2048]{4,2,3,1,0:T(1,128)S(1)} copy-done((f32[1,5,1,5,2048]{4,2,3,1,0:T(1,128)S(1)}, f32[1,5,1,5,2048]{4,2,3,1,0:T(1,128)}, u32[]{:S(2)}) %copy-start.4) | copy-done | bytes 204824
  12.2 0.1 copy-done.5
  12.3 0.0 copy-done.7
  12.3 0.4 copy-done.11
  12.7 0.0 copy-done.6
  12.7 0.0 copy-done.8
  12.8 1.3 %shard_map.133 = (bf16[152,160]{1,0:T(8,128)(2,1)S(1)}, bf16[160,152]{1,0:T(8,128)(2,1)S(1)}, f32[16,56,128]{2,1,0:T(8,128)S(1)}, bf16[64,80]{1,0:T(8,128)(2,1)S...) custom-call(f32[8,128]{1,0:T(8,128)S(1)} %select_select_fusion.place_ref, f32[10,1,5]{2,1,0:T(1,128)S(1)} %bitcast.7, ...), custom_call_target="tpu_custom_call" | custom-call | flops 1000000000 | bytes 1048576 | tf_op jit(solution)/shard_map/pallas_call | solution.py:624
  14.1 0.0 collective-permute-done.2.corner_ref
  14.1 0.0 collective-permute-done.row_ref
  14.1 0.0 collective-permute-done.1.col_ref
  14.1 0.0 copy-done
  14.2 0.1 copy-done.1
  14.3 2.3 %shard_map.134 = (f32[80,2176]{1,0:T(8,128)S(1)}, bf16[16,2048]{1,0:T(8,128)(2,1)S(1)}, bf16[16,2048]{1,0:T(8,128)(2,1)S(1)}, bf16[32,2048]{1,0:T(8,128)(2,1)S(1)}) custom-call(f32[48,2048]{1,0:T(8,128)S(1)} %get-tuple-element.25.own_ref, f32[48,2048]{1,0:T(8,128)S(1)} %get-tuple-element.26.free_ref, f32[56,128]{1,0:T(8,128)S(1)} %get-tuple-element.27.info_ref, ...), custom_call_target="tpu_custom_call" | custom-call | flops 1000000000 | bytes 1048576 | tf_op jit(solution)/shard_map/pallas_call | solution.py:649
  16.6 1.6 %collective-permute-start.3 = (bf16[16,2048]{1,0:T(8,128)(2,1)S(1)}, bf16[16,2048]{1,0:T(8,128)(2,1)S(1)}, u32[]{:S(2)}, u32[]{:S(2)}) collective-permute-start(bf16[16,2048]{1,0:T(8,128)(2,1)S(1)} %get-tuple-element.36), channel_id=1, source_target_pairs={{0,1},{1,0},{2,3},{3,2},{4,5},{5,4},{6,7},{7,6},{8,16},{9,17},{10,... | collective-permute-start | bytes 196616 | tf_op jit(solution)/shard_map/ppermute | solution.py:591
  18.1 0.0 collective-permute-start.4
  18.1 4.3 %collective-permute-done.3.side_ref.cside_ref = bf16[16,2048]{1,0:T(8,128)(2,1)S(1)} collective-permute-done((bf16[16,2048]{1,0:T(8,128)(2,1)S(1)}, bf16[16,2048]{1,0:T(8,128)(2,1)S(1)}, u32[]{:S(2)}, u32[]{:S(2)}) %collective-permute-start.3) | collective-permute-done | bytes 65568 | tf_op jit(solution)/shard_map/ppermute | solution.py:591
  22.5 0.0 collective-permute-done.4.pair_ref.cpair_ref
  22.5 0.2 shard_map.135
  22.6 4.3 %collective-permute-start.5 = (bf16[16,2048]{1,0:T(8,128)(2,1)S(1)}, bf16[16,2048]{1,0:T(8,128)(2,1)S(1)}, u32[]{:S(2)}, u32[]{:S(2)}) collective-permute-start(bf16[16,2048]{1,0:T(8,128)(2,1)S(1)} %get-tuple-element.40), channel_id=1, source_target_pairs={{0,8},{1,2},{2,1},{3,4},{4,3},{5,6},{6,5},{7,15},{8,0},{9,10},{10,... | collective-permute-start | bytes 196616 | tf_op jit(solution)/shard_map/ppermute | solution.py:591
  26.9 0.0 collective-permute-start.6
  26.9 3.7 %collective-permute-done.5.dside_ref = bf16[16,2048]{1,0:T(8,128)(2,1)S(1)} collective-permute-done((bf16[16,2048]{1,0:T(8,128)(2,1)S(1)}, bf16[16,2048]{1,0:T(8,128)(2,1)S(1)}, u32[]{:S(2)}, u32[]{:S(2)}) %collective-permute-start.5) | collective-permute-done | bytes 65568 | tf_op jit(solution)/shard_map/ppermute | solution.py:591
  30.6 0.6 %collective-permute-done.6.dpair_ref = bf16[16,2048]{1,0:T(8,128)(2,1)S(1)} collective-permute-done((bf16[16,2048]{1,0:T(8,128)(2,1)S(1)}, bf16[16,2048]{1,0:T(8,128)(2,1)S(1)}, u32[]{:S(2)}, u32[]{:S(2)}) %collective-permute-start.6) | collective-permute-done | bytes 65568 | tf_op jit(solution)/shard_map/ppermute | solution.py:591
  31.2 2.3 %shard_map.136 = (f32[48,2048]{1,0:T(8,128)S(1)}, f32[3,4,4,2048]{3,2,1,0:T(4,128)S(1)}, bf16[3,4,2048]{2,1,0:T(4,128)(2,1)S(1)}, bf16[3,4,2048]{2,1,0:T(4,128)(2,1)S(1)}, bf16[3,1,2048]{2,1,0:T(2,128)(2,1)S(1)}) custom-call(f32[48,2048]{1,0:T(8,128)S(1)} %get-tuple-element.25.own_ref, f32[80,2176]{1,0:T(8,128)S(1)} %get-tuple-element.35.sum_ref, ...), custom_call_target="tpu_custom_call" | custom-call | flops 1000000000 | bytes 1048576 | tf_op jit(solution)/shard_map/pallas_call | solution.py:661
  33.5 0.1 collective-permute-start.8
  33.5 0.1 collective-permute-start.7
  33.6 0.1 collective-permute-start.9
  33.7 0.8 %shard_map.137 = f32[3,4,4,2048]{3,2,1,0:T(4,128)} custom-call(f32[48,2048]{1,0:T(8,128)S(1)} %get-tuple-element.43.rows_ref), custom_call_target="tpu_custom_call" | custom-call | flops 20000000000 | bytes 1048576 | tf_op jit(solution)/shard_map/pallas_call | solution.py:673
  34.5 7.8 %collective-permute-done.8.corner_ref = bf16[3,1,2048]{2,1,0:T(2,128)(2,1)S(1)} collective-permute-done((bf16[3,1,2048]{2,1,0:T(2,128)(2,1)S(1)}, bf16[3,1,2048]{2,1,0:T(2,128)(2,1)S(1)}, u32[]{:S(2)}, u32[]{:S(2)}) %collective-permute-start.8) | collective-permute-done | bytes 12320 | tf_op jit(solution)/shard_map/ppermute | solution.py:577
  42.3 0.0 collective-permute-done.7.col_ref
  42.3 0.0 collective-permute-done.9.row_ref
  42.3 0.8 %shard_map.138 = f32[3,4,4,2048]{3,2,1,0:T(4,128)} custom-call(f32[3,4,4,2048]{3,2,1,0:T(4,128)S(1)} %get-tuple-element.44.sum_ref, bf16[3,4,2048]{2,1,0:T(4,128)(2,1)S(1)} %collective-permute-done.7.col_ref, bf16[3,1,2048]{2,1,0:T(2,128)(2,1)S(1)} %collective-permute-done.8.corner_ref, bf16[3,4,2048]{2,1,0:T(4,128)(2,1)S(1)} %collective-permute-done.9.row_ref), custom_call_target="tpu_custom_call" | custom-call | bytes 1048576 | tf_op jit(solution)/shard_map/pallas_call | solution.py:674
  (9 shorter events, 0.0 us)
Async XLA Ops:
  0.6 10.0 %copy-start.2 = (f32[3,4,4,2048]{3,2,1,0:T(4,128)S(1)}, f32[3,4,4,2048]{3,2,1,0:T(4,128)}, u32[]{:S(2)}) copy-start(f32[3,4,4,2048]{3,2,1,0:T(4,128)} %disp_hbm.1) | copy-start | bytes 1179652
  0.6 10.0 %copy-start.3 = (f32[3,4,4,2048]{3,2,1,0:T(4,128)S(1)}, f32[3,4,4,2048]{3,2,1,0:T(4,128)}, u32[]{:S(2)}) copy-start(f32[3,4,4,2048]{3,2,1,0:T(4,128)} %prev_ref.1) | copy-start | bytes 1179652
  2.5 11.6 %collective-permute-start.2 = (bf16[3,1,2176]{2,1,0:T(2,128)(2,1)}, bf16[3,1,2176]{2,1,0:T(2,128)(2,1)S(1)}, u32[]{:S(2)}, u32[]{:S(2)}) collective-permute-start(bf16[3,1,2176]{2,1,0:T(2,128)(2,1)} %get-tuple-element.30), channel_id=1, source_target_pairs={{0,63},{1,120},{2,121},{3,122},{4,123},{5,124},{6,125},{7,126},{8,... | collective-permute-start | bytes 39176 | tf_op jit(solution)/shard_map/ppermute | solution.py:577
  8.4 5.7 %collective-permute-start = (bf16[3,4,2176]{2,1,0:T(4,128)(2,1)}, bf16[3,4,2176]{2,1,0:T(4,128)(2,1)S(1)}, u32[]{:S(2)}, u32[]{:S(2)}) collective-permute-start(bf16[3,4,2176]{2,1,0:T(4,128)(2,1)} %get-tuple-element.28), channel_id=1, source_target_pairs={{0,120},{1,121},{2,122},{3,123},{4,124},{5,125},{6,126},{7,127},{8... | collective-permute-start | bytes 156680 | tf_op jit(solution)/shard_map/ppermute | solution.py:577
  9.5 4.6 %collective-permute-start.1 = (bf16[3,4,2176]{2,1,0:T(4,128)(2,1)}, bf16[3,4,2176]{2,1,0:T(4,128)(2,1)S(1)}, u32[]{:S(2)}, u32[]{:S(2)}) collective-permute-start(bf16[3,4,2176]{2,1,0:T(4,128)(2,1)} %get-tuple-element.29), channel_id=1, source_target_pairs={{0,71},{1,0},{2,1},{3,2},{4,3},{5,4},{6,5},{7,6},{8,79},{9,8},{10,... | collective-permute-start | bytes 156680 | tf_op jit(solution)/shard_map/ppermute | solution.py:577
  10.6 0.7 %copy-start.9 = (s32[4,4]{1,0:T(4,128)S(1)}, s32[4,4]{1,0:T(4,128)}, u32[]{:S(2)}) copy-start(s32[4,4]{1,0:T(4,128)} %blocks_hbm.1) | copy-start | bytes 196
  10.6 0.7 %copy-start.10 = (f32[4,4]{1,0:T(4,128)S(1)}, f32[4,4]{1,0:T(4,128)}, u32[]{:S(2)}) copy-start(f32[4,4]{1,0:T(4,128)} %mass_hbm.1) | copy-start | bytes 196
  11.3 0.9 %copy-start.4 = (f32[1,5,1,5,2048]{4,2,3,1,0:T(1,128)S(1)}, f32[1,5,1,5,2048]{4,2,3,1,0:T(1,128)}, u32[]{:S(2)}) copy-start(f32[1,5,1,5,2048]{4,2,3,1,0:T(1,128)} %param.19) | copy-start | bytes 614404
  11.3 1.0 %copy-start.5 = (f32[1,5,1,5,2048]{4,2,3,1,0:T(1,128)S(1)}, f32[1,5,1,5,2048]{4,2,3,1,0:T(1,128)}, u32[]{:S(2)}) copy-start(f32[1,5,1,5,2048]{4,2,3,1,0:T(1,128)} %param.20) | copy-start | bytes 614404
  11.3 1.0 %copy-start.7 = (f32[2,1,5,1,5]{4,3,2,1,0:T(1,128)S(1)}, f32[2,1,5,1,5]{4,3,2,1,0:T(1,128)}, u32[]{:S(2)}) copy-start(f32[2,1,5,1,5]{4,3,2,1,0:T(1,128)} %param.17) | copy-start | bytes 604
  11.3 1.4 %copy-start.11 = (f32[1016,256]{1,0:T(8,128)S(1)}, f32[1016,256]{1,0:T(8,128)}, u32[]{:S(2)}) copy-start(f32[1016,256]{1,0:T(8,128)} %constant.53.clone.packed_ref) | copy-start | bytes 3121156
  11.5 1.2 %copy-start.6 = (f32[2,1,5,1,5]{4,3,2,1,0:T(1,128)S(1)}, f32[2,1,5,1,5]{4,3,2,1,0:T(1,128)}, u32[]{:S(2)}) copy-start(f32[2,1,5,1,5]{4,3,2,1,0:T(1,128)} %param.16) | copy-start | bytes 604
  11.6 1.2 %copy-start.8 = (f32[1,5,1,5]{3,2,1,0:T(1,128)S(1)}, f32[1,5,1,5]{3,2,1,0:T(1,128)}, u32[]{:S(2)}) copy-start(f32[1,5,1,5]{3,2,1,0:T(1,128)} %param.18) | copy-start | bytes 304
  12.8 1.4 %copy-start = (bf16[16,128,256]{2,1,0:T(8,128)(2,1)S(1)}, bf16[16,128,256]{2,1,0:T(8,128)(2,1)}, u32[]{:S(2)}) copy-start(bf16[16,128,256]{2,1,0:T(8,128)(2,1)} %constant.55.clone.tback_ref) | copy-start | bytes 3145732
  12.8 1.5 %copy-start.1 = (bf16[16,256,128]{2,1,0:T(8,128)(2,1)S(1)}, bf16[16,256,128]{2,1,0:T(8,128)(2,1)}, u32[]{:S(2)}) copy-start(bf16[16,256,128]{2,1,0:T(8,128)(2,1)} %constant.54.clone.table_ref) | copy-start | bytes 3145732
  16.6 5.9 %collective-permute-start.3 = (bf16[16,2048]{1,0:T(8,128)(2,1)S(1)}, bf16[16,2048]{1,0:T(8,128)(2,1)S(1)}, u32[]{:S(2)}, u32[]{:S(2)}) collective-permute-start(bf16[16,2048]{1,0:T(8,128)(2,1)S(1)} %get-tuple-element.36), channel_id=1, source_target_pairs={{0,1},{1,0},{2,3},{3,2},{4,5},{5,4},{6,7},{7,6},{8,16},{9,17},{10,... | collective-permute-start | bytes 196616 | tf_op jit(solution)/shard_map/ppermute | solution.py:591
  18.1 4.3 %collective-permute-start.4 = (bf16[16,2048]{1,0:T(8,128)(2,1)S(1)}, bf16[16,2048]{1,0:T(8,128)(2,1)S(1)}, u32[]{:S(2)}, u32[]{:S(2)}) collective-permute-start(bf16[16,2048]{1,0:T(8,128)(2,1)S(1)} %get-tuple-element.37), channel_id=1, source_target_pairs={{0,8},{1,9},{2,10},{3,11},{4,12},{5,13},{6,14},{7,15},{8,0},{9,1},... | collective-permute-start | bytes 196616 | tf_op jit(solution)/shard_map/ppermute | solution.py:591
  22.6 8.0 %collective-permute-start.5 = (bf16[16,2048]{1,0:T(8,128)(2,1)S(1)}, bf16[16,2048]{1,0:T(8,128)(2,1)S(1)}, u32[]{:S(2)}, u32[]{:S(2)}) collective-permute-start(bf16[16,2048]{1,0:T(8,128)(2,1)S(1)} %get-tuple-element.40), channel_id=1, source_target_pairs={{0,8},{1,2},{2,1},{3,4},{4,3},{5,6},{6,5},{7,15},{8,0},{9,10},{10,... | collective-permute-start | bytes 196616 | tf_op jit(solution)/shard_map/ppermute | solution.py:591
  26.9 4.3 %collective-permute-start.6 = (bf16[16,2048]{1,0:T(8,128)(2,1)S(1)}, bf16[16,2048]{1,0:T(8,128)(2,1)S(1)}, u32[]{:S(2)}, u32[]{:S(2)}) collective-permute-start(bf16[16,2048]{1,0:T(8,128)(2,1)S(1)} %get-tuple-element.41), channel_id=1, source_target_pairs={{0,1},{1,0},{2,3},{3,2},{4,5},{5,4},{6,7},{7,6},{8,9},{9,8},{10,11... | collective-permute-start | bytes 196616 | tf_op jit(solution)/shard_map/ppermute | solution.py:591
  33.5 8.8 %collective-permute-start.8 = (bf16[3,1,2048]{2,1,0:T(2,128)(2,1)S(1)}, bf16[3,1,2048]{2,1,0:T(2,128)(2,1)S(1)}, u32[]{:S(2)}, u32[]{:S(2)}) collective-permute-start(bf16[3,1,2048]{2,1,0:T(2,128)(2,1)S(1)} %get-tuple-element.46), channel_id=1, source_target_pairs={{0,9},{1,10},{2,11},{3,12},{4,13},{5,14},{6,15},{7,72},{8,17},{9,1... | collective-permute-start | bytes 36872 | tf_op jit(solution)/shard_map/ppermute | solution.py:577
  33.5 8.7 %collective-permute-start.7 = (bf16[3,4,2048]{2,1,0:T(4,128)(2,1)S(1)}, bf16[3,4,2048]{2,1,0:T(4,128)(2,1)S(1)}, u32[]{:S(2)}, u32[]{:S(2)}) collective-permute-start(bf16[3,4,2048]{2,1,0:T(4,128)(2,1)S(1)} %get-tuple-element.45), channel_id=1, source_target_pairs={{0,1},{1,2},{2,3},{3,4},{4,5},{5,6},{6,7},{7,64},{8,9},{9,10},{10,... | collective-permute-start | bytes 147464 | tf_op jit(solution)/shard_map/ppermute | solution.py:577
  33.6 8.7 %collective-permute-start.9 = (bf16[3,4,2048]{2,1,0:T(4,128)(2,1)S(1)}, bf16[3,4,2048]{2,1,0:T(4,128)(2,1)S(1)}, u32[]{:S(2)}, u32[]{:S(2)}) collective-permute-start(bf16[3,4,2048]{2,1,0:T(4,128)(2,1)S(1)} %get-tuple-element.47), channel_id=1, source_target_pairs={{0,8},{1,9},{2,10},{3,11},{4,12},{5,13},{6,14},{7,15},{8,16},{9,17... | collective-permute-start | bytes 147464 | tf_op jit(solution)/shard_map/ppermute | solution.py:577
